TPU v7x, 32 devices: a whole 2x2x4 slice. The times are simulated.
32 devices in a mesh: dp: 8 (over z, core), fsdp: 4 (over y, x).
Axes of the slice: x: 2, y: 2, z: 4, core: 2. Of those that a mesh axis runs over, the one named last changes fastest.
Arguments:
- tokens: bfloat16 [8192, 1024], P(('dp', 'fsdp')), may hold values from -6 to 6
- cotangent: bfloat16 [8192, 1024], P(('dp', 'fsdp')), may hold values from -6 to 6
- lengths: int32 [32, 8], P(('dp', 'fsdp')), may hold values from 0 to 256, as said below
- value_proj: bfloat16 [1024, 2048], P('dp', 'fsdp'), may hold values from -0.1875 to 0.1875
- mix_proj: bfloat16 [1024, 4224], P('dp', 'fsdp'), may hold values from -0.1875 to 0.1875
- merge_proj: bfloat16 [2048, 1024], P('dp', 'fsdp'), may hold values from -0.5 to 0.5
- up_proj: bfloat16 [1024, 4096], P('dp', 'fsdp'), may hold values from -0.1875 to 0.1875
- down_proj: bfloat16 [4096, 1024], P('dp', 'fsdp'), may hold values from -0.09375 to 0.09375
- norm_gains: bfloat16 [3, 1024], P(None, ('dp', 'fsdp')), may hold values from 0.5 to 1.5
- ema_params: bfloat16 [4, 1024, 16], P(None, ('dp', 'fsdp')), may hold values from -6 to 4
- attn_params: bfloat16 [512], P(('dp', 'fsdp')), may hold values from -6 to 6
Outputs:
- result: bfloat16 [8192, 1024], P(('dp', 'fsdp'))
- grad_tokens: bfloat16 [8192, 1024], P(('dp', 'fsdp'))
- grad_value: float32 [1024, 2048], P('dp', 'fsdp')
- grad_mix: float32 [1024, 4224], P('dp', 'fsdp')
- grad_merge: float32 [2048, 1024], P('dp', 'fsdp')
- grad_up: float32 [1024, 4096], P('dp', 'fsdp')
- grad_down: float32 [4096, 1024], P('dp', 'fsdp')
- grad_gains: float32 [3, 1024], P(None, ('dp', 'fsdp'))
- grad_ema: float32 [4, 1024, 16], P(None, ('dp', 'fsdp'))
- grad_attn: float32 [512], P(('dp', 'fsdp'))
Inputs may be any that keep to these rules, and one draw needn't show every extreme that they name: Each row lists the lengths of up to 8 sequences packed from the start of one device's buffer of 256 slots. Every nonzero length is 256 times a power of two, a row sums to at most 256, its first entry is nonzero, zeros come only after the nonzero entries, and slots past the row's sum are padding.
All inputs are finite; a program needn't handle non-finite values.
Results may differ from a plain program's by a relative error of at most 0.018.
Values may be sent and summed in bfloat16 or wider, within the bound.
A program may use at most 320 MiB of HBM per device.

v0:
```python
import jax
import jax.numpy as jnp
from jax import lax
from jax.sharding import PartitionSpec as P

D = 1024
Z = 128
V = 2048
STRETCH = 128


highest = lax.Precision.HIGHEST


def layer_norm(values, gain):
    centred = values - jnp.mean(values, axis=-1, keepdims=True)
    spread_sq = jnp.mean(centred * centred, axis=-1, keepdims=True)
    return centred * lax.rsqrt(spread_sq + 1e-05) * gain


def token_layout(length_row, row_count):
    places = jnp.arange(row_count, dtype=jnp.int32)
    running = jnp.cumsum(length_row)
    before = (running[None, :] <= places[:, None]).astype(jnp.int32)
    starts = jnp.sum(before * length_row[None, :], axis=1)
    return (places - starts, places < running[-1])


def ema_apply(normed, ema_float, omega_gain, position):
    row_count = normed.shape[0]
    block_len = STRETCH // 4
    damping = jax.nn.sigmoid(ema_float[0])
    decay_gate = jax.nn.sigmoid(ema_float[1])
    keep_rate = 1.0 - damping * decay_gate
    weights_out = damping * ema_float[2] * ema_float[3] * ema_float.shape[2] ** (-0.5)
    lag_axis = jnp.arange(block_len + 1, dtype=normed.dtype)
    powers = jnp.exp(lag_axis[None, None, :] * jnp.log(keep_rate)[:, :, None])
    kernel = jnp.einsum("cj,cjl->cl", weights_out, powers[:, :, :block_len], precision=highest)
    offsets = (
        jnp.arange(block_len, dtype=jnp.int32)[:, None]
        - jnp.arange(block_len, dtype=jnp.int32)[None, :]
    )
    toeplitz = jnp.where(
        offsets[None] >= 0, jnp.take(kernel, jnp.clip(offsets, 0, block_len - 1), axis=1), 0.0
    )
    leaving = powers[:, :, block_len - 1 :: -1]
    arriving = weights_out[:, :, None] * powers[:, :, 1:]
    blocks = normed.reshape(row_count // block_len, block_len, normed.shape[1])
    resets = position.reshape(row_count // block_len, block_len)[:, 0] == 0

    def advance(ema_state, inputs):
        block_in, is_reset = inputs
        ema_state = jnp.where(is_reset, 0.0, ema_state)
        inner_part = jnp.einsum("cts,sc->tc", toeplitz, block_in, precision=highest)
        carried = jnp.einsum("cjt,cj->tc", arriving, ema_state, precision=highest)
        ema_state = ema_state * powers[:, :, block_len] + jnp.einsum(
            "cjs,sc->cj", leaving, block_in, precision=highest
        )
        return (ema_state, inner_part + carried)

    zero_state = jnp.zeros(keep_rate.shape, normed.dtype)
    final_state, mixed_out = lax.scan(advance, zero_state, (blocks, resets))
    return mixed_out.reshape(row_count, normed.shape[1]) + omega_gain * normed


def silu_slope(values):
    logistic = jax.nn.sigmoid(values)
    return logistic * (1.0 + values * (1.0 - logistic))


def relative_table(rel_bias):
    lag_grid = (
        jnp.arange(STRETCH, dtype=jnp.int32)[:, None]
        - jnp.arange(STRETCH, dtype=jnp.int32)[None, :]
    )
    one_hot = (lag_grid[:, :, None] == jnp.arange(STRETCH, dtype=jnp.int32)[None, None, :]).astype(
        jnp.float32
    )
    bias_grid = jnp.einsum("ijl,l->ij", one_hot, rel_bias, precision=highest)
    return (lag_grid, one_hot, bias_grid)


def gather_forward(value_proj, mix_proj, merge_proj, up_proj, down_proj):
    first = (
        lax.all_gather(value_proj, "dp", axis=0, tiled=True),
        lax.all_gather(mix_proj, "dp", axis=0, tiled=True),
        lax.all_gather(merge_proj, "dp", axis=0, tiled=True),
        lax.all_gather(up_proj, "dp", axis=0, tiled=True),
        lax.all_gather(down_proj, "dp", axis=0, tiled=True),
    )
    return (
        lax.all_gather(first[0], "fsdp", axis=1, tiled=True),
        lax.all_gather(first[1], "fsdp", axis=1, tiled=True),
        lax.all_gather(first[2], "fsdp", axis=1, tiled=True),
        lax.all_gather(first[3], "fsdp", axis=1, tiled=True),
        lax.all_gather(first[4], "fsdp", axis=1, tiled=True),
    )


def gather_backward(value_proj, mix_proj, merge_proj, up_proj, down_proj):
    first = (
        lax.all_gather(value_proj, "dp", axis=0, tiled=True),
        lax.all_gather(mix_proj, "dp", axis=0, tiled=True),
        lax.all_gather(merge_proj, "dp", axis=0, tiled=True),
        lax.all_gather(up_proj, "dp", axis=0, tiled=True),
        lax.all_gather(down_proj, "dp", axis=0, tiled=True),
    )
    return (
        lax.all_gather(first[0], "fsdp", axis=1, tiled=True),
        lax.all_gather(first[1], "fsdp", axis=1, tiled=True),
        lax.all_gather(first[2], "fsdp", axis=1, tiled=True),
        lax.all_gather(first[3], "fsdp", axis=1, tiled=True),
        lax.all_gather(first[4], "fsdp", axis=1, tiled=True),
    )


def reduce_gradients(value_grad, mix_grad, merge_grad, up_grad, down_grad):
    first = (
        lax.psum_scatter(
            value_grad.astype(jnp.bfloat16), "dp", scatter_dimension=0, tiled=True
        ).astype(jnp.float32),
        lax.psum_scatter(
            mix_grad.astype(jnp.bfloat16), "dp", scatter_dimension=0, tiled=True
        ).astype(jnp.float32),
        lax.psum_scatter(
            merge_grad.astype(jnp.bfloat16), "dp", scatter_dimension=0, tiled=True
        ).astype(jnp.float32),
        lax.psum_scatter(
            up_grad.astype(jnp.bfloat16), "dp", scatter_dimension=0, tiled=True
        ).astype(jnp.float32),
        lax.psum_scatter(
            down_grad.astype(jnp.bfloat16), "dp", scatter_dimension=0, tiled=True
        ).astype(jnp.float32),
    )
    return (
        lax.psum_scatter(
            first[0].astype(jnp.bfloat16), "fsdp", scatter_dimension=1, tiled=True
        ).astype(jnp.float32),
        lax.psum_scatter(
            first[1].astype(jnp.bfloat16), "fsdp", scatter_dimension=1, tiled=True
        ).astype(jnp.float32),
        lax.psum_scatter(
            first[2].astype(jnp.bfloat16), "fsdp", scatter_dimension=1, tiled=True
        ).astype(jnp.float32),
        lax.psum_scatter(
            first[3].astype(jnp.bfloat16), "fsdp", scatter_dimension=1, tiled=True
        ).astype(jnp.float32),
        lax.psum_scatter(
            first[4].astype(jnp.bfloat16), "fsdp", scatter_dimension=1, tiled=True
        ).astype(jnp.float32),
    )


def on_device(
    tokens,
    cotangent,
    lengths,
    value_proj,
    mix_proj,
    merge_proj,
    up_proj,
    down_proj,
    norm_gains,
    ema_params,
    attn_params,
):
    gains_full, ema_full, attn_full = (
        lax.all_gather(norm_gains, ("dp", "fsdp"), axis=1, tiled=True),
        lax.all_gather(ema_params, ("dp", "fsdp"), axis=1, tiled=True),
        lax.all_gather(attn_params, ("dp", "fsdp"), axis=0, tiled=True),
    )
    value_full, mix_full, merge_full, up_full, down_full = gather_forward(
        value_proj, mix_proj, merge_proj, up_proj, down_proj
    )
    gains_float = gains_full.astype(jnp.float32)
    ema_float = ema_full.astype(jnp.float32)
    attn_float = attn_full.astype(jnp.float32)
    row_count = tokens.shape[0]
    position, live_rows = token_layout(lengths[0], row_count)
    tokens_float = tokens.astype(jnp.float32)
    normed, norm_back = jax.vjp(layer_norm, tokens_float, gains_float[0])
    normed_low = normed.astype(jnp.bfloat16)
    value_pre = jnp.dot(normed_low, value_full, preferred_element_type=jnp.float32)
    value_low = jax.nn.silu(value_pre).astype(jnp.bfloat16)

    def ema_local(normed_in, ema_in, omega_in):
        return ema_apply(normed_in, ema_in, omega_in, position)

    ema_out, ema_back = jax.vjp(ema_local, normed, ema_float, gains_float[2])
    mixed_low = jax.nn.silu(ema_out).astype(jnp.bfloat16)
    projected = jnp.dot(mixed_low, mix_full, preferred_element_type=jnp.float32)
    update_gate = jax.nn.sigmoid(projected[:, :D])
    shared_pre = projected[:, D : D + Z]
    reset_pre = projected[:, D + Z : D + Z + V]
    hidden_x = projected[:, D + Z + V :]
    shared = jax.nn.silu(shared_pre)
    reset_gate = jax.nn.silu(reset_pre)
    query_low = (shared * attn_float[:Z] + attn_float[Z : 2 * Z]).astype(jnp.bfloat16)
    key_low = (shared * attn_float[2 * Z : 3 * Z]).astype(jnp.bfloat16)
    block_count = row_count // STRETCH
    lag_grid, one_hot, bias_grid = relative_table(attn_float[3 * Z :])
    query_blocks = query_low.reshape(block_count, STRETCH, Z)
    key_blocks = key_low.reshape(block_count, STRETCH, Z)
    value_blocks = value_low.reshape(block_count, STRETCH, V)
    score_scale = Z ** (-0.5)

    def block_scores():
        raw_scores = (
            jnp.einsum("nik,njk->nij", query_blocks, key_blocks, preferred_element_type=jnp.float32)
            * score_scale
            + bias_grid
        )
        return jnp.where(lag_grid >= 0, raw_scores, -1000000000.0)

    scores = block_scores()
    row_max = jnp.max(scores, axis=-1, keepdims=True)
    log_total = row_max + jnp.log(jnp.sum(jnp.exp(scores - row_max), axis=-1, keepdims=True))
    probs_low = jnp.exp(scores - log_total).astype(jnp.bfloat16)
    attended = jnp.einsum(
        "nij,njv->niv", probs_low, value_blocks, preferred_element_type=jnp.float32
    ).reshape(row_count, V)
    gated_low = (attended * reset_gate).astype(jnp.bfloat16)
    hidden_in = jnp.dot(gated_low, merge_full, preferred_element_type=jnp.float32) + hidden_x
    hidden = jax.nn.silu(hidden_in)
    after_mixer = update_gate * hidden + (1.0 - update_gate) * tokens_float
    normed_two, norm_two_back = jax.vjp(layer_norm, after_mixer, gains_float[1])
    normed_two_low = normed_two.astype(jnp.bfloat16)
    up_pre = jnp.dot(normed_two_low, up_full, preferred_element_type=jnp.float32)
    up_low = jax.nn.silu(up_pre).astype(jnp.bfloat16)
    result = (after_mixer + jnp.dot(up_low, down_full, preferred_element_type=jnp.float32)).astype(
        jnp.bfloat16
    )
    value_back, mix_back, merge_back, up_back, down_back = gather_backward(
        value_proj, mix_proj, merge_proj, up_proj, down_proj
    )
    grad_rows = cotangent.astype(jnp.float32) * live_rows[:, None].astype(jnp.float32)
    grad_down_low = grad_rows.astype(jnp.bfloat16)
    down_grad = jnp.einsum("tf,td->fd", up_low, grad_down_low, preferred_element_type=jnp.float32)
    grad_up_act = jnp.einsum(
        "td,fd->tf", grad_down_low, down_back, preferred_element_type=jnp.float32
    )
    grad_up_low = (grad_up_act * silu_slope(up_pre)).astype(jnp.bfloat16)
    up_grad = jnp.einsum(
        "td,tf->df", normed_two_low, grad_up_low, preferred_element_type=jnp.float32
    )
    grad_normed_two = jnp.einsum(
        "tf,df->td", grad_up_low, up_back, preferred_element_type=jnp.float32
    )
    grad_after_norm, gain_two_grad = norm_two_back(grad_normed_two)
    grad_after = grad_after_norm + grad_rows
    grad_hidden_in = grad_after * update_gate * silu_slope(hidden_in)
    grad_merge_low = grad_hidden_in.astype(jnp.bfloat16)
    merge_grad = jnp.einsum(
        "tv,td->vd", gated_low, grad_merge_low, preferred_element_type=jnp.float32
    )
    grad_gated = jnp.einsum(
        "td,vd->tv", grad_merge_low, merge_back, preferred_element_type=jnp.float32
    )
    grad_reset = grad_gated * attended
    grad_attended_low = (
        (grad_gated * reset_gate).astype(jnp.bfloat16).reshape(block_count, STRETCH, V)
    )
    grad_probs = jnp.einsum(
        "niv,njv->nij", grad_attended_low, value_blocks, preferred_element_type=jnp.float32
    )
    soft_probs = jnp.exp(block_scores() - log_total)
    grad_scores_low = (
        soft_probs * (grad_probs - jnp.sum(soft_probs * grad_probs, axis=-1, keepdims=True))
    ).astype(jnp.bfloat16)
    grad_query = (
        jnp.einsum(
            "nij,njk->nik", grad_scores_low, key_blocks, preferred_element_type=jnp.float32
        ).reshape(row_count, Z)
        * score_scale
    )
    grad_key = (
        jnp.einsum(
            "nij,nik->njk", grad_scores_low, query_blocks, preferred_element_type=jnp.float32
        ).reshape(row_count, Z)
        * score_scale
    )
    grad_value_act = jnp.einsum(
        "nij,niv->njv",
        soft_probs.astype(jnp.bfloat16),
        grad_attended_low,
        preferred_element_type=jnp.float32,
    ).reshape(row_count, V)
    rel_grad = jnp.einsum(
        "ij,ijl->l",
        jnp.sum(grad_scores_low.astype(jnp.float32), axis=0),
        one_hot,
        precision=highest,
    )
    attn_grad = jnp.concatenate(
        [
            jnp.sum(grad_query * shared, axis=0),
            jnp.sum(grad_query, axis=0),
            jnp.sum(grad_key * shared, axis=0),
            rel_grad,
        ]
    )
    grad_shared = grad_query * attn_float[:Z] + grad_key * attn_float[2 * Z : 3 * Z]
    grad_projected_low = jnp.concatenate(
        [
            grad_after * (hidden - tokens_float) * update_gate * (1.0 - update_gate),
            grad_shared * silu_slope(shared_pre),
            grad_reset * silu_slope(reset_pre),
            grad_hidden_in,
        ],
        axis=1,
    ).astype(jnp.bfloat16)
    mix_grad = jnp.einsum(
        "td,tm->dm", mixed_low, grad_projected_low, preferred_element_type=jnp.float32
    )
    grad_mixed = jnp.einsum(
        "tm,dm->td", grad_projected_low, mix_back, preferred_element_type=jnp.float32
    )
    grad_normed_ema, ema_grad, omega_grad = ema_back(grad_mixed * silu_slope(ema_out))
    grad_value_low = (grad_value_act * silu_slope(value_pre)).astype(jnp.bfloat16)
    value_grad = jnp.einsum(
        "td,tv->dv", normed_low, grad_value_low, preferred_element_type=jnp.float32
    )
    grad_normed = grad_normed_ema + jnp.einsum(
        "tv,dv->td", grad_value_low, value_back, preferred_element_type=jnp.float32
    )
    grad_input, gain_one_grad = norm_back(grad_normed)
    grad_tokens = (grad_input + grad_after * (1.0 - update_gate)).astype(jnp.bfloat16)
    gains_grad = jnp.stack([gain_one_grad, gain_two_grad, omega_grad])
    small_totals = (
        lax.psum_scatter(gains_grad, ("dp", "fsdp"), scatter_dimension=1, tiled=True),
        lax.psum_scatter(ema_grad, ("dp", "fsdp"), scatter_dimension=1, tiled=True),
        lax.psum_scatter(attn_grad, ("dp", "fsdp"), scatter_dimension=0, tiled=True),
    )
    totals = reduce_gradients(value_grad, mix_grad, merge_grad, up_grad, down_grad)
    return (
        result,
        grad_tokens,
        totals[0],
        totals[1],
        totals[2],
        totals[3],
        totals[4],
        small_totals[0],
        small_totals[1],
        small_totals[2],
    )


def solution(mesh):
    in_specs = (
        P(("dp", "fsdp"), None),
        P(("dp", "fsdp"), None),
        P(("dp", "fsdp"), None),
        P("dp", "fsdp"),
        P("dp", "fsdp"),
        P("dp", "fsdp"),
        P("dp", "fsdp"),
        P("dp", "fsdp"),
        P(None, ("dp", "fsdp")),
        P(None, ("dp", "fsdp"), None),
        P(("dp", "fsdp")),
    )
    out_specs = (
        P(("dp", "fsdp"), None),
        P(("dp", "fsdp"), None),
        P("dp", "fsdp"),
        P("dp", "fsdp"),
        P("dp", "fsdp"),
        P("dp", "fsdp"),
        P("dp", "fsdp"),
        P(None, ("dp", "fsdp")),
        P(None, ("dp", "fsdp"), None),
        P(("dp", "fsdp")),
    )
    return jax.shard_map(
        on_device, mesh=mesh, in_specs=in_specs, out_specs=out_specs, check_vma=False
    )
```

profile of v0, /device:TPU:0, one launch (start us, length us, event | category | flops | bytes accessed | tf_op | source)
XLA Modules:
  0.0 1848.4 jit_solution(17480808488657259730)
XLA Ops:
  10.6 23.8 %all-gather.16.cloned.1.call-done = bf16[1024,512]{1,0:T(8,128)(2,1)} async-done(((bf16[128,512]{1,0:T(8,128)(2,1)}), bf16[1024,512]{1,0:T(8,128)(2,1)}) %all-gather.16.cloned.1.call-update) | async-done | bytes 1048592 | tf_op jit(solution)/shard_map/all_gather | solution.py:85
  34.5 32.5 %all-gather.12.cloned.1.call-done = bf16[1024,1056]{0,1:T(8,128)(2,1)} async-done(((bf16[128,1056]{0,1:T(8,128)(2,1)}), bf16[1024,1056]{0,1:T(8,128)(2,1)}) %all-gather.12.cloned.1.call-update) | async-done | bytes 2162704 | tf_op jit(solution)/shard_map/all_gather | solution.py:86
  67.1 22.7 %all-gather.20.cloned.1.call-done = bf16[2048,256]{1,0:T(8,128)(2,1)} async-done(((bf16[256,256]{1,0:T(8,128)(2,1)}), bf16[2048,256]{1,0:T(8,128)(2,1)}) %all-gather.20.cloned.1.call-update) | async-done | bytes 1048592 | tf_op jit(solution)/shard_map/all_gather | solution.py:87
  89.9 30.1 %all-gather.24.cloned.1.call-done = bf16[1024,1024]{1,0:T(8,128)(2,1)} async-done(((bf16[128,1024]{1,0:T(8,128)(2,1)}), bf16[1024,1024]{1,0:T(8,128)(2,1)}) %all-gather.24.cloned.1.call-update) | async-done | bytes 2097168 | tf_op jit(solution)/shard_map/all_gather | solution.py:88
  120.6 67.3 %all-gather = bf16[32,32,3]{1,2,0:T(4,128)(2,1)S(1)} all-gather(bf16[1,32,3]{1,2,0:T(4,128)(2,1)S(1)} %bitcast.333), channel_id=1, replica_groups=mesh['dp'=8,'fsdp'=4] {'dp','fsdp'}, dimensions={0}, use_global_device_ids=true | all-gather | bytes 6336 | tf_op jit(solution)/shard_map/all_gather | solution.py:168
  188.0 75.2 %all_gather.49 = bf16[4,1024,16]{2,0,1:T(4,128)(2,1)S(1)} all-gather(bf16[4,32,16]{2,0,1:T(4,128)(2,1)S(1)} %copy.147), channel_id=1, replica_groups=mesh['dp'=8,'fsdp'=4] {'dp','fsdp'}, dimensions={1}, use_global_device_ids=true | all-gather | bytes 135168 | tf_op jit(solution)/shard_map/all_gather | solution.py:169
  319.9 201.4 %while.41 = (s32[]{:T(128)}, f32[1024,16]{0,1:T(8,128)S(1)}, f32[8,32,1024]{2,1,0:T(8,128)}, f32[8,1024,16]{1,2,0:T(8,128)}, pred[8]{0:T(512)(128)(4,1)S(1)}, /*...) while((s32[]{:T(128)}, f32[1024,16]{0,1:T(8,128)S(1)}, ...), condition=%wide.region_5.6_spmd.clone, body=%wide.region_4.5_spmd.clone.sunk | while | flops 4210691 | bytes 11207321 | solution.py:62
  522.4 37.6 %all-reduce.8 = bf16[512]{0:T(512)(128)(2,1)S(1)} all-reduce(bf16[512]{0:T(512)(128)(2,1)S(1)} %dynamic-update-slice), channel_id=1, replica_groups=mesh['dp'=8,'fsdp'=4] {'dp','fsdp'}, use_global_device_ids=true, to_apply=%add.8 | all-reduce | flops 512 | bytes 2048
  670.3 694.0 %while.42 = (s32[]{:T(128)}, f32[1024,32,32]{2,1,0:T(8,128)}, f32[1024,16,32]{2,1,0:T(8,128)}, f32[1024,16,33]{1,0,2:T(8,128)}, f32[1024,16,32]{2,1,0:T(8,128)},...) while((s32[]{:T(128)}, f32[1024,32,32]{2,1,0:T(8,128)}, ...), condition=%wide.region_14.15_spmd.clone, body=%wide.region_13.14_spmd.clone.sunk | while | flops 32653316 | bytes 103612960 | solution.py:62
  796.0 16.5 bitcast_add_fusion.5
  839.9 16.4 fusion.147
  884.3 16.8 bitcast_add_fusion.5
  928.2 16.4 fusion.147
  972.5 16.5 bitcast_add_fusion.5
  1060.6 16.4 bitcast_add_fusion.5
  1148.4 16.4 bitcast_add_fusion.5
  1438.9 42.2 %all-reduce.9 = f32[512]{0:T(512)S(1)} all-reduce(f32[512]{0:T(512)S(1)} %pad_maximum_fusion.4), channel_id=14, replica_groups=mesh['dp'=8,'fsdp'=4] {'dp','fsdp'}, use_global_device_ids=true, to_apply=%region_39.40.clone | all-reduce | flops 512 | bytes 4096
  1491.8 70.7 %reduce-scatter.39.cloned.1.call-done = f32[32,3]{1,0:T(8,128)} async-done(((f32[1024,3]{1,0:T(8,128)}), f32[32,3]{1,0:T(8,128)}) %reduce-scatter.39.cloned.1.call-update) | async-done | bytes 400
  1563.8 131.7 %reduce-scatter.41.cloned.1.call-done = f32[32,64]{1,0:T(8,128)} async-done(((f32[1024,64]{1,0:T(8,128)}), f32[32,64]{1,0:T(8,128)}) %reduce-scatter.41.cloned.1.call-update) | async-done | bytes 8208
  1697.0 22.1 %reduce-scatter.27.cloned.1.call-done = bf16[256,256]{1,0:T(8,128)(2,1)} async-done(((bf16[256,1024]{1,0:T(8,128)(2,1)}), bf16[256,256]{1,0:T(8,128)(2,1)}) %reduce-scatter.27.cloned.1.call-update) | async-done | bytes 131088 | tf_op jit(solution)/shard_map/reduce_scatter | solution.py:142
  1720.7 26.2 %reduce-scatter.21.cloned.1.call-done = bf16[128,512]{1,0:T(8,128)(2,1)} async-done(((bf16[128,2048]{1,0:T(8,128)(2,1)}), bf16[128,512]{1,0:T(8,128)(2,1)}) %reduce-scatter.21.cloned.1.call-update) | async-done | bytes 131088 | tf_op jit(solution)/shard_map/reduce_scatter | solution.py:136
  1748.6 28.8 %reduce-scatter.35.cloned.1.call-done = bf16[512,256]{1,0:T(8,128)(2,1)} async-done(((bf16[512,1024]{1,0:T(8,128)(2,1)}), bf16[512,256]{1,0:T(8,128)(2,1)}) %reduce-scatter.35.cloned.1.call-update) | async-done | bytes 262160 | tf_op jit(solution)/shard_map/reduce_scatter | solution.py:148
  1779.2 29.1 %reduce-scatter.31.cloned.1.call-done = bf16[128,1024]{1,0:T(8,128)(2,1)} async-done(((bf16[128,4096]{1,0:T(8,128)(2,1)}), bf16[128,1024]{1,0:T(8,128)(2,1)}) %reduce-scatter.31.cloned.1.call-update) | async-done | bytes 262160 | tf_op jit(solution)/shard_map/reduce_scatter | solution.py:145
  1810.1 29.1 %reduce-scatter.37.cloned.1.call-done = bf16[1056,128]{1,0:T(8,128)(2,1)} async-done(((bf16[4224,128]{1,0:T(8,128)(2,1)}), bf16[1056,128]{1,0:T(8,128)(2,1)}) %reduce-scatter.37.cloned.1.call-update) | async-done | bytes 270352
  (772 shorter events, 1045.6 us)
Async XLA Ops:
  7.2 27.3 %all-gather.16.cloned.1.call-start = ((), (), s32[]{:S(2)}) async-start(), calls=%async_computation.14 | async-start | bytes 1179648 | tf_op jit(solution)/shard_map/all_gather | solution.py:85
  7.9 59.1 %all-gather.12.cloned.1.call-start = ((), (), s32[]{:S(2)}) async-start(), calls=%async_computation.12 | async-start | bytes 2433024 | tf_op jit(solution)/shard_map/all_gather | solution.py:86
  8.7 81.1 %all-gather.20.cloned.1.call-start = ((), (), s32[]{:S(2)}) async-start(), calls=%async_computation.16 | async-start | bytes 1179648 | tf_op jit(solution)/shard_map/all_gather | solution.py:87
  9.4 110.6 %all-gather.24.cloned.1.call-start = ((), (), s32[]{:S(2)}) async-start(), calls=%async_computation.18 | async-start | bytes 2359296 | tf_op jit(solution)/shard_map/all_gather | solution.py:88
  10.0 308.5 %all-gather.28.cloned.1.call-start = ((), (), s32[]{:S(2)}) async-start(), calls=%async_computation.20 | async-start | bytes 2359296 | tf_op jit(solution)/shard_map/all_gather | solution.py:89
  10.6 557.0 %all-gather.18.cloned.1.call-start = ((), (), s32[]{:S(2)}) async-start(), calls=%async_computation.15 | async-start | bytes 5242880 | tf_op jit(solution)/shard_map/all_gather | solution.py:92
  34.5 538.0 %all-gather.14.cloned.1.call-start = ((), (), s32[]{:S(2)}) async-start(), calls=%async_computation.13 | async-start | bytes 10813440 | tf_op jit(solution)/shard_map/all_gather | solution.py:93
  67.1 516.4 %all-gather.22.cloned.1.call-start = ((), (), s32[]{:S(2)}) async-start(), calls=%async_computation.17 | async-start | bytes 5242880 | tf_op jit(solution)/shard_map/all_gather | solution.py:94
  89.8 499.6 %all-gather.26.cloned.1.call-start = ((), (), s32[]{:S(2)}) async-start(), calls=%async_computation.19 | async-start | bytes 10485760 | tf_op jit(solution)/shard_map/all_gather | solution.py:95
  120.0 477.3 %all-gather.30.cloned.1.call-start = ((), (), s32[]{:S(2)}) async-start(), calls=%async_computation.21 | async-start | bytes 10485760 | tf_op jit(solution)/shard_map/all_gather | solution.py:96
  318.6 1111.4 %reduce-scatter.25.cloned.1.call-start = ((), (), s32[]{:S(2)}) async-start(), calls=%async_computation.25 | async-start | bytes 4718592 | tf_op jit(solution)/shard_map/reduce_scatter | solution.py:125
  619.3 811.4 %reduce-scatter.19.cloned.1.call-start = ((), (), s32[]{:S(2)}) async-start(), calls=%async_computation.22 | async-start | bytes 4718592 | tf_op jit(solution)/shard_map/reduce_scatter | solution.py:119
  632.2 799.2 %reduce-scatter.33.cloned.1.call-start = ((), (), s32[]{:S(2)}) async-start(), calls=%async_computation.29 | async-start | bytes 9437184 | tf_op jit(solution)/shard_map/reduce_scatter | solution.py:131
  640.7 791.2 %reduce-scatter.29.cloned.1.call-start = ((), (), s32[]{:S(2)}) async-start(), calls=%async_computation.27 | async-start | bytes 9437184 | tf_op jit(solution)/shard_map/reduce_scatter | solution.py:128
  648.3 784.8 %reduce-scatter.23.cloned.1.call-start = ((), (), s32[]{:S(2)}) async-start(), calls=%async_computation.24 | async-start | bytes 9732096 | tf_op jit(solution)/shard_map/reduce_scatter | solution.py:122
  661.6 900.9 %reduce-scatter.39.cloned.1.call-start = ((), (), s32[]{:S(2)}) async-start(), calls=%async_computation.32 | async-start | bytes 540672
  670.3 695.5 %copy-start.48 = (f32[1,1024]{1,0:T(1,128)S(1)}, f32[1,1024]{1,0:T(1,128)}, u32[]{:S(2)}) copy-start(f32[1,1024]{1,0:T(1,128)} %copy-done.47) | copy-start | bytes 12292
  670.3 695.5 %copy-start.51 = (f32[256]{0:T(256)S(1)}, f32[256]{0:T(256)}, u32[]{:S(2)}) copy-start(f32[256]{0:T(256)} %copy-done.50) | copy-start | bytes 3076
  1427.2 268.3 %reduce-scatter.41.cloned.1.call-start = ((), (), s32[]{:S(2)}) async-start(), calls=%async_computation.33 | async-start | bytes 540672
  1429.9 289.2 %reduce-scatter.27.cloned.1.call-start = ((), (), s32[]{:S(2)}) async-start(), calls=%async_computation.26 | async-start | bytes 655360 | tf_op jit(solution)/shard_map/reduce_scatter | solution.py:142
  1430.5 316.5 %reduce-scatter.21.cloned.1.call-start = ((), (), s32[]{:S(2)}) async-start(), calls=%async_computation.23 | async-start | bytes 655360 | tf_op jit(solution)/shard_map/reduce_scatter | solution.py:136
  1431.3 346.1 %reduce-scatter.35.cloned.1.call-start = ((), (), s32[]{:S(2)}) async-start(), calls=%async_computation.30 | async-start | bytes 1310720 | tf_op jit(solution)/shard_map/reduce_scatter | solution.py:148
  1431.9 376.4 %reduce-scatter.31.cloned.1.call-start = ((), (), s32[]{:S(2)}) async-start(), calls=%async_computation.28 | async-start | bytes 1310720 | tf_op jit(solution)/shard_map/reduce_scatter | solution.py:145
  1432.6 406.6 %reduce-scatter.37.cloned.1.call-start = ((), (), s32[]{:S(2)}) async-start(), calls=%async_computation.31 | async-start | bytes 1351680
  (169 other events, 5775.5 us)
Sparse Core Ops, SparseCore 0:
  9.6 24.7 all-gather.15
  36.1 30.9 all-gather.11
  68.7 21.1 all-gather.19
  91.3 28.7 all-gather.23
  121.5 28.6 all-gather.27
  151.8 58.4 all-gather.17
  212.2 99.1 all-gather.13
  313.2 52.5 all-gather.21
  367.7 87.6 all-gather.25
  457.0 88.1 all-gather.29
  619.4 50.7 reduce-scatter.24
  672.3 48.1 reduce-scatter.18
  722.8 87.7 reduce-scatter.32
  812.7 87.9 reduce-scatter.28
  902.9 90.4 reduce-scatter.22
  1427.3 135.0 reduce-scatter.38
  1565.2 130.2 reduce-scatter.40
  1698.2 20.8 reduce-scatter.26
  1722.1 24.7 reduce-scatter.20
  1749.7 27.6 reduce-scatter.34
  1780.6 27.7 reduce-scatter.30
  1811.2 27.9 reduce-scatter.36
where the time goes:
time: 1860 us; the launch traced here: 1850 us
  other arithmetic  528 us (28%)
  waiting for transfers between devices  453 us (24%)
  matrix products  431 us (23%)
  blocking collectives  222 us (12%)
  local copies, waits for them, and re-layouts  194 us (10%)
    unnamed x25, waiting for transfers between devices  237 us
    while x32, other arithmetic  173 us
    dot_general x8, matrix products, advance(): inner_part = jnp.einsum('cts,sc->tc', toeplitz, block_in, precision=highest)  131 us
    add_any x8, other arithmetic, advance(): jnp.einsum('cjs,sc->cj', leaving, block_in, precision=highest)  126 us
    dot_general x8, matrix products, advance(): carried = jnp.einsum('cjt,cj->tc', arriving, ema_state, precision=highest)  123 us
    add_any x8, other arithmetic, advance(): inner_part = jnp.einsum('cts,sc->tc', toeplitz, block_in, precision=highest)  115 us
    unnamed x2, blocking collectives  79.8 us
    all_gather x1, blocking collectives, on_device(): lax.all_gather(ema_params, ('dp', 'fsdp'), axis=1, tiled=True)  75.2 us
  transfers between devices with their start and end apart: 22, of which 11 were waited for; matrix products, arithmetic and copies ran while one was open for 58% of the time, Pallas kernels for 0%

commit v1 on v0

--- a/solution.py
+++ b/solution.py
@@ -1,6 +1,8 @@
 import jax
 import jax.numpy as jnp
 from jax import lax
+from jax.experimental import pallas as pl
+from jax.experimental.pallas import tpu as pltpu
 from jax.sharding import PartitionSpec as P
 
 D = 1024
@@ -26,41 +28,116 @@
     return (places - starts, places < running[-1])
 
 
-def ema_apply(normed, ema_float, omega_gain, position):
-    row_count = normed.shape[0]
-    block_len = STRETCH // 4
-    damping = jax.nn.sigmoid(ema_float[0])
-    decay_gate = jax.nn.sigmoid(ema_float[1])
+def ema_coefficients(ema):
+    damping = jax.nn.sigmoid(ema[0])
+    decay_gate = jax.nn.sigmoid(ema[1])
     keep_rate = 1.0 - damping * decay_gate
-    weights_out = damping * ema_float[2] * ema_float[3] * ema_float.shape[2] ** (-0.5)
-    lag_axis = jnp.arange(block_len + 1, dtype=normed.dtype)
-    powers = jnp.exp(lag_axis[None, None, :] * jnp.log(keep_rate)[:, :, None])
-    kernel = jnp.einsum("cj,cjl->cl", weights_out, powers[:, :, :block_len], precision=highest)
-    offsets = (
-        jnp.arange(block_len, dtype=jnp.int32)[:, None]
-        - jnp.arange(block_len, dtype=jnp.int32)[None, :]
-    )
-    toeplitz = jnp.where(
-        offsets[None] >= 0, jnp.take(kernel, jnp.clip(offsets, 0, block_len - 1), axis=1), 0.0
-    )
-    leaving = powers[:, :, block_len - 1 :: -1]
-    arriving = weights_out[:, :, None] * powers[:, :, 1:]
-    blocks = normed.reshape(row_count // block_len, block_len, normed.shape[1])
-    resets = position.reshape(row_count // block_len, block_len)[:, 0] == 0
-
-    def advance(ema_state, inputs):
-        block_in, is_reset = inputs
-        ema_state = jnp.where(is_reset, 0.0, ema_state)
-        inner_part = jnp.einsum("cts,sc->tc", toeplitz, block_in, precision=highest)
-        carried = jnp.einsum("cjt,cj->tc", arriving, ema_state, precision=highest)
-        ema_state = ema_state * powers[:, :, block_len] + jnp.einsum(
-            "cjs,sc->cj", leaving, block_in, precision=highest
-        )
-        return (ema_state, inner_part + carried)
-
-    zero_state = jnp.zeros(keep_rate.shape, normed.dtype)
-    final_state, mixed_out = lax.scan(advance, zero_state, (blocks, resets))
-    return mixed_out.reshape(row_count, normed.shape[1]) + omega_gain * normed
+    weights_out = damping * ema[2] * ema[3] * ema.shape[1] ** (-0.5)
+    return damping, decay_gate, keep_rate, weights_out
+
+
+CHUNK = 32
+
+
+def ema_forward_kernel(x_ref, ema_ref, omega_ref, keep_ref, y_ref, mark_ref):
+    _, _, rate, weight = ema_coefficients(ema_ref[...])
+    omega = omega_ref[...]
+
+    def chunk(k, state):
+        state = state * keep_ref[k][None]
+        mark_ref[k] = state
+
+        def step(i, state):
+            t = k * CHUNK + i
+            x = x_ref[t]
+            state = rate * state + x[None]
+            y_ref[t] = jnp.sum(weight * state, axis=0) + omega * x
+            return state
+
+        return lax.fori_loop(0, CHUNK, step, state, unroll=4)
+
+    lax.fori_loop(0, x_ref.shape[0] // CHUNK, chunk, jnp.zeros_like(rate))
+
+
+def ema_backward_kernel(x_ref, g_ref, ema_ref, omega_ref, keep_ref, mark_ref, dx_ref, dema_ref, domega_ref, h_ref):
+    ema = ema_ref[...]
+    damping, decay_gate, rate_all, weight_all = ema_coefficients(ema)
+    omega = omega_ref[...]
+    half = rate_all.shape[0] // 2
+    chunks = x_ref.shape[0] // CHUNK
+    sums = []
+    for part in range(2):
+        js = slice(part * half, (part + 1) * half)
+        rate, weight = rate_all[js], weight_all[js]
+        zero = jnp.zeros_like(rate)
+
+        def chunk(m, carry, js=js, rate=rate, weight=weight, part=part):
+            k = chunks - 1 - m
+            h_ref[0] = mark_ref[k, js]
+
+            def ahead(i, state):
+                state = rate * state + x_ref[k * CHUNK + i][None]
+                h_ref[i + 1] = state
+                return state
+
+            lax.fori_loop(0, CHUNK, ahead, h_ref[0], unroll=4)
+
+            def back(n, carry):
+                s, dw, dr, dom = carry
+                i = CHUNK - 1 - n
+                t = k * CHUNK + i
+                g = g_ref[t]
+                s = rate * s + g[None]
+                dx = jnp.sum(weight * s, axis=0)
+                if part == 0:
+                    dx_ref[t] = dx + omega * g
+                    dom = dom + g * x_ref[t]
+                else:
+                    dx_ref[t] = dx_ref[t] + dx
+                dw = dw + h_ref[i + 1] * g[None]
+                dr = dr + h_ref[i] * s
+                return s, dw, dr, dom
+
+            s, dw, dr, dom = lax.fori_loop(0, CHUNK, back, carry, unroll=2)
+            return s * keep_ref[k][None], dw, dr, dom
+
+        out = lax.fori_loop(0, chunks, chunk, (zero, zero, zero, jnp.zeros_like(omega)))
+        sums.append(out)
+    dw = jnp.concatenate([sums[0][1], sums[1][1]], axis=0)
+    dr = jnp.concatenate([sums[0][2], sums[1][2]], axis=0) * weight_all
+    scale = ema.shape[1] ** (-0.5)
+    d_damp = dw * ema[2] * ema[3] * scale - dr * decay_gate
+    dema_ref[0] = d_damp * damping * (1.0 - damping)
+    dema_ref[1] = -dr * damping * decay_gate * (1.0 - decay_gate)
+    dema_ref[2] = dw * damping * ema[3] * scale
+    dema_ref[3] = dw * damping * ema[2] * scale
+    domega_ref[...] = sums[0][3]
+
+
+def ema_keep(position):
+    starts = position.reshape(-1, CHUNK)[:, 0] != 0
+    return jnp.broadcast_to(starts.astype(jnp.float32)[:, None, None], (starts.shape[0], 8, 128))
+
+
+def ema_apply(x, ema, omega, keep):
+    f32 = jnp.float32
+    shape = jax.ShapeDtypeStruct
+    return pl.pallas_call(
+        ema_forward_kernel,
+        out_shape=(shape(x.shape, f32), shape((keep.shape[0],) + ema.shape[1:], f32)),
+        compiler_params=pltpu.CompilerParams(vmem_limit_bytes=32 << 20),
+    )(x, ema, omega, keep)
+
+
+def ema_reverse(x, g, ema, omega, keep, mark):
+    f32 = jnp.float32
+    shape = jax.ShapeDtypeStruct
+    return pl.pallas_call(
+        ema_backward_kernel,
+        out_shape=(shape(x.shape, f32), shape(ema.shape, f32), shape(omega.shape, f32)),
+        scratch_shapes=[pltpu.VMEM((CHUNK + 1, ema.shape[1] // 2) + ema.shape[2:], f32)],
+        compiler_params=pltpu.CompilerParams(vmem_limit_bytes=32 << 20),
+    )(x, g, ema, omega, keep, mark)
 
 
 def silu_slope(values):
@@ -81,23 +158,6 @@
 
 
 def gather_forward(value_proj, mix_proj, merge_proj, up_proj, down_proj):
-    first = (
-        lax.all_gather(value_proj, "dp", axis=0, tiled=True),
-        lax.all_gather(mix_proj, "dp", axis=0, tiled=True),
-        lax.all_gather(merge_proj, "dp", axis=0, tiled=True),
-        lax.all_gather(up_proj, "dp", axis=0, tiled=True),
-        lax.all_gather(down_proj, "dp", axis=0, tiled=True),
-    )
-    return (
-        lax.all_gather(first[0], "fsdp", axis=1, tiled=True),
-        lax.all_gather(first[1], "fsdp", axis=1, tiled=True),
-        lax.all_gather(first[2], "fsdp", axis=1, tiled=True),
-        lax.all_gather(first[3], "fsdp", axis=1, tiled=True),
-        lax.all_gather(first[4], "fsdp", axis=1, tiled=True),
-    )
-
-
-def gather_backward(value_proj, mix_proj, merge_proj, up_proj, down_proj):
     first = (
         lax.all_gather(value_proj, "dp", axis=0, tiled=True),
         lax.all_gather(mix_proj, "dp", axis=0, tiled=True),
@@ -183,10 +243,13 @@
     value_pre = jnp.dot(normed_low, value_full, preferred_element_type=jnp.float32)
     value_low = jax.nn.silu(value_pre).astype(jnp.bfloat16)
 
-    def ema_local(normed_in, ema_in, omega_in):
-        return ema_apply(normed_in, ema_in, omega_in, position)
-
-    ema_out, ema_back = jax.vjp(ema_local, normed, ema_float, gains_float[2])
+    lanes = (8, tokens.shape[1] // 8)
+    ema_by_state = jnp.swapaxes(ema_float, 1, 2).reshape(4, -1, *lanes)
+    omega = gains_float[2].reshape(lanes)
+    keep = ema_keep(position)
+    normed_rows = normed.reshape(row_count, *lanes)
+    ema_rows, ema_marks = ema_apply(normed_rows, ema_by_state, omega, keep)
+    ema_out = ema_rows.reshape(row_count, -1)
     mixed_low = jax.nn.silu(ema_out).astype(jnp.bfloat16)
     projected = jnp.dot(mixed_low, mix_full, preferred_element_type=jnp.float32)
     update_gate = jax.nn.sigmoid(projected[:, :D])
@@ -230,8 +293,8 @@
     result = (after_mixer + jnp.dot(up_low, down_full, preferred_element_type=jnp.float32)).astype(
         jnp.bfloat16
     )
-    value_back, mix_back, merge_back, up_back, down_back = gather_backward(
-        value_proj, mix_proj, merge_proj, up_proj, down_proj
+    value_back, mix_back, merge_back, up_back, down_back = (
+        value_full, mix_full, merge_full, up_full, down_full
     )
     grad_rows = cotangent.astype(jnp.float32) * live_rows[:, None].astype(jnp.float32)
     grad_down_low = grad_rows.astype(jnp.bfloat16)
@@ -315,7 +378,13 @@
     grad_mixed = jnp.einsum(
         "tm,dm->td", grad_projected_low, mix_back, preferred_element_type=jnp.float32
     )
-    grad_normed_ema, ema_grad, omega_grad = ema_back(grad_mixed * silu_slope(ema_out))
+    grad_ema_rows = (grad_mixed * silu_slope(ema_out)).reshape(row_count, *lanes)
+    grad_normed_rows, ema_grad_rows, omega_grad = ema_reverse(
+        normed_rows, grad_ema_rows, ema_by_state, omega, keep, ema_marks
+    )
+    grad_normed_ema = grad_normed_rows.reshape(row_count, -1)
+    ema_grad = jnp.swapaxes(ema_grad_rows.reshape(4, -1, tokens.shape[1]), 1, 2)
+    omega_grad = omega_grad.reshape(-1)
     grad_value_low = (grad_value_act * silu_slope(value_pre)).astype(jnp.bfloat16)
     value_grad = jnp.einsum(
         "td,tv->dv", normed_low, grad_value_low, preferred_element_type=jnp.float32

time: 1860 us -> 1370 us (0.74)
  waiting for transfers between devices: 453 us -> 972 us
  other arithmetic: 528 us -> 24.1 us
  matrix products: 431 us -> 99.9 us
  local copies, waits for them, and re-layouts: 194 us -> 24.5 us
    dot_general x24 -> x0, matrix products: 328 us -> none  [the longest x8 131 us: advance(): inner_part = jnp.einsum('cts,sc->tc', toeplitz, block_in, precision=highest)]
    add_any x26 -> x0, other arithmetic: 267 us -> none  [the longest x8 126 us: advance(): jnp.einsum('cjs,sc->cj', leaving, block_in, precision=highest)]
    while x32 -> x0, other arithmetic: 173 us -> none
    while x220 -> x0, local copies, waits for them, and re-layouts: 92.2 us -> none
    reduce_scatter x1, waiting for transfers between devices: 0.02 us -> 92.2 us  [reduce_gradients(): lax.psum_scatter(mix_grad.astype(jnp.bfloat16), 'dp', scatter_dimension=0...]
    reduce_scatter x1, waiting for transfers between devices: 0.02 us -> 90.1 us  [reduce_gradients(): lax.psum_scatter(down_grad.astype(jnp.bfloat16), 'dp', scatter_dimension=...]
    reduce_scatter x1, waiting for transfers between devices: 0.02 us -> 89.9 us  [reduce_gradients(): lax.psum_scatter(up_grad.astype(jnp.bfloat16), 'dp', scatter_dimension=0,...]
    all_gather x1, waiting for transfers between devices: 0.02 us -> 82.6 us  [gather_forward(): lax.all_gather(first[3], 'fsdp', axis=1, tiled=True)]
  transfers between devices with their start and end apart: 22 -> 22, of which waited for: 11 -> 19; matrix products, arithmetic and copies ran while one was open for 58% -> 8% of each run, Pallas kernels for 0% -> 1%
where the time goes in v1:
time: 1370 us
  waiting for transfers between devices  972 us (71%)
  blocking collectives  218 us (16%)
  matrix products  99.9 us (7%)
  local copies, waits for them, and re-layouts  24.5 us (2%)
  other arithmetic  24.1 us (2%)
  between operations  15.5 us (1%)
    unnamed x25, waiting for transfers between devices  245 us
    reduce_scatter x1, waiting for transfers between devices, reduce_gradients(): lax.psum_scatter(mix_grad.astype(jnp.bfloat16), 'dp', scatter_dimension=0...  92.2 us
    reduce_scatter x1, waiting for transfers between devices, reduce_gradients(): lax.psum_scatter(down_grad.astype(jnp.bfloat16), 'dp', scatter_dimension=...  90.1 us
    reduce_scatter x1, waiting for transfers between devices, reduce_gradients(): lax.psum_scatter(up_grad.astype(jnp.bfloat16), 'dp', scatter_dimension=0,...  89.9 us
    all_gather x1, waiting for transfers between devices, gather_forward(): lax.all_gather(first[3], 'fsdp', axis=1, tiled=True)  82.6 us
    all_gather x1, waiting for transfers between devices, gather_forward(): lax.all_gather(first[4], 'fsdp', axis=1, tiled=True)  81.1 us
    all_gather x1, blocking collectives, on_device(): lax.all_gather(ema_params, ('dp', 'fsdp'), axis=1, tiled=True)  75.9 us
    unnamed x2, blocking collectives  75.5 us
  transfers between devices with their start and end apart: 22, of which 19 were waited for; matrix products, arithmetic and copies ran while one was open for 8% of the time, Pallas kernels for 1%

profile of v1, /device:TPU:0, one launch (start us, length us, event | category | flops | bytes accessed | tf_op | source)
XLA Modules:
  0.0 1368.6 jit_solution(17421343836478509568)
XLA Ops:
  10.6 23.8 %all-gather.16.cloned.1.call-done = bf16[1024,512]{1,0:T(8,128)(2,1)} async-done(((bf16[128,512]{1,0:T(8,128)(2,1)}), bf16[1024,512]{1,0:T(8,128)(2,1)}) %all-gather.16.cloned.1.call-update) | async-done | bytes 1048592 | tf_op jit(solution)/shard_map/all_gather | solution.py:162
  34.5 32.5 %all-gather.12.cloned.1.call-done = bf16[1024,1056]{0,1:T(8,128)(2,1)} async-done(((bf16[128,1056]{0,1:T(8,128)(2,1)}), bf16[1024,1056]{0,1:T(8,128)(2,1)}) %all-gather.12.cloned.1.call-update) | async-done | bytes 2162704 | tf_op jit(solution)/shard_map/all_gather | solution.py:163
  67.1 22.7 %all-gather.20.cloned.1.call-done = bf16[2048,256]{1,0:T(8,128)(2,1)} async-done(((bf16[256,256]{1,0:T(8,128)(2,1)}), bf16[2048,256]{1,0:T(8,128)(2,1)}) %all-gather.20.cloned.1.call-update) | async-done | bytes 1048592 | tf_op jit(solution)/shard_map/all_gather | solution.py:164
  89.9 30.1 %all-gather.24.cloned.1.call-done = bf16[1024,1024]{1,0:T(8,128)(2,1)} async-done(((bf16[128,1024]{1,0:T(8,128)(2,1)}), bf16[1024,1024]{1,0:T(8,128)(2,1)}) %all-gather.24.cloned.1.call-update) | async-done | bytes 2097168 | tf_op jit(solution)/shard_map/all_gather | solution.py:165
  120.1 30.0 %all-gather.28.cloned.1.call-done = bf16[4096,256]{1,0:T(8,128)(2,1)} async-done(((bf16[512,256]{1,0:T(8,128)(2,1)}), bf16[4096,256]{1,0:T(8,128)(2,1)}) %all-gather.28.cloned.1.call-update) | async-done | bytes 2097168 | tf_op jit(solution)/shard_map/all_gather | solution.py:166
  150.2 66.9 %all-gather = bf16[32,32,3]{1,2,0:T(4,128)(2,1)S(1)} all-gather(bf16[1,32,3]{1,2,0:T(4,128)(2,1)S(1)} %bitcast.179), channel_id=1, replica_groups=mesh['dp'=8,'fsdp'=4] {'dp','fsdp'}, dimensions={0}, use_global_device_ids=true | all-gather | bytes 6336 | tf_op jit(solution)/shard_map/all_gather | solution.py:228
  218.3 75.9 %all_gather.40 = bf16[4,1024,16]{2,0,1:T(4,128)(2,1)S(1)} all-gather(bf16[4,32,16]{2,0,1:T(4,128)(2,1)S(1)} %copy.55), channel_id=1, replica_groups=mesh['dp'=8,'fsdp'=4] {'dp','fsdp'}, dimensions={1}, use_global_device_ids=true | all-gather | bytes 135168 | tf_op jit(solution)/shard_map/all_gather | solution.py:229
  299.2 37.4 %all-reduce = bf16[512]{0:T(512)(128)(2,1)S(1)} all-reduce(bf16[512]{0:T(512)(128)(2,1)S(1)} %dynamic-update-slice), channel_id=1, replica_groups=mesh['dp'=8,'fsdp'=4] {'dp','fsdp'}, use_global_device_ids=true, to_apply=%add | all-reduce | flops 512 | bytes 2048
  375.5 82.6 %all-gather.26.cloned.1.call-done = bf16[1024,4096]{1,0:T(8,128)(2,1)} async-done(((bf16[1024,1024]{1,0:T(8,128)(2,1)}), bf16[1024,4096]{1,0:T(8,128)(2,1)}) %all-gather.26.cloned.1.call-update) | async-done | bytes 8388624 | tf_op jit(solution)/shard_map/all_gather | solution.py:172
  466.1 81.1 %all-gather.30.cloned.1.call-done = bf16[4096,1024]{1,0:T(8,128)(2,1)} async-done(((bf16[4096,256]{1,0:T(8,128)(2,1)}), bf16[4096,1024]{1,0:T(8,128)(2,1)}) %all-gather.30.cloned.1.call-update) | async-done | bytes 8388624 | tf_op jit(solution)/shard_map/all_gather | solution.py:173
  587.4 8.3 convolution_convert_fusion.1
  617.6 8.9 shard_map.187
  634.1 40.7 %reduce-scatter.25.cloned.1.call-done = bf16[256,1024]{1,0:T(8,128)(2,1)} async-done(((bf16[2048,1024]{1,0:T(8,128)(2,1)}), bf16[256,1024]{1,0:T(8,128)(2,1)}) %reduce-scatter.25.cloned.1.call-update) | async-done | bytes 524304 | tf_op jit(solution)/shard_map/reduce_scatter | solution.py:185
  674.9 89.9 %reduce-scatter.29.cloned.1.call-done = bf16[128,4096]{1,0:T(8,128)(2,1)} async-done(((bf16[1024,4096]{1,0:T(8,128)(2,1)}), bf16[128,4096]{1,0:T(8,128)(2,1)}) %reduce-scatter.29.cloned.1.call-update) | async-done | bytes 1048592 | tf_op jit(solution)/shard_map/reduce_scatter | solution.py:188
  764.9 90.1 %reduce-scatter.33.cloned.1.call-done = bf16[512,1024]{1,0:T(8,128)(2,1)} async-done(((bf16[4096,1024]{1,0:T(8,128)(2,1)}), bf16[512,1024]{1,0:T(8,128)(2,1)}) %reduce-scatter.33.cloned.1.call-update) | async-done | bytes 1048592 | tf_op jit(solution)/shard_map/reduce_scatter | solution.py:191
  855.4 92.2 %reduce-scatter.23.cloned.1.call-done = bf16[128,4224]{1,0:T(8,128)(2,1)} async-done(((bf16[1024,4224]{1,0:T(8,128)(2,1)}), bf16[128,4224]{1,0:T(8,128)(2,1)}) %reduce-scatter.23.cloned.1.call-update) | async-done | bytes 1081360 | tf_op jit(solution)/shard_map/reduce_scatter | solution.py:182
  953.5 38.1 %all-reduce.1 = f32[512]{0:T(512)S(1)} all-reduce(f32[512]{0:T(512)S(1)} %pad_maximum_fusion.4), channel_id=14, replica_groups=mesh['dp'=8,'fsdp'=4] {'dp','fsdp'}, use_global_device_ids=true, to_apply=%region_31.32.clone | all-reduce | flops 512 | bytes 4096
  1002.2 80.6 %reduce-scatter.39.cloned.1.call-done = f32[32,3]{1,0:T(8,128)} async-done(((f32[1024,3]{1,0:T(8,128)}), f32[32,3]{1,0:T(8,128)}) %reduce-scatter.39.cloned.1.call-update) | async-done | bytes 400
  1084.2 131.3 %reduce-scatter.41.cloned.1.call-done = f32[32,64]{1,0:T(8,128)} async-done(((f32[1024,64]{1,0:T(8,128)}), f32[32,64]{1,0:T(8,128)}) %reduce-scatter.41.cloned.1.call-update) | async-done | bytes 8208
  1217.0 22.0 %reduce-scatter.21.cloned.1.call-done = bf16[128,512]{1,0:T(8,128)(2,1)} async-done(((bf16[128,2048]{1,0:T(8,128)(2,1)}), bf16[128,512]{1,0:T(8,128)(2,1)}) %reduce-scatter.21.cloned.1.call-update) | async-done | bytes 131088 | tf_op jit(solution)/shard_map/reduce_scatter | solution.py:196
  1240.6 26.2 %reduce-scatter.27.cloned.1.call-done = bf16[256,256]{1,0:T(8,128)(2,1)} async-done(((bf16[256,1024]{1,0:T(8,128)(2,1)}), bf16[256,256]{1,0:T(8,128)(2,1)}) %reduce-scatter.27.cloned.1.call-update) | async-done | bytes 131088 | tf_op jit(solution)/shard_map/reduce_scatter | solution.py:202
  1268.5 28.9 %reduce-scatter.31.cloned.1.call-done = bf16[128,1024]{1,0:T(8,128)(2,1)} async-done(((bf16[128,4096]{1,0:T(8,128)(2,1)}), bf16[128,1024]{1,0:T(8,128)(2,1)}) %reduce-scatter.31.cloned.1.call-update) | async-done | bytes 262160 | tf_op jit(solution)/shard_map/reduce_scatter | solution.py:205
  1299.2 29.1 %reduce-scatter.35.cloned.1.call-done = bf16[512,256]{1,0:T(8,128)(2,1)} async-done(((bf16[512,1024]{1,0:T(8,128)(2,1)}), bf16[512,256]{1,0:T(8,128)(2,1)}) %reduce-scatter.35.cloned.1.call-update) | async-done | bytes 262160 | tf_op jit(solution)/shard_map/reduce_scatter | solution.py:208
  1330.1 29.1 %reduce-scatter.37.cloned.1.call-done = bf16[1056,128]{1,0:T(8,128)(2,1)} async-done(((bf16[4224,128]{1,0:T(8,128)(2,1)}), bf16[1056,128]{1,0:T(8,128)(2,1)}) %reduce-scatter.37.cloned.1.call-update) | async-done | bytes 270352
  (225 shorter events, 154.5 us)
Async XLA Ops:
  7.2 27.3 %all-gather.16.cloned.1.call-start = ((), (), s32[]{:S(2)}) async-start(), calls=%async_computation.14 | async-start | bytes 1179648 | tf_op jit(solution)/shard_map/all_gather | solution.py:162
  7.9 59.1 %all-gather.12.cloned.1.call-start = ((), (), s32[]{:S(2)}) async-start(), calls=%async_computation.12 | async-start | bytes 2433024 | tf_op jit(solution)/shard_map/all_gather | solution.py:163
  8.7 81.1 %all-gather.20.cloned.1.call-start = ((), (), s32[]{:S(2)}) async-start(), calls=%async_computation.16 | async-start | bytes 1179648 | tf_op jit(solution)/shard_map/all_gather | solution.py:164
  9.4 110.6 %all-gather.24.cloned.1.call-start = ((), (), s32[]{:S(2)}) async-start(), calls=%async_computation.18 | async-start | bytes 2359296 | tf_op jit(solution)/shard_map/all_gather | solution.py:165
  10.0 140.1 %all-gather.28.cloned.1.call-start = ((), (), s32[]{:S(2)}) async-start(), calls=%async_computation.20 | async-start | bytes 2359296 | tf_op jit(solution)/shard_map/all_gather | solution.py:166
  10.6 335.8 %all-gather.18.cloned.1.call-start = ((), (), s32[]{:S(2)}) async-start(), calls=%async_computation.15 | async-start | bytes 5242880 | tf_op jit(solution)/shard_map/all_gather | solution.py:169
  34.5 317.3 %all-gather.14.cloned.1.call-start = ((), (), s32[]{:S(2)}) async-start(), calls=%async_computation.13 | async-start | bytes 10813440 | tf_op jit(solution)/shard_map/all_gather | solution.py:170
  67.0 301.5 %all-gather.22.cloned.1.call-start = ((), (), s32[]{:S(2)}) async-start(), calls=%async_computation.17 | async-start | bytes 5242880 | tf_op jit(solution)/shard_map/all_gather | solution.py:171
  89.8 368.2 %all-gather.26.cloned.1.call-start = ((), (), s32[]{:S(2)}) async-start(), calls=%async_computation.19 | async-start | bytes 10485760 | tf_op jit(solution)/shard_map/all_gather | solution.py:172
  120.0 427.2 %all-gather.30.cloned.1.call-start = ((), (), s32[]{:S(2)}) async-start(), calls=%async_computation.21 | async-start | bytes 10485760 | tf_op jit(solution)/shard_map/all_gather | solution.py:173
  150.1 483.7 %reduce-scatter.19.cloned.1.call-start = ((), (), s32[]{:S(2)}) async-start(), calls=%async_computation.22 | async-start | bytes 4718592 | tf_op jit(solution)/shard_map/reduce_scatter | solution.py:179
  574.3 100.5 %reduce-scatter.25.cloned.1.call-start = ((), (), s32[]{:S(2)}) async-start(), calls=%async_computation.25 | async-start | bytes 4718592 | tf_op jit(solution)/shard_map/reduce_scatter | solution.py:185
  579.1 185.8 %reduce-scatter.29.cloned.1.call-start = ((), (), s32[]{:S(2)}) async-start(), calls=%async_computation.27 | async-start | bytes 9437184 | tf_op jit(solution)/shard_map/reduce_scatter | solution.py:188
  587.2 267.8 %reduce-scatter.33.cloned.1.call-start = ((), (), s32[]{:S(2)}) async-start(), calls=%async_computation.29 | async-start | bytes 9437184 | tf_op jit(solution)/shard_map/reduce_scatter | solution.py:191
  595.8 351.9 %reduce-scatter.23.cloned.1.call-start = ((), (), s32[]{:S(2)}) async-start(), calls=%async_computation.24 | async-start | bytes 9732096 | tf_op jit(solution)/shard_map/reduce_scatter | solution.py:182
  610.4 472.4 %reduce-scatter.39.cloned.1.call-start = ((), (), s32[]{:S(2)}) async-start(), calls=%async_computation.32 | async-start | bytes 540672
  630.8 584.7 %reduce-scatter.41.cloned.1.call-start = ((), (), s32[]{:S(2)}) async-start(), calls=%async_computation.33 | async-start | bytes 540672
  633.5 605.6 %reduce-scatter.21.cloned.1.call-start = ((), (), s32[]{:S(2)}) async-start(), calls=%async_computation.23 | async-start | bytes 655360 | tf_op jit(solution)/shard_map/reduce_scatter | solution.py:196
  634.0 632.8 %reduce-scatter.27.cloned.1.call-start = ((), (), s32[]{:S(2)}) async-start(), calls=%async_computation.26 | async-start | bytes 655360 | tf_op jit(solution)/shard_map/reduce_scatter | solution.py:202
  674.8 317.3 %copy-start.5 = (f32[256,1024]{1,0:T(8,128)S(1)}, f32[256,1024]{1,0:T(8,128)}, u32[]{:S(2)}) copy-start(f32[256,1024]{1,0:T(8,128)} %copy-done.4) | copy-start | bytes 3145732
  674.9 317.3 %copy-start.18 = (bf16[256,1024]{1,0:T(8,128)(2,1)S(1)}, bf16[256,1024]{1,0:T(8,128)(2,1)}, u32[]{:S(2)}) copy-start(bf16[256,1024]{1,0:T(8,128)(2,1)} %param.12) | copy-start | bytes 1572868
  674.9 622.5 %reduce-scatter.31.cloned.1.call-start = ((), (), s32[]{:S(2)}) async-start(), calls=%async_computation.28 | async-start | bytes 1310720 | tf_op jit(solution)/shard_map/reduce_scatter | solution.py:205
  764.9 563.4 %reduce-scatter.35.cloned.1.call-start = ((), (), s32[]{:S(2)}) async-start(), calls=%async_computation.30 | async-start | bytes 1310720 | tf_op jit(solution)/shard_map/reduce_scatter | solution.py:208
  855.0 504.2 %reduce-scatter.37.cloned.1.call-start = ((), (), s32[]{:S(2)}) async-start(), calls=%async_computation.31 | async-start | bytes 1351680
  (41 other events, 2098.7 us)
Sparse Core Ops, SparseCore 0:
  9.6 24.7 all-gather.15
  36.0 30.9 all-gather.11
  68.6 21.1 all-gather.19
  91.2 28.7 all-gather.23
  121.4 28.5 all-gather.27
  151.7 52.3 all-gather.17
  206.0 106.8 all-gather.13
  314.8 53.7 all-gather.21
  370.4 87.6 all-gather.25
  459.7 87.4 all-gather.29
  574.4 50.0 reduce-scatter.18
  626.6 48.1 reduce-scatter.24
  677.1 87.7 reduce-scatter.28
  767.0 87.9 reduce-scatter.32
  857.2 90.4 reduce-scatter.22
  950.3 132.4 reduce-scatter.38
  1085.5 129.8 reduce-scatter.40
  1218.1 20.8 reduce-scatter.20
  1242.1 24.7 reduce-scatter.26
  1269.6 27.7 reduce-scatter.30
  1300.5 27.7 reduce-scatter.34
  1331.2 27.9 reduce-scatter.36

commit v2 on v1

--- a/solution.py
+++ b/solution.py
@@ -1,3 +1,6 @@
+import functools
+import types
+
 import jax
 import jax.numpy as jnp
 from jax import lax
@@ -11,6 +14,7 @@
 STRETCH = 128
 
 
+DP, FS = "dp", "fsdp"
 highest = lax.Precision.HIGHEST
 
 
@@ -159,54 +163,54 @@
 
 def gather_forward(value_proj, mix_proj, merge_proj, up_proj, down_proj):
     first = (
-        lax.all_gather(value_proj, "dp", axis=0, tiled=True),
-        lax.all_gather(mix_proj, "dp", axis=0, tiled=True),
-        lax.all_gather(merge_proj, "dp", axis=0, tiled=True),
-        lax.all_gather(up_proj, "dp", axis=0, tiled=True),
-        lax.all_gather(down_proj, "dp", axis=0, tiled=True),
+        lax.all_gather(value_proj, DP, axis=0, tiled=True),
+        lax.all_gather(mix_proj, DP, axis=0, tiled=True),
+        lax.all_gather(merge_proj, DP, axis=0, tiled=True),
+        lax.all_gather(up_proj, DP, axis=0, tiled=True),
+        lax.all_gather(down_proj, DP, axis=0, tiled=True),
     )
     return (
-        lax.all_gather(first[0], "fsdp", axis=1, tiled=True),
-        lax.all_gather(first[1], "fsdp", axis=1, tiled=True),
-        lax.all_gather(first[2], "fsdp", axis=1, tiled=True),
-        lax.all_gather(first[3], "fsdp", axis=1, tiled=True),
-        lax.all_gather(first[4], "fsdp", axis=1, tiled=True),
+        lax.all_gather(first[0], FS, axis=1, tiled=True),
+        lax.all_gather(first[1], FS, axis=1, tiled=True),
+        lax.all_gather(first[2], FS, axis=1, tiled=True),
+        lax.all_gather(first[3], FS, axis=1, tiled=True),
+        lax.all_gather(first[4], FS, axis=1, tiled=True),
     )
 
 
 def reduce_gradients(value_grad, mix_grad, merge_grad, up_grad, down_grad):
     first = (
         lax.psum_scatter(
-            value_grad.astype(jnp.bfloat16), "dp", scatter_dimension=0, tiled=True
+            value_grad.astype(jnp.bfloat16), DP, scatter_dimension=0, tiled=True
         ).astype(jnp.float32),
         lax.psum_scatter(
-            mix_grad.astype(jnp.bfloat16), "dp", scatter_dimension=0, tiled=True
+            mix_grad.astype(jnp.bfloat16), DP, scatter_dimension=0, tiled=True
         ).astype(jnp.float32),
         lax.psum_scatter(
-            merge_grad.astype(jnp.bfloat16), "dp", scatter_dimension=0, tiled=True
+            merge_grad.astype(jnp.bfloat16), DP, scatter_dimension=0, tiled=True
         ).astype(jnp.float32),
         lax.psum_scatter(
-            up_grad.astype(jnp.bfloat16), "dp", scatter_dimension=0, tiled=True
+            up_grad.astype(jnp.bfloat16), DP, scatter_dimension=0, tiled=True
         ).astype(jnp.float32),
         lax.psum_scatter(
-            down_grad.astype(jnp.bfloat16), "dp", scatter_dimension=0, tiled=True
+            down_grad.astype(jnp.bfloat16), DP, scatter_dimension=0, tiled=True
         ).astype(jnp.float32),
     )
     return (
         lax.psum_scatter(
-            first[0].astype(jnp.bfloat16), "fsdp", scatter_dimension=1, tiled=True
+            first[0].astype(jnp.bfloat16), FS, scatter_dimension=1, tiled=True
         ).astype(jnp.float32),
         lax.psum_scatter(
-            first[1].astype(jnp.bfloat16), "fsdp", scatter_dimension=1, tiled=True
+            first[1].astype(jnp.bfloat16), FS, scatter_dimension=1, tiled=True
         ).astype(jnp.float32),
         lax.psum_scatter(
-            first[2].astype(jnp.bfloat16), "fsdp", scatter_dimension=1, tiled=True
+            first[2].astype(jnp.bfloat16), FS, scatter_dimension=1, tiled=True
         ).astype(jnp.float32),
         lax.psum_scatter(
-            first[3].astype(jnp.bfloat16), "fsdp", scatter_dimension=1, tiled=True
+            first[3].astype(jnp.bfloat16), FS, scatter_dimension=1, tiled=True
         ).astype(jnp.float32),
         lax.psum_scatter(
-            first[4].astype(jnp.bfloat16), "fsdp", scatter_dimension=1, tiled=True
+            first[4].astype(jnp.bfloat16), FS, scatter_dimension=1, tiled=True
         ).astype(jnp.float32),
     )
 
@@ -225,9 +229,9 @@
     attn_params,
 ):
     gains_full, ema_full, attn_full = (
-        lax.all_gather(norm_gains, ("dp", "fsdp"), axis=1, tiled=True),
-        lax.all_gather(ema_params, ("dp", "fsdp"), axis=1, tiled=True),
-        lax.all_gather(attn_params, ("dp", "fsdp"), axis=0, tiled=True),
+        lax.all_gather(norm_gains, (DP, FS), axis=1, tiled=True),
+        lax.all_gather(ema_params, (DP, FS), axis=1, tiled=True),
+        lax.all_gather(attn_params, (DP, FS), axis=0, tiled=True),
     )
     value_full, mix_full, merge_full, up_full, down_full = gather_forward(
         value_proj, mix_proj, merge_proj, up_proj, down_proj
@@ -396,9 +400,9 @@
     grad_tokens = (grad_input + grad_after * (1.0 - update_gate)).astype(jnp.bfloat16)
     gains_grad = jnp.stack([gain_one_grad, gain_two_grad, omega_grad])
     small_totals = (
-        lax.psum_scatter(gains_grad, ("dp", "fsdp"), scatter_dimension=1, tiled=True),
-        lax.psum_scatter(ema_grad, ("dp", "fsdp"), scatter_dimension=1, tiled=True),
-        lax.psum_scatter(attn_grad, ("dp", "fsdp"), scatter_dimension=0, tiled=True),
+        lax.psum_scatter(gains_grad, (DP, FS), scatter_dimension=1, tiled=True),
+        lax.psum_scatter(ema_grad, (DP, FS), scatter_dimension=1, tiled=True),
+        lax.psum_scatter(attn_grad, (DP, FS), scatter_dimension=0, tiled=True),
     )
     totals = reduce_gradients(value_grad, mix_grad, merge_grad, up_grad, down_grad)
     return (
@@ -415,32 +419,1230 @@
     )
 
 
+STRIP = 128
+MESH = pl.DeviceIdType.MESH
+F32 = jnp.float32
+LOW = jnp.bfloat16
+SHARDED = VALUE, MIX, MERGE, UP, DOWN = range(5)
+
+
+def mm(a, b):
+    return lax.dot_general(a, b, (((1,), (0,)), ((), ())), preferred_element_type=F32)
+
+
+def mm_nt(a, b):
+    return lax.dot_general(a, b, (((1,), (1,)), ((), ())), preferred_element_type=F32)
+
+
+def mm_tn(a, b):
+    return lax.dot_general(a, b, (((0,), (0,)), ((), ())), preferred_element_type=F32)
+
+
+def at_rows(start, size, unit=16):
+    return pl.ds(pl.multiple_of(start, unit), size)
+
+
+def row_loop(count, size, body):
+    def step(i, carry):
+        body(pl.multiple_of(i * size, size))
+        return carry
+
+    lax.fori_loop(0, count // size, step, 0)
+
+
+def slope_of(value, gate):
+    return gate * (1.0 + value * (1.0 - gate))
+
+
+def layer_kernel(trees, depth, *refs):
+    ref, at = types.SimpleNamespace(), 0
+    for tree in trees:
+        ref.__dict__.update(jax.tree.unflatten(tree, refs[at : at + tree.num_leaves]))
+        at += tree.num_leaves
+    tok, cot, gains, ema_in, omega_in, attn = ref.tok, ref.cot, ref.gains, ref.ema_in, ref.omega_in, ref.attn
+    rows, width = tok.shape
+    tiles = width // 128
+    dp, fs = lax.axis_index(DP), lax.axis_index(FS)
+    z, c, y, x = dp // 2, dp % 2, fs // 2, fs % 2
+    q = c * 2 + x
+
+    def place(z, c, y, x):
+        return (z * 2 + c, y * 2 + x)
+
+    sib, xn, xc, yn = place(z, 1 - c, y, x), place(z, c, y, 1 - x), place(z, 1 - c, y, 1 - x), place(z, c, 1 - y, x)
+    zs = [None] + [place((z + d) % depth, c, y, x) for d in range(1, depth)]
+    mates = ((sib, 1 - c, x), (xn, c, 1 - x), (xc, 1 - c, 1 - x))
+    plane = [(pc, py, px) for pc in range(2) for py in range(2) for px in range(2)][1:]
+    plane = [((c + pc) % 2, (y + py) % 2, (x + px) % 2) for pc, py, px in plane]
+
+    barrier = pltpu.get_barrier_semaphore()
+    peers = [place(z, *p) for p in plane] + zs[1:]
+    for peer in peers:
+        pl.semaphore_signal(barrier, inc=1, device_id=peer, device_id_type=MESH)
+    pl.semaphore_wait(barrier, len(peers))
+
+    send_sems, recv_sems, local_sems = ref.send_sems, ref.recv_sems, ref.local_sems
+    used, used_local, pending = [0], [0], []
+
+    def send(src, dst, peer, slot=None):
+        k = used[0]
+        used[0] += 1
+        copy = pltpu.make_async_remote_copy(
+            src_ref=src, dst_ref=dst, send_sem=send_sems.at[k], recv_sem=recv_sems.at[k],
+            device_id=peer, device_id_type=MESH,
+        )
+        copy.start()
+        handle = [k, copy, False]
+        pending.append(handle)
+        return handle
+
+    def sent(handle):
+        if not handle[2]:
+            handle[1].wait_send()
+            handle[2] = True
+
+    def received(handle, landed):
+        k = handle[0]
+        pltpu.make_async_remote_copy(
+            src_ref=landed, dst_ref=landed, send_sem=send_sems.at[k], recv_sem=recv_sems.at[k],
+            device_id=sib, device_id_type=MESH,
+        ).wait_recv()
+
+    def local(src, dst):
+        k = used_local[0]
+        used_local[0] += 1
+        copy = pltpu.make_async_copy(src, dst, local_sems.at[k])
+        copy.start()
+        return copy
+
+    lens = ref.lens
+    ends, run = [], 0
+    for i in range(lens.shape[1]):
+        run = run + lens[0, i]
+        ends.append(run)
+
+    def kept(k):
+        start = 0
+        for i, end in enumerate(ends):
+            start = start + jnp.where(end <= k * CHUNK, lens[0, i], 0)
+        return jnp.where(k * CHUNK - start == 0, 0.0, 1.0)
+
+    def live_rows(r, size):
+        places = r + lax.broadcasted_iota(jnp.int32, (size, 1), 0)
+        return (places < ends[-1]).astype(F32)
+
+    small_all, packed = ref.small_all, ref.packed
+    lane_group = lax.broadcasted_iota(jnp.int32, (1, 128), 1) // 32
+
+    def slot(pc, py, px, pz):
+        return (pc * 4 + py * 2 + px) * depth + pz
+
+    def small_start():
+        return [send(packed, small_all.at[slot(c, y, x, z)], zs[d]) for d in range(1, depth)]
+
+    def small_relay(handles):
+        for d, handle in enumerate(handles):
+            received(handle, small_all.at[slot(c, y, x, (z + depth - 1 - d) % depth)])
+        small_all[slot(c, y, x, z)] = packed[...]
+        mine = small_all.at[pl.ds(slot(c, y, x, 0), depth)]
+        return [send(mine, mine, place(z, *p)) for p in plane]
+
+    def small_finish(handles):
+        for handle, p in zip(handles, plane):
+            received(handle, small_all.at[pl.ds(slot(*p, 0), depth)])
+        states = ema_in.shape[0] // (4 * tiles)
+        gains[...] = jnp.zeros_like(gains)
+        attn[...] = jnp.zeros_like(attn)
+        for t in range(tiles):
+            pz, pc = t // 2, t % 2
+            got = [small_all[slot(pc, f // 2, f % 2, pz)].astype(F32)[0 : states + 8, :] for f in range(4)]
+            for p in range(4):
+                v = jnp.zeros_like(got[0])
+                for f in range(4):
+                    turn = (f - p) * 32 % 128
+                    v = jnp.where(lane_group == f, pltpu.roll(got[f], turn, 1) if turn else got[f], v)
+                ema_in[pl.ds(p * states * tiles + t, states, stride=tiles), :] = v[0:states]
+                row = v[states : states + 1]
+                if p < 3:
+                    gains[p : p + 1, t * 128 : (t + 1) * 128] = row
+                    if p == 2:
+                        omega_in[t : t + 1, :] = row
+                    continue
+                for f in range(4):
+                    turn = (t % 2 * 64 - f * 16) % 128
+                    mine = lax.broadcasted_iota(jnp.int32, (1, 128), 1) // 16 == t % 2 * 4 + f
+                    moved = pltpu.roll(row, turn, 1) if turn else row
+                    attn[t // 2 : t // 2 + 1, :] += jnp.where(mine, moved, 0.0)
+
+    lane = lax.broadcasted_iota(jnp.int32, (1, 128), 1)
+    shift = fs * 32
+
+    def mix_align():
+        raw, win = ref.s[MIX], ref.mix_win
+        last = raw.shape[1] // 128 * 128
+
+        def step(r):
+            at = pl.ds(r, 32)
+            before = jnp.zeros((32, 128), F32)
+            for t in range(win.shape[1] // 128):
+                if t * 128 < last:
+                    v = raw[at, t * 128 : (t + 1) * 128].astype(F32)
+                else:
+                    v = jnp.concatenate(
+                        [raw[at, last:].astype(F32), jnp.zeros((32, 128 - raw.shape[1] + last), F32)], axis=1
+                    )
+                v = pltpu.roll(v, shift, 1)
+                win[at, t * 128 : (t + 1) * 128] = jnp.where(lane < shift, before, v).astype(LOW)
+                before = v
+
+        row_loop(raw.shape[0], 32, step)
+
+    weights = {m: ref.w[m] for m in SHARDED}
+    block_shape = {m: (w.shape[0] // depth, w.shape[1] // 2) for m, w in weights.items()}
+
+    def block(m, zz, yy):
+        rb, cb = block_shape[m]
+        return weights[m].at[at_rows(zz * rb, rb), at_rows(yy * cb, cb, 128)]
+
+    def piece(m, src_c, src_x):
+        rb, cb = block_shape[m]
+        half = cb // 2
+        if m in (VALUE, UP):
+            return weights[m].at[at_rows(z * rb + src_c * (rb // 2), rb // 2), at_rows(y * cb + src_x * half, half, 128)]
+        return weights[m].at[at_rows(z * rb, rb), at_rows(y * cb + src_x * half, half, 128)]
+
+    swaps, own_copies = {m: [] for m in SHARDED}, {m: [] for m in SHARDED}
+
+    def swap_start(m):
+        shard = ref.s[m] if m != MIX else ref.mix_win
+        if m == MIX:
+            first, last = 1 - (fs + 2) // 3, fs // 3
+            middle = 1 - first - last
+            for peer, pc, px in ((None, c, x),) + mates:
+                pq = pc * 2 + px
+                tiles_at = (
+                    first * 2 * pq,
+                    (first + last) * (1 + 2 * pq) + middle * (1 + pq),
+                    first * 8 + last * (2 + 2 * pq) + middle * (5 + pq),
+                )
+                for i, tile in enumerate(tiles_at):
+                    src = shard.at[:, at_rows(tile * 128, 128, 128)]
+                    dst = ref.mix_in.at[x, at_rows(c * 128, 128), pl.ds(i * 128, 128)]
+                    if peer is None:
+                        own_copies[m].append(local(src, dst))
+                    else:
+                        swaps[m].append((send(src, dst, peer), pc, px, i))
+            return
+        if m in (VALUE, UP):
+            wide = shard.shape[1] // 4
+            for peer, pc, px in ((None, c, x),) + mates:
+                src = shard.at[:, at_rows((pc * 2 + px) * wide, wide, 128)]
+                if peer is None:
+                    own_copies[m].append(local(src, piece(m, c, x)))
+                else:
+                    swaps[m].append((send(src, piece(m, c, x), peer), pc, px, 0))
+            return
+        tall = shard.shape[0] // 2
+        own_copies[m].append(local(shard.at[at_rows(x * tall, tall), :], piece(m, c, x)))
+        swaps[m].append((send(shard.at[at_rows((1 - x) * tall, tall), :], piece(m, c, x), xn), c, 1 - x, 0))
+
+    z_sends, y_sends = {}, {}
+
+    def swap_finish(m):
+        for copy in own_copies[m]:
+            copy.wait()
+        for handle, pc, px, i in swaps[m]:
+            if m == MIX:
+                received(handle, ref.mix_in.at[px, at_rows(pc * 128, 128), pl.ds(i * 128, 128)])
+            else:
+                received(handle, piece(m, pc, px))
+        if m == MIX:
+            only = (q == 3).astype(F32)
+            low_y = (y == 0).astype(F32)
+            lead = jnp.broadcast_to(jnp.maximum(low_y, only), (1, 128))
+            rb, cb = block_shape[m]
+            a, b, w = ref.mix_in.at[0], ref.mix_in.at[1], weights[m]
+
+            def combine(r):
+                at = pl.ds(r, 64)
+                to = at_rows(z * rb + r, 64)
+
+                def put(i, v):
+                    w[to, at_rows(y * cb + i * 128, 128, 128)] = v.astype(LOW)
+
+                put(0, a[at, 0:128].astype(F32) * lead)
+                put(1, a[at, 128:256])
+                put(2, a[at, 256:384].astype(F32) + b[at, 0:128].astype(F32) * lead)
+                put(3, b[at, 128:256])
+                put(4, b[at, 256:384])
+
+            row_loop(rb, 64, combine)
+
+    def y_own(m):
+        y_sends[m] = [send(block(m, z, y), block(m, z, y), yn)]
+
+    def z_start(m):
+        z_sends[m] = [None] + [send(block(m, z, y), block(m, z, y), zs[d]) for d in range(1, depth)]
+
+    def y_forward(m, steps=range(1, depth)):
+        for d in steps:
+            zz = (z + depth - d) % depth
+            received(z_sends[m][d], block(m, zz, y))
+            y_sends[m].append(send(block(m, zz, y), block(m, zz, y), yn))
+
+    def y_finish(m):
+        for d in range(depth):
+            received(y_sends[m][d], block(m, (z + depth - d) % depth, 1 - y))
+
+    def group_rows(c, x):
+        return at_rows((c * 2 + x) * rows, rows)
+
+    def gather_start(buf):
+        own = buf.at[group_rows(c, x), :]
+        return [send(own, own, xn), send(own, own, sib)]
+
+    def gather_relay(buf, handles):
+        other = buf.at[group_rows(c, 1 - x), :]
+        received(handles[0], other)
+        handles.append(send(other, other, sib))
+
+    def gather_finish(buf, handles):
+        received(handles[1], buf.at[group_rows(1 - c, x), :])
+        received(handles[2], buf.at[group_rows(1 - c, 1 - x), :])
+
+    total = ref.total
+    stage = ref.stage
+    staged = [None, None, None]
+
+    def stage_out(k, extra=None):
+        if staged[k] is not None:
+            sent(staged[k])
+
+        def put(r):
+            at = pl.ds(r, 32)
+            v = total[at, :]
+            if extra is not None:
+                v = v + extra[at, :].astype(F32)
+            stage[k, at, :] = v.astype(LOW)
+
+        row_loop(rows, 32, put)
+
+    def reduce_early(partial, sibs, cross):
+        partial(1 - c, 1 - x)
+        stage_out(0)
+        h0 = staged[0] = send(stage.at[0], sibs.at[0], sib)
+        partial(1 - c, x)
+        stage_out(1)
+        h1 = staged[1] = send(stage.at[1], sibs.at[1], sib)
+        partial(c, 1 - x)
+        received(h0, sibs.at[0])
+        stage_out(2, sibs.at[0])
+        h2 = staged[2] = send(stage.at[2], cross, xn)
+        return h1, h2
+
+    def reduce_late(partial, sibs, cross, handles):
+        partial(c, x)
+        received(handles[0], sibs.at[1])
+        received(handles[1], cross)
+
+    def reduced(r, size, sibs, cross):
+        at = pl.ds(r, size)
+        return total[at, :] + sibs[1, at, :].astype(F32) + cross[at, :].astype(F32)
+
+    sibs_a, cross_a, sibs_b, cross_b = ref.sibs_a, ref.cross_a, ref.sibs_b, ref.cross_b
+
+    w_up = weights[UP]
+    y_out = {
+        DOWN: ref.yo[1],
+        UP: ref.yo[0],
+        MERGE: ref.gc.at[0 : weights[MERGE].shape[0], 0 : block_shape[MERGE][1]],
+        MIX: w_up.at[:, 0 : block_shape[MIX][1]],
+        VALUE: w_up.at[:, block_shape[MIX][1] : block_shape[MIX][1] + block_shape[VALUE][1]],
+    }
+    y_in = {m: ref.yi[m] for m in SHARDED}
+    z_in = {m: ref.zi[m] for m in SHARDED}
+    f_in = {m: ref.fi[m] for m in SHARDED}
+    gy, gz, gf = {}, {}, {}
+
+    def y_grad_send(m, product):
+        rb, cb = block_shape[m]
+        gy[m] = []
+        for d in list(range(1, depth)) + [0]:
+            zz = (z + d) % depth
+            at = at_rows(zz * rb, rb)
+            y_out[m][at, :] = product(zz, 1 - y).astype(LOW)
+            gy[m].append(send(y_out[m].at[at, :], y_in[m].at[at, :], yn))
+
+    def y_grad_add(m, product, steps=(*range(1, depth), 0)):
+        rb, cb = block_shape[m]
+        gz.setdefault(m, [])
+        for d in steps:
+            zz = (z + d) % depth
+            at = at_rows(zz * rb, rb)
+            own = product(zz, y)
+            received(gy[m][(d - 1) % depth], y_in[m].at[at, :])
+            y_in[m][at, :] = (own + y_in[m][at, :].astype(F32)).astype(LOW)
+            if d:
+                gz[m].append(send(y_in[m].at[at, :], z_in[m].at[d - 1], zs[d]))
+
+    def z_grad_add(m):
+        rb, cb = block_shape[m]
+        for d in range(1, depth):
+            received(gz[m][d - 1], z_in[m].at[d - 1])
+
+        def add(r):
+            at = at_rows(z * rb + r, 64)
+            v = y_in[m][at, :].astype(F32)
+            for d in range(1, depth):
+                v = v + z_in[m][d - 1, pl.ds(r, 64), :].astype(F32)
+            y_in[m][at, :] = v.astype(LOW)
+
+        row_loop(rb, 64, add)
+        gf[m] = []
+        if m in (MERGE, DOWN):
+            land = f_in[m].at[at_rows(x * rb, rb), :]
+
+            def part(px):
+                return y_in[m].at[at_rows(z * rb, rb), at_rows(px * (cb // 2), cb // 2, 128)]
+
+            gf[m].append((send(part(1 - x), land, xn), f_in[m].at[at_rows((1 - x) * rb, rb), :]))
+            gf[m].append((local(part(x), land), None))
+            return
+        half = rb // 2
+
+        def land_at(pc, px):
+            if m == MIX:
+                return f_in[m].at[pc * 2 + px]
+            wide = f_in[m].shape[1] // 4
+            return f_in[m].at[:, at_rows((pc * 2 + px) * wide, wide, 128)]
+
+        def part(pc, px):
+            if m == MIX:
+                return y_in[m].at[at_rows(z * rb + pc * half, half), at_rows(px * 256, 384, 128)]
+            return y_in[m].at[at_rows(z * rb + pc * half, half), at_rows(px * (cb // 2), cb // 2, 128)]
+
+        for peer, pc, px in mates:
+            gf[m].append((send(part(pc, px), land_at(c, x), peer), land_at(pc, px)))
+        gf[m].append((local(part(c, x), land_at(c, x)), None))
+
+    def grad_out(m):
+        for handle, landed in gf[m]:
+            if landed is None:
+                handle.wait()
+            else:
+                received(handle, landed)
+        if m != MIX:
+            return
+        out, src = ref.g_mix, f_in[MIX]
+        first, last = (fs == 0).astype(F32), (fs == 3).astype(F32)
+        mid = 1.0 - first - last
+        first, last, mid = (jnp.broadcast_to(v, (1, 128)) for v in (first, last, mid))
+
+        def write(r):
+            at = pl.ds(r, 16)
+
+            def get(p, t):
+                return src[p, at, t * 128 : (t + 1) * 128].astype(F32)
+
+            turned = []
+            for tile in range(9):
+                v = first * (get(tile // 2, tile % 2) if tile < 8 else src[q, at, 256:384].astype(F32))
+                if tile == 0:
+                    v = v + (mid + last) * get(3, 0)
+                else:
+                    v = v + mid * get((tile - 1) % 4, 1 + (tile - 1) // 4)
+                    v = v + last * get((tile - 1) // 2, 1 + (tile - 1) % 2)
+                turned.append(pltpu.roll(v, (128 - shift) % 128, 1))
+            for tile in range(9):
+                v = turned[tile]
+                if tile < 8:
+                    v = jnp.where(lane < 128 - shift, v, turned[tile + 1])
+                wide = min(128, out.shape[1] - tile * 128)
+                out[at, tile * 128 : tile * 128 + wide] = v[:, :wide].astype(LOW)
+
+        row_loop(out.shape[0], 16, write)
+
+    h_small = small_start()
+    swap_start(VALUE)
+    mix_align()
+    h_small = small_relay(h_small)
+    swap_start(MIX)
+    swap_start(MERGE)
+    swap_finish(VALUE)
+    y_own(VALUE)
+    z_start(VALUE)
+
+    nl, ml, n2, gc, gm = (ref.nl, ref.ml, ref.n2, ref.gc, ref.gm)
+    by_time, out_time, back_time = ref.by_time, ref.out_time, ref.back_time
+
+    def centre(v):
+        cen = v - jnp.mean(v, axis=-1, keepdims=True)
+        return cen, lax.rsqrt(jnp.mean(cen * cen, axis=-1, keepdims=True) + 1e-05)
+
+    def norm_one(r):
+        cen, rate = centre(tok[pl.ds(r, 16), :].astype(F32))
+        v = cen * rate * gains[0:1, :]
+        nl[at_rows(q * rows + r, 16), :] = v.astype(LOW)
+        for s in range(tiles):
+            by_time[pl.ds(r * tiles + s, 16, stride=tiles), :] = v[:, s * 128 : (s + 1) * 128]
+
+    small_finish(h_small)
+    row_loop(rows, 16, norm_one)
+    h_nl = gather_start(nl)
+    swap_start(UP)
+    swap_finish(MIX)
+    y_own(MIX)
+    z_start(MIX)
+    swap_finish(MERGE)
+    y_own(MERGE)
+    z_start(MERGE)
+
+    def cot_low(r):
+        at = pl.ds(r, 32)
+        gc[at_rows(q * rows + r, 32), :] = (cot[at, :].astype(F32) * live_rows(r, 32)).astype(LOW)
+
+    def load_ema():
+        return ema_in[...].reshape(4, -1, tiles, 128)
+
+    _, _, rate_all, weight_all = ema_coefficients(load_ema())
+    omega = omega_in[...]
+    marks = ref.marks
+
+    def at_time(t):
+        return at_rows(t * tiles, tiles, 8)
+
+    def ema_chunk(k, state):
+        state = state * kept(k)
+        marks[k] = state
+
+        def step(i, state):
+            t = k * CHUNK + i
+            v = by_time[at_time(t), :]
+            state = rate_all * state + v[None]
+            out_time[at_time(t), :] = jnp.sum(weight_all * state, axis=0) + omega * v
+            return state
+
+        return lax.fori_loop(0, CHUNK, step, state, unroll=4)
+
+    lax.fori_loop(0, rows // CHUNK, ema_chunk, jnp.zeros_like(rate_all))
+
+    def mixed(r):
+        for s in range(tiles):
+            at = pl.ds(r * tiles + s, 16, stride=tiles)
+            v = out_time[at, :]
+            gate = jax.nn.sigmoid(v)
+            ml[at_rows(q * rows + r, 16), s * 128 : (s + 1) * 128] = (v * gate).astype(LOW)
+            out_time[at, :] = slope_of(v, gate)
+
+    row_loop(rows, 16, mixed)
+    h_ml = gather_start(ml)
+    swap_start(DOWN)
+    swap_finish(UP)
+    z_start(UP)
+    row_loop(rows, 32, cot_low)
+    y_forward(VALUE)
+    y_own(UP)
+    gather_relay(nl, h_nl)
+    h_gc = gather_start(gc)
+    swap_finish(DOWN)
+    z_start(DOWN)
+    gather_finish(nl, h_nl)
+    y_finish(VALUE)
+
+    value_low, value_slope = ref.value_low, ref.value_slope
+    vq = value_low.shape[1]
+
+    def value_block(r):
+        total[:, :vq] = mm(nl[pl.ds(r, rows), :], weights[VALUE][...])
+
+        def act(s):
+            v = total[pl.ds(s, 32), :vq]
+            gate = jax.nn.sigmoid(v)
+            value_low[at_rows(r + s, 32), :] = (v * gate).astype(LOW)
+            value_slope[at_rows(r + s, 32), :] = slope_of(v, gate).astype(LOW)
+
+        row_loop(rows, 32, act)
+
+    row_loop(4 * rows, rows, value_block)
+    gather_relay(ml, h_ml)
+    y_forward(MIX)
+    y_own(DOWN)
+    gather_finish(ml, h_ml)
+    gather_relay(gc, h_gc)
+    y_finish(MIX)
+
+    w_mix, reset_w = weights[MIX], ref.reset_w
+    half_mix = w_mix.shape[1] // 2
+
+    def fix_reset(r):
+        at = pl.ds(r, 64)
+        reset_w[at, 0:128] = w_mix[at, 384:512]
+        reset_w[at, 128:256] = (w_mix[at, 512:640].astype(F32) + w_mix[at, half_mix : half_mix + 128].astype(F32)).astype(LOW)
+
+    row_loop(width, 64, fix_reset)
+
+    def w_update():
+        return w_mix[:, 0:256]
+
+    def w_shared():
+        return w_mix[:, 256:384]
+
+    def w_late():
+        return w_mix[:, half_mix + 128 : half_mix + 384]
+
+    def w_hidden():
+        return w_mix[:, half_mix + 384 : half_mix + 640]
+
+    scale = float(STRETCH) ** -0.5
+    stretch = STRETCH
+    shared_pre, query, key, probs = ref.shared_pre, ref.query, ref.key, ref.probs
+    probs_low = ref.probs_low
+    shared_pre[...] = mm(ml[group_rows(c, x), :], w_shared())
+    sv = shared_pre[...]
+    shared = sv * jax.nn.sigmoid(sv)
+    query[...] = (shared * attn[0:1, :] + attn[1:2, :]).astype(LOW)
+    key[...] = (shared * attn[2:3, :]).astype(LOW)
+    bias = pltpu.roll(jnp.broadcast_to(attn[3:4, :], (stretch, stretch)), 0, 1, stride=1, stride_axis=0).T
+    row_id = lax.broadcasted_iota(jnp.int32, (stretch, stretch), 0)
+    col_id = lax.broadcasted_iota(jnp.int32, (stretch, stretch), 1)
+    for n in range(rows // stretch):
+        at = pl.ds(n * stretch, stretch)
+        scores = mm_nt(query[at, :], key[at, :]) * scale + bias
+        scores = jnp.where(row_id >= col_id, scores, -1000000000.0)
+        ex = jnp.exp(scores - jnp.max(scores, axis=-1, keepdims=True))
+        pr = ex / jnp.sum(ex, axis=-1, keepdims=True)
+        probs[at, :] = pr
+        probs_low[at_rows(q * rows + n * stretch, stretch), :] = pr.astype(LOW)
+    own_probs = probs_low.at[group_rows(c, x), :]
+    h_probs = [send(own_probs, own_probs, peer) for peer, _, _ in mates]
+
+    mix_pack, update_in = ref.mix_pack, ref.update_in
+    hidden_at = pl.ds(mix_pack.shape[1] - 256, 256)
+    update_out = mix_pack.at[:, hidden_at]
+
+    def update_block(r):
+        update_out[pl.ds(r, rows), :] = mm(ml[pl.ds(r, rows), :], w_update()).astype(LOW)
+
+    row_loop(4 * rows, rows, update_block)
+    part_w = width // 4
+    own_cols = at_rows(q * part_w, part_w, 128)
+    h_update = [
+        send(update_out.at[group_rows(pc, px), :], update_in.at[:, own_cols], peer) for peer, pc, px in mates
+    ]
+    update_in[:, own_cols] = update_out[group_rows(c, x), :]
+
+    reset_gate, reset_slope = ref.reset_gate, ref.reset_slope
+
+    def reset_block(r):
+        at = pl.ds(r, rows)
+        total[:, 0:256] = mm(ml[at, :], reset_w[...])
+        total[:, 256:512] = mm(ml[at, :], w_late())
+
+        def act(s):
+            v = total[pl.ds(s, 32), :vq]
+            gate = jax.nn.sigmoid(v)
+            reset_gate[at_rows(r + s, 32), :] = (v * gate).astype(LOW)
+            reset_slope[at_rows(r + s, 32), :] = slope_of(v, gate).astype(LOW)
+
+        row_loop(rows, 32, act)
+
+    row_loop(4 * rows, rows, reset_block)
+    y_forward(MERGE)
+    for handle, (_, pc, px) in zip(h_probs, mates):
+        received(handle, probs_low.at[group_rows(pc, px), :])
+
+    gated = ref.gated
+
+    def attend(r):
+        at = pl.ds(r, stretch)
+        total[0:stretch, :vq] = mm(probs_low[at, :], value_low[at, :])
+
+        def act(s):
+            v = total[pl.ds(s, 32), :vq]
+            to = at_rows(r + s, 32)
+            gated[to, :] = (v * reset_gate[to, :].astype(F32)).astype(LOW)
+            reset_slope[to, :] = (v * reset_slope[to, :].astype(F32)).astype(LOW)
+
+        row_loop(stretch, 32, act)
+
+    row_loop(4 * rows, stretch, attend)
+    y_forward(UP, (1,))
+    y_finish(MERGE)
+
+    def merge_partial(c, x):
+        at = group_rows(c, x)
+        total[...] = mm(gated[at, :], weights[MERGE][...])
+        total[:, own_cols] += mm(ml[at, :], w_hidden())
+
+    h_red = reduce_early(merge_partial, sibs_a, cross_a)
+    for handle, (_, pc, px) in zip(h_update, mates):
+        received(handle, update_in.at[:, at_rows((pc * 2 + px) * part_w, part_w, 128)])
+    gather_finish(gc, h_gc)
+    y_forward(UP, (2, 3))
+    reduce_late(merge_partial, sibs_a, cross_a, h_red)
+
+    after, hidden_mul, update_mul = ref.after, ref.hidden_mul, ref.update_mul
+
+    def norm_two(r):
+        at = pl.ds(r, 16)
+        v = reduced(r, 16, sibs_a, cross_a)
+        gate = jax.nn.sigmoid(v)
+        hidden = v * gate
+        u = jax.nn.sigmoid(update_in[at, :].astype(F32))
+        xv = tok[at, :].astype(F32)
+        av = u * hidden + (1.0 - u) * xv
+        after[at, :] = av
+        hidden_mul[at, :] = (u * slope_of(v, gate)).astype(LOW)
+        update_mul[at, :] = ((hidden - xv) * u * (1.0 - u)).astype(LOW)
+        cen, rate = centre(av)
+        n2[at_rows(q * rows + r, 16), :] = (cen * rate * gains[1:2, :]).astype(LOW)
+
+    row_loop(rows, 16, norm_two)
+    h_n2 = gather_start(n2)
+    y_forward(DOWN, (1,))
+    gather_relay(n2, h_n2)
+    y_forward(DOWN, (2,))
+    gather_finish(n2, h_n2)
+    y_forward(DOWN, (3,))
+    y_finish(UP)
+
+    up_low, up_slope = ref.up_low, ref.up_slope
+
+    def up_block(r):
+        total[...] = mm(n2[pl.ds(r, rows), :], weights[UP][...])
+
+        def act(s):
+            v = total[pl.ds(s, 16), :]
+            gate = jax.nn.sigmoid(v)
+            up_low[at_rows(r + s, 16), :] = (v * gate).astype(LOW)
+            up_slope[at_rows(r + s, 16), :] = slope_of(v, gate).astype(LOW)
+
+        row_loop(rows, 16, act)
+
+    row_loop(4 * rows, rows, up_block)
+
+    def cols_of(m, yy):
+        cb = block_shape[m][1]
+        return at_rows(yy * cb, cb, 128)
+
+    def rows_of(m, zz):
+        rb = block_shape[m][0]
+        return at_rows(zz * rb, rb, 128)
+
+    def down_product(zz, yy):
+        return mm_tn(up_low[:, rows_of(DOWN, zz)], gc[:, cols_of(DOWN, yy)])
+
+    y_grad_send(DOWN, down_product)
+    y_finish(DOWN)
+
+    def up_back(r):
+        at = pl.ds(r, rows)
+        total[...] = mm_nt(gc[at, :], weights[DOWN][...])
+
+        def act(s):
+            to = at_rows(r + s, 16)
+            up_slope[to, :] = (total[pl.ds(s, 16), :] * up_slope[to, :].astype(F32)).astype(LOW)
+
+        row_loop(rows, 16, act)
+
+    row_loop(4 * rows, rows, up_back)
+    grad_up = up_slope
+
+    def two_partial(c, x):
+        total[...] = mm_nt(grad_up[group_rows(c, x), :], weights[UP][...])
+
+    def down_partial(c, x):
+        total[...] = mm(up_low[group_rows(c, x), :], weights[DOWN][...])
+
+    def up_product(zz, yy):
+        return mm_tn(n2[:, rows_of(UP, zz)], grad_up[:, cols_of(UP, yy)])
+
+    h_red = reduce_early(two_partial, sibs_a, cross_a)
+    y_grad_send(UP, up_product)
+    y_grad_add(DOWN, down_product)
+    reduce_late(two_partial, sibs_a, cross_a, h_red)
+
+    gain_sum, update_back = ref.gain_sum, hidden_mul
+    gain_sum[...] = jnp.zeros_like(gain_sum)
+
+    def norm_two_back(r):
+        at = pl.ds(r, 16)
+        g = reduced(r, 16, sibs_a, cross_a)
+        cen, rate = centre(after[at, :])
+        unit = cen * rate
+        gain_sum[1] += g * unit
+        g = g * gains[1:2, :]
+        back = rate * (g - jnp.mean(g, axis=-1, keepdims=True) - unit * jnp.mean(g * unit, axis=-1, keepdims=True))
+        back = back + cot[at, :].astype(F32) * live_rows(r, 16)
+        gm[at_rows(q * rows + r, 16), :] = (back * hidden_mul[at, :].astype(F32)).astype(LOW)
+        hidden_mul[at, :] = (back * update_mul[at, :].astype(F32)).astype(LOW)
+        u = jax.nn.sigmoid(update_in[at, :].astype(F32))
+        update_mul[at, :] = (back * (1.0 - u)).astype(LOW)
+
+    row_loop(rows, 16, norm_two_back)
+    h_gm = gather_start(gm)
+    for handle in h_update:
+        sent(handle)
+    update_grad = mix_pack.at[:, 0:256]
+    own_rows = group_rows(c, x)
+    h_update = [
+        send(update_back.at[:, at_rows((pc * 2 + px) * part_w, part_w, 128)], update_grad.at[own_rows, :], peer)
+        for peer, pc, px in mates
+    ]
+    update_grad[own_rows, :] = update_back[:, own_cols]
+
+    h_red = reduce_early(down_partial, sibs_b, cross_b)
+    y_grad_add(UP, up_product, (1, 2))
+    gather_relay(gm, h_gm)
+    y_grad_add(UP, up_product, (3,))
+    gather_finish(gm, h_gm)
+
+    def merge_product(zz, yy):
+        return mm_tn(gated[:, rows_of(MERGE, zz)], gm[:, cols_of(MERGE, yy)])
+
+    for handle in z_sends[UP][1:] + y_sends[UP] + h_gc:
+        sent(handle)
+    y_grad_send(MERGE, merge_product)
+
+    grad_probs, probs_in = ref.grad_probs, ref.probs_in
+
+    def gated_back(r):
+        at = pl.ds(r, rows)
+        total[:, :vq] = mm_nt(gm[at, :], weights[MERGE][...])
+
+        def act(s):
+            to = at_rows(r + s, 32)
+            g = total[pl.ds(s, 32), :vq]
+            back = (g * reset_slope[to, :].astype(F32)).astype(LOW)
+            mix_pack[to, 384:640] = back[:, 0:256]
+            mix_pack[to, 640:768] = back[:, 128:256]
+            mix_pack[to, 768:1024] = back[:, 256:512]
+            mix_pack[to, hidden_at] = gm[to, own_cols]
+            reset_gate[to, :] = (g * reset_gate[to, :].astype(F32)).astype(LOW)
+
+        row_loop(rows, 32, act)
+
+    row_loop(4 * rows, rows, gated_back)
+    grad_att = reset_gate
+
+    def probs_back(r):
+        at = pl.ds(r, stretch)
+        grad_probs[at, :] = mm_nt(grad_att[at, :], value_low[at, :])
+
+    row_loop(4 * rows, stretch, probs_back)
+    h_probs = [
+        send(grad_probs.at[group_rows(pc, px), :], probs_in.at[i], peer) for i, (peer, pc, px) in enumerate(mates)
+    ]
+    for handle, (_, pc, px) in zip(h_update, mates):
+        received(handle, update_grad.at[group_rows(pc, px), :])
+
+    shared_grad = mix_pack.at[:, 256:384]
+
+    def mixed_partial(cc, xx):
+        at = group_rows(cc, xx)
+        total[...] = (
+            mm_nt(update_grad[at, :], w_update())
+            + mm_nt(mix_pack[at, 384:640], reset_w[...])
+            + mm_nt(mix_pack[at, 768:1024], w_late())
+            + mm_nt(mix_pack[at, hidden_at], w_hidden())
+        )
+
+    y_grad_add(UP, up_product, (0,))
+    h_mixed = reduce_early(mixed_partial, sibs_a, cross_a)
+    z_grad_add(DOWN)
+
+    def value_back(r):
+        at = pl.ds(r, stretch)
+        total[0:stretch, :vq] = mm_tn(probs_low[at, :], grad_att[at, :])
+
+        def act(s):
+            to = at_rows(r + s, 32)
+            value_slope[to, :] = (total[pl.ds(s, 32), :vq] * value_slope[to, :].astype(F32)).astype(LOW)
+
+        row_loop(stretch, 32, act)
+
+    row_loop(4 * rows, stretch, value_back)
+    grad_value = value_slope
+
+    def value_product(zz, yy):
+        return mm_tn(nl[:, rows_of(VALUE, zz)], grad_value[:, cols_of(VALUE, yy)])
+
+    y_grad_send(VALUE, value_product)
+    y_grad_add(MERGE, merge_product, (1,))
+    reduce_late(down_partial, sibs_b, cross_b, h_red)
+
+    def finish(r):
+        at = pl.ds(r, 16)
+        ref.result[at, :] = (after[at, :] + reduced(r, 16, sibs_b, cross_b)).astype(LOW)
+
+    row_loop(rows, 16, finish)
+
+    for i, handle in enumerate(h_probs):
+        received(handle, probs_in.at[i])
+    anti = (row_id + col_id == stretch - 1).astype(LOW)
+    lag_sum = jnp.zeros((1, stretch), F32)
+    grads_q = jnp.zeros((1, stretch), F32)
+    grads_o = jnp.zeros((1, stretch), F32)
+    grads_k = jnp.zeros((1, stretch), F32)
+    for n in range(rows // stretch):
+        at = pl.ds(n * stretch, stretch)
+        to = at_rows(q * rows + n * stretch, stretch)
+        g = grad_probs[to, :] + probs_in[0, at, :] + probs_in[1, at, :] + probs_in[2, at, :]
+        pr = probs[at, :]
+        gs = (pr * (g - jnp.sum(pr * g, axis=-1, keepdims=True))).astype(LOW)
+        gq = mm(gs, key[at, :]) * scale
+        gk = mm_tn(gs, query[at, :]) * scale
+        lags = pltpu.roll(mm_nt(anti, gs), 1, 1, stride=1, stride_axis=0)
+        lag_sum += jnp.sum(lags, axis=0, keepdims=True)
+        sv = shared_pre[at, :]
+        gate = jax.nn.sigmoid(sv)
+        sh = sv * gate
+        grads_q += jnp.sum(gq * sh, axis=0, keepdims=True)
+        grads_o += jnp.sum(gq, axis=0, keepdims=True)
+        grads_k += jnp.sum(gk * sh, axis=0, keepdims=True)
+        gsh = gq * attn[0:1, :] + gk * attn[2:3, :]
+        shared_grad[to, :] = (gsh * slope_of(sv, gate)).astype(LOW)
+    attn_rows = (grads_q, grads_o, grads_k, lag_sum)
+    own_shared = shared_grad.at[own_rows, :]
+    h_shared = [send(own_shared, own_shared, peer) for peer, _, _ in mates]
+
+    y_grad_add(MERGE, merge_product, (2, 3, 0))
+    for handle, (_, pc, px) in zip(h_shared, mates):
+        received(handle, shared_grad.at[group_rows(pc, px), :])
+
+    def mix_product(zz, yy):
+        return mm_tn(ml[:, rows_of(MIX, zz)], mix_pack[:, cols_of(MIX, yy)])
+
+    y_grad_send(MIX, mix_product)
+
+    def mixed_own(cc, xx):
+        mixed_partial(cc, xx)
+        total[...] += mm_nt(shared_grad[own_rows, :], w_shared())
+
+    reduce_late(mixed_own, sibs_a, cross_a, h_mixed)
+
+    def to_time(r):
+        v = reduced(r, 16, sibs_a, cross_a)
+        for s in range(tiles):
+            at = pl.ds(r * tiles + s, 16, stride=tiles)
+            out_time[at, :] = out_time[at, :] * v[:, s * 128 : (s + 1) * 128]
+
+    row_loop(rows, 16, to_time)
+
+    def value_partial(cc, xx):
+        total[...] = mm_nt(grad_value[group_rows(cc, xx), :], weights[VALUE][...])
+
+    h_red = reduce_early(value_partial, sibs_b, cross_b)
+    y_grad_add(VALUE, value_product)
+    z_grad_add(UP)
+
+    held = ref.held
+    ema = load_ema()
+    damping, decay_gate, rate_all, weight_all = ema_coefficients(ema)
+    omega = omega_in[...]
+    half = rate_all.shape[0] // 2
+    chunks = rows // CHUNK
+    sums = []
+    for part in range(2):
+        js = slice(part * half, (part + 1) * half)
+        rate, weight = rate_all[js], weight_all[js]
+
+        def chunk(m, carry, js=js, rate=rate, weight=weight, part=part):
+            k = chunks - 1 - m
+            held[0] = marks[k, js]
+
+            def ahead(i, state):
+                state = rate * state + by_time[at_time(k * CHUNK + i), :][None]
+                held[i + 1] = state
+                return state
+
+            lax.fori_loop(0, CHUNK, ahead, held[0], unroll=4)
+
+            def back(n, carry):
+                s, dw, dr, dom = carry
+                i = CHUNK - 1 - n
+                t = at_time(k * CHUNK + i)
+                g = out_time[t, :]
+                s = rate * s + g[None]
+                dx = jnp.sum(weight * s, axis=0)
+                if part == 0:
+                    back_time[t, :] = dx + omega * g
+                    dom = dom + g * by_time[t, :]
+                else:
+                    back_time[t, :] = back_time[t, :] + dx
+                return s, dw + held[i + 1] * g[None], dr + held[i] * s, dom
+
+            s, dw, dr, dom = lax.fori_loop(0, CHUNK, back, carry, unroll=2)
+            return s * kept(k), dw, dr, dom
+
+        zero = jnp.zeros_like(rate)
+        sums.append(lax.fori_loop(0, chunks, chunk, (zero, zero, zero, jnp.zeros_like(omega))))
+    small = ref.small_by_time
+    rate_scale = ema.shape[1] ** (-0.5)
+    for part in range(2):
+        js = slice(part * half, (part + 1) * half)
+        dw, dr = sums[part][1], sums[part][2] * weight_all[js]
+        d_damp = dw * ema[2, js] * ema[3, js] * rate_scale - dr * decay_gate[js]
+        parts = (
+            d_damp * damping[js] * (1.0 - damping[js]),
+            -dr * damping[js] * decay_gate[js] * (1.0 - decay_gate[js]),
+            dw * damping[js] * ema[3, js] * rate_scale,
+            dw * damping[js] * ema[2, js] * rate_scale,
+        )
+        for p in range(4):
+            for j in range(half):
+                small[pl.ds((p * 2 * half + part * half + j) * tiles, tiles), :] = parts[p][j]
+
+    y_grad_add(MIX, mix_product, (1,))
+    reduce_late(value_partial, sibs_b, cross_b, h_red)
+
+    def norm_one_back(r):
+        at = pl.ds(r, 16)
+        ema_part = jnp.concatenate(
+            [back_time[pl.ds(r * tiles + s, 16, stride=tiles), :] for s in range(tiles)], axis=1
+        )
+        g = reduced(r, 16, sibs_b, cross_b) + ema_part
+        cen, rate = centre(tok[at, :].astype(F32))
+        unit = cen * rate
+        gain_sum[0] += g * unit
+        g = g * gains[0:1, :]
+        back = rate * (g - jnp.mean(g, axis=-1, keepdims=True) - unit * jnp.mean(g * unit, axis=-1, keepdims=True))
+        ref.grad_tokens[at, :] = (back + update_mul[at, :].astype(F32)).astype(LOW)
+
+    row_loop(rows, 16, norm_one_back)
+    y_grad_add(MIX, mix_product, (2,))
+
+    tile_rows = ref.tile_rows
+    states = 4 * ema.shape[1]
+    gain_one = jnp.sum(gain_sum[0], axis=0, keepdims=True)
+    gain_two = jnp.sum(gain_sum[1], axis=0, keepdims=True)
+    for t in range(tiles):
+        at = (t % 2) * depth + t // 2
+        tile_rows[at, 0:states, :] = small[pl.ds(t, states, stride=tiles), :]
+        tail = jnp.concatenate(
+            [
+                gain_one[:, t * 128 : (t + 1) * 128],
+                gain_two[:, t * 128 : (t + 1) * 128],
+                sums[0][3][t : t + 1],
+                attn_rows[t // 2],
+                jnp.zeros((4, 128), F32),
+            ],
+            axis=0,
+        )
+        tile_rows[at, states : states + 8, :] = tail
+    sib_in, z_small, x_small, y_small = ref.sib_in, ref.z_small, ref.x_small, ref.y_small
+    h_sib = send(tile_rows.at[pl.ds((1 - c) * depth, depth)], sib_in, sib)
+    y_grad_add(MIX, mix_product, (3, 0))
+    z_grad_add(MERGE)
+    received(h_sib, sib_in)
+    sib_in[...] += tile_rows[pl.ds(c * depth, depth)]
+    h_zs = [send(sib_in.at[(z + d) % depth], z_small.at[d - 1], zs[d]) for d in range(1, depth)]
+    z_grad_add(VALUE)
+    for d, handle in enumerate(h_zs):
+        received(handle, z_small.at[d])
+    x_small[0] = sib_in[z] + z_small[0] + z_small[1] + z_small[2]
+    h_x = send(x_small.at[0], x_small.at[1], xn)
+    z_grad_add(MIX)
+    received(h_x, x_small.at[1])
+    y_small[0] = x_small[0] + x_small[1]
+    h_y = send(y_small.at[0], y_small.at[1], yn)
+    for m in (DOWN, UP, MERGE, VALUE, MIX):
+        grad_out(m)
+    received(h_y, y_small.at[1])
+    totals = y_small[0] + y_small[1]
+    states = 4 * ema.shape[1]
+    ref.small_out[...] = pltpu.roll(totals, (128 - shift) % 128, 1)
+    ref.attn_out[...] = pltpu.roll(totals[states : states + 8], (128 - c * 64 - fs * 16) % 128, 1)
+    for handle in pending:
+        sent(handle)
+
+
+def pack_small(norm_gains, ema_params, attn_params):
+    states, mine = ema_params.shape[2], ema_params.shape[1]
+    last = jnp.pad(attn_params, (0, mine - attn_params.shape[0]))
+    rows = [
+        jnp.transpose(ema_params, (2, 0, 1)).reshape(states, 4 * mine),
+        jnp.concatenate([norm_gains.reshape(-1), last])[None],
+        jnp.zeros((32 - states - 1, 4 * mine), LOW),
+    ]
+    return jnp.concatenate(rows, axis=0)
+
+
+def finish_kernel(result, grad_tokens, value, mix, merge, up, down, small, attn, *outs):
+    for src, out in zip((result, grad_tokens, value, mix, merge, up, down), outs):
+
+        def widen(r, src=src, out=out):
+            out[pl.ds(r, 32), :] = src[pl.ds(r, 32), :].astype(out.dtype)
+
+        row_loop(out.shape[0], 32, widen)
+    gains, ema, per = outs[7:]
+    mine, states = ema.shape[1:]
+    gains[...] = small[4 * states : 4 * states + 3, :mine]
+    turned = small[0 : 4 * states, :].T
+    for p in range(4):
+        ema[p] = turned[:mine, p * states : (p + 1) * states]
+    per[...] = attn[3:4, : per.shape[1]]
+
+
+def layer_on_device(depth, tokens, cotangent, lengths, value_proj, mix_proj, merge_proj, up_proj, down_proj, norm_gains, ema_params, attn_params):
+    rows, width = tokens.shape
+    fs = lax.axis_index(FS)
+    window = -(-mix_proj.shape[1] // 128) * 128
+    group = 4 * rows
+    vq = value_proj.shape[1]
+    fq = up_proj.shape[1]
+    quarters = ((width, vq), (width, 10 * STRIP), (vq, width), (width, fq), (fq, width))
+    tiles = width // 128
+    states = ema_params.shape[2]
+    small_rows = 4 * states + 8
+    shape = jax.ShapeDtypeStruct
+    shards = (value_proj, mix_proj, merge_proj, up_proj, down_proj)
+    inputs = dict(
+        tok=tokens,
+        cot=cotangent,
+        lens=lengths,
+        packed=pack_small(norm_gains, ema_params, attn_params),
+        s=shards,
+    )
+    landings = [w.shape for w in shards]
+    landings[MIX] = (4, mix_proj.shape[0], 3 * STRIP)
+    outputs = dict(
+        result=shape((rows, width), LOW),
+        grad_tokens=shape((rows, width), LOW),
+        fi=tuple(shape(d, LOW) for d in landings),
+        g_mix=shape(mix_proj.shape, LOW),
+        small_out=shape((small_rows, 128), F32),
+        attn_out=shape((8, 128), F32),
+    )
+    copies = pltpu.SemaphoreType.DMA((200,))
+
+    def low(*dims):
+        return pltpu.VMEM(dims, LOW)
+
+    def full(*dims):
+        return pltpu.VMEM(dims, F32)
+
+    scratch = dict(
+        send_sems=copies,
+        recv_sems=copies,
+        local_sems=pltpu.SemaphoreType.DMA((24,)),
+        w=tuple(low(*d) for d in quarters),
+        yo=tuple(low(quarters[m][0], quarters[m][1] // 2) for m in (UP, DOWN)),
+        yi=tuple(low(r, k // 2) for r, k in quarters),
+        zi=tuple(low(depth - 1, r // depth, k // 2) for r, k in quarters),
+        mix_win=low(mix_proj.shape[0], window),
+        small_all=low(8 * depth, 32, 128),
+        ema_in=full(4 * states * tiles, 128),
+        omega_in=full(tiles, 128),
+        gains=full(8, width),
+        attn=full(8, 128),
+        nl=low(group, width),
+        ml=low(group, width),
+        n2=low(group, width),
+        gc=low(group, width),
+        gm=low(group, width),
+        mix_in=low(2, 2 * mix_proj.shape[0], 3 * STRIP),
+        reset_w=low(width, 256),
+        value_low=low(group, vq),
+        value_slope=low(group, vq),
+        reset_gate=low(group, vq),
+        reset_slope=low(group, vq),
+        gated=low(group, vq),
+        up_low=low(group, fq),
+        up_slope=low(group, fq),
+        update_in=low(rows, width),
+        probs_low=low(group, STRETCH),
+        probs=full(rows, STRETCH),
+        shared_pre=full(rows, Z),
+        query=low(rows, Z),
+        key=low(rows, Z),
+        grad_probs=full(group, STRETCH),
+        probs_in=full(3, rows, STRETCH),
+        mix_pack=low(group, 10 * STRIP),
+        by_time=full(rows * tiles, 128),
+        out_time=full(rows * tiles, 128),
+        back_time=full(rows * tiles, 128),
+        marks=full(rows // CHUNK, states, tiles, 128),
+        held=full(CHUNK + 1, states // 2, tiles, 128),
+        total=full(rows, width),
+        stage=low(3, rows, width),
+        sibs_a=low(2, rows, width),
+        sibs_b=low(2, rows, width),
+        cross_a=low(rows, width),
+        cross_b=low(rows, width),
+        after=full(rows, width),
+        hidden_mul=low(rows, width),
+        update_mul=low(rows, width),
+        gain_sum=full(2, 16, width),
+        small_by_time=full(4 * states * tiles, 128),
+        tile_rows=full(tiles, small_rows, 128),
+        sib_in=full(depth, small_rows, 128),
+        z_small=full(depth - 1, small_rows, 128),
+        x_small=full(2, small_rows, 128),
+        y_small=full(2, small_rows, 128),
+    )
+    in_vmem = pl.BlockSpec(memory_space=pltpu.VMEM)
+    specs = jax.tree.map(lambda _: in_vmem, inputs)
+    anywhere = pl.BlockSpec(memory_space=pl.ANY)
+    specs.update(
+        lens=pl.BlockSpec(memory_space=pltpu.SMEM), s=tuple(in_vmem if m == MIX else anywhere for m in SHARDED)
+    )
+    in_leaves, in_tree = jax.tree.flatten(inputs)
+    out_leaves, out_tree = jax.tree.flatten(outputs)
+    scratch_leaves, scratch_tree = jax.tree.flatten(scratch, is_leaf=lambda v: not isinstance(v, (dict, tuple)))
+    outs = pl.pallas_call(
+        functools.partial(layer_kernel, (in_tree, out_tree, scratch_tree), depth),
+        out_shape=tuple(out_leaves),
+        in_specs=jax.tree.leaves(specs),
+        out_specs=tuple(in_vmem for _ in out_leaves),
+        scratch_shapes=scratch_leaves,
+        compiler_params=pltpu.CompilerParams(collective_id=0, has_side_effects=True, vmem_limit_bytes=VMEM_BYTES),
+        name="layer",
+    )(*in_leaves)
+    by = types.SimpleNamespace(**jax.tree.unflatten(out_tree, outs))
+    grads = list(by.fi)
+    grads[MIX] = by.g_mix
+    wide = [shape(g.shape, F32) for g in (*grads, norm_gains, ema_params)]
+    *finals, attn_grad = pl.pallas_call(
+        finish_kernel,
+        out_shape=(shape((rows, width), LOW), shape((rows, width), LOW), *wide, shape((1, attn_params.shape[0]), F32)),
+        in_specs=[in_vmem] * 9,
+        out_specs=(in_vmem,) * 10,
+        compiler_params=pltpu.CompilerParams(vmem_limit_bytes=32 << 20),
+        name="finish",
+    )(by.result, by.grad_tokens, *grads, by.small_out, by.attn_out)
+    return (*finals, attn_grad[0])
+
+
+VMEM_BYTES = 64 << 20
+
+
 def solution(mesh):
     in_specs = (
-        P(("dp", "fsdp"), None),
-        P(("dp", "fsdp"), None),
-        P(("dp", "fsdp"), None),
-        P("dp", "fsdp"),
-        P("dp", "fsdp"),
-        P("dp", "fsdp"),
-        P("dp", "fsdp"),
-        P("dp", "fsdp"),
-        P(None, ("dp", "fsdp")),
-        P(None, ("dp", "fsdp"), None),
-        P(("dp", "fsdp")),
+        P((DP, FS), None),
+        P((DP, FS), None),
+        P((DP, FS), None),
+        P(DP, FS),
+        P(DP, FS),
+        P(DP, FS),
+        P(DP, FS),
+        P(DP, FS),
+        P(None, (DP, FS)),
+        P(None, (DP, FS), None),
+        P((DP, FS)),
     )
     out_specs = (
-        P(("dp", "fsdp"), None),
-        P(("dp", "fsdp"), None),
-        P("dp", "fsdp"),
-        P("dp", "fsdp"),
-        P("dp", "fsdp"),
-        P("dp", "fsdp"),
-        P("dp", "fsdp"),
-        P(None, ("dp", "fsdp")),
-        P(None, ("dp", "fsdp"), None),
-        P(("dp", "fsdp")),
-    )
-    return jax.shard_map(
-        on_device, mesh=mesh, in_specs=in_specs, out_specs=out_specs, check_vma=False
-    )
+        P((DP, FS), None),
+        P((DP, FS), None),
+        P(DP, FS),
+        P(DP, FS),
+        P(DP, FS),
+        P(DP, FS),
+        P(DP, FS),
+        P(None, (DP, FS)),
+        P(None, (DP, FS), None),
+        P((DP, FS)),
+    )
+    fits = mesh.shape[DP] // 2 * 4 * STRIP == V and mesh.shape[FS] * 4 * STRIP == V
+    body = functools.partial(layer_on_device, mesh.shape[DP] // 2) if fits else on_device
+    return jax.shard_map(body, mesh=mesh, in_specs=in_specs, out_specs=out_specs, check_vma=False)

time: 1370 us -> 303 us (0.22)
  waiting for transfers between devices: 972 us -> 0 us
  Pallas kernels: 12.8 us -> 287 us
  blocking collectives: 218 us -> 0 us
  matrix products: 99.9 us -> 0 us
  other arithmetic: 24.1 us -> 0.75 us
  between operations: 15.5 us -> 0.68 us
    reduce_scatter x9 -> x0, waiting for transfers between devices: 419 us -> none  [the longest x1 92.2 us: reduce_gradients(): lax.psum_scatter(mix_grad.astype(jnp.bfloat16), 'dp', scatter_dimension=0...]
    all_gather x10 -> x0, waiting for transfers between devices: 308 us -> none  [the longest x1 82.6 us: gather_forward(): lax.all_gather(first[3], 'fsdp', axis=1, tiled=True)]
    pallas_call x2, Pallas kernels: 12.8 us -> 287 us  [the longest x1 285 us: layer_on_device(): pl.pallas_call(functools.partial(layer_kernel, (in_tree, out_tree, scratc...]
    unnamed x25 -> x0, waiting for transfers between devices: 245 us -> none
    all_gather x2 -> x0, blocking collectives: 143 us -> none  [the longest x1 75.9 us: on_device(): lax.all_gather(ema_params, ('dp', 'fsdp'), axis=1, tiled=True)]
    dot_general x23 -> x0, matrix products: 99.9 us -> none  [the longest x1 8.28 us: on_device(): jnp.einsum('tf,td->fd', up_low, grad_down_low, preferred_element_type=jnp...]
    unnamed x2 -> x0, blocking collectives: 75.5 us -> none
  transfers between devices with their start and end apart: 22 -> 0, of which waited for: 19 -> 0; matrix products, arithmetic and copies ran while one was open for 8% -> 0% of each run, Pallas kernels for 1% -> 0%
where the time goes in v2:
time: 303 us; the launch traced here: 302 us
  Pallas kernels  287 us (95%)
  local copies, waits for them, and re-layouts  14 us (5%)
    pallas_call x1, Pallas kernels, layer_on_device(): pl.pallas_call(functools.partial(layer_kernel, (in_tree, out_tree, scratc...  285 us
    unnamed x25, local copies, waits for them, and re-layouts  13 us

profile of v2, /device:TPU:0, one launch (start us, length us, event | category | flops | bytes accessed | tf_op | source)
XLA Modules:
  0.0 302.0 jit_solution(7386284048810794446)
XLA Ops:
  0.6 0.0 copy-start.9
  0.7 0.7 copy-done.9
  1.3 0.1 reshape.27
  1.4 0.6 copy-done.10
  2.0 0.1 fusion.1
  2.1 0.1 pad.7.clone
  2.1 0.7 copy.21
  2.9 0.1 reshape.26
  3.0 0.7 maximum_maximum_fusion.refs_2_
  3.6 1.8 copy.22.refs_4_
  5.5 284.7 %layer.1 = (f32[8,128]{1,0:T(8,128)}, bf16[128,512]{1,0:T(8,128)(2,1)}, bf16[4,128,384]{2,1,0:T(8,128)(2,1)}, bf16[256,256]{1,0:T(8,128)(2,1)}, bf16[128,1024]{1...) custom-call(bf16[256,1024]{1,0:T(8,128)(2,1)} %refs_0_.1, ...), custom_call_target="tpu_custom_call" | custom-call | tf_op jit(solution)/shard_map/layer/pallas_call | solution.py:1593
  290.2 0.0 copy-start.8
  290.2 0.7 copy-done.8
  290.9 1.0 copy-done
  291.9 1.0 copy-done.1
  293.0 1.0 copy-done.2
  293.9 0.9 copy-done.3
  294.9 0.9 copy-done.4
  295.8 0.9 copy-done.5
  296.7 0.9 copy-done.6
  297.6 0.8 copy-done.7
  298.4 1.9 finish.1
  300.3 0.7 copy.24
  301.0 1.0 copy.23
  (10 shorter events, 0.0 us)
Async XLA Ops:
  0.6 0.7 copy-start.9
  1.3 0.7 copy-start.10
  290.2 0.7 copy-start.8
  290.9 1.0 copy-start
  291.9 1.0 copy-start.1
  293.0 1.0 copy-start.2
  293.9 0.9 copy-start.3
  294.9 0.9 copy-start.4
  295.8 0.9 copy-start.5
  296.7 0.9 copy-start.6
  297.6 0.8 copy-start.7

commit v3 on v2

--- a/solution.py
+++ b/solution.py
@@ -442,12 +442,12 @@
     return pl.ds(pl.multiple_of(start, unit), size)
 
 
-def row_loop(count, size, body):
+def row_loop(count, size, body, first=0, unroll=1):
     def step(i, carry):
-        body(pl.multiple_of(i * size, size))
+        body(pl.multiple_of(first + i * size, size))
         return carry
 
-    lax.fori_loop(0, count // size, step, 0)
+    lax.fori_loop(0, count // size, step, 0, unroll=unroll)
 
 
 def slope_of(value, gate):
@@ -470,6 +470,11 @@
         return (z * 2 + c, y * 2 + x)
 
     sib, xn, xc, yn = place(z, 1 - c, y, x), place(z, c, y, 1 - x), place(z, 1 - c, y, 1 - x), place(z, c, 1 - y, x)
+    half_z = z // 2
+    partner, far_mid, far_end = z + 1 - 2 * (z % 2), 2 - half_z, 3 * (1 - half_z)
+    middle = (z % 2 + half_z) % 2 == 1
+    outer = (z % 2 + half_z) % 2 == 0
+    line = (far_end, far_mid, partner, z)
     zs = [None] + [place((z + d) % depth, c, y, x) for d in range(1, depth)]
     mates = ((sib, 1 - c, x), (xn, c, 1 - x), (xc, 1 - c, 1 - x))
     plane = [(pc, py, px) for pc in range(2) for py in range(2) for px in range(2)][1:]
@@ -484,25 +489,34 @@
     send_sems, recv_sems, local_sems = ref.send_sems, ref.recv_sems, ref.local_sems
     used, used_local, pending = [0], [0], []
 
-    def send(src, dst, peer, slot=None):
-        k = used[0]
+    def new_id():
         used[0] += 1
+        return used[0] - 1
+
+    def send(src, dst, peer, arrives=None, when=None):
+        k = new_id()
         copy = pltpu.make_async_remote_copy(
-            src_ref=src, dst_ref=dst, send_sem=send_sems.at[k], recv_sem=recv_sems.at[k],
+            src_ref=src, dst_ref=dst, send_sem=send_sems.at[k], recv_sem=recv_sems.at[k if arrives is None else arrives],
             device_id=peer, device_id_type=MESH,
         )
-        copy.start()
-        handle = [k, copy, False]
+        if when is None:
+            copy.start()
+        else:
+            pl.when(when)(copy.start)
+        handle = [k, copy, False, when]
         pending.append(handle)
         return handle
 
     def sent(handle):
         if not handle[2]:
-            handle[1].wait_send()
+            if handle[3] is None:
+                handle[1].wait_send()
+            else:
+                pl.when(handle[3])(handle[1].wait_send)
             handle[2] = True
 
     def received(handle, landed):
-        k = handle[0]
+        k = handle if isinstance(handle, int) else handle[0]
         pltpu.make_async_remote_copy(
             src_ref=landed, dst_ref=landed, send_sem=send_sems.at[k], recv_sem=recv_sems.at[k],
             device_id=sib, device_id_type=MESH,
@@ -611,14 +625,31 @@
             return weights[m].at[at_rows(z * rb + src_c * (rb // 2), rb // 2), at_rows(y * cb + src_x * half, half, 128)]
         return weights[m].at[at_rows(z * rb, rb), at_rows(y * cb + src_x * half, half, 128)]
 
-    swaps, own_copies = {m: [] for m in SHARDED}, {m: [] for m in SHARDED}
+    def move(src, dst):
+        rows_at_once = 32
+
+        def step(r):
+            dst[pl.ds(r, rows_at_once), :] = src[pl.ds(r, rows_at_once), :]
+
+        row_loop(src.shape[0], rows_at_once, step)
+
+    spare, near, loads, top = ref.up_low, {MIX: ref.mix_win}, {}, 0
+    for m in (VALUE, MERGE, UP, DOWN):
+        tall, wide = ref.s[m].shape
+        near[m] = spare.at[top : top + tall, 0:wide]
+        loads[m] = local(ref.s[m], near[m])
+        top += tall
+    for m in loads:
+        loads[m].wait()
+
+    swaps = {m: [] for m in SHARDED}
 
     def swap_start(m):
-        shard = ref.s[m] if m != MIX else ref.mix_win
+        shard = near[m]
         if m == MIX:
             first, last = 1 - (fs + 2) // 3, fs // 3
             middle = 1 - first - last
-            for peer, pc, px in ((None, c, x),) + mates:
+            for peer, pc, px in mates + ((None, c, x),):
                 pq = pc * 2 + px
                 tiles_at = (
                     first * 2 * pq,
@@ -629,28 +660,26 @@
                     src = shard.at[:, at_rows(tile * 128, 128, 128)]
                     dst = ref.mix_in.at[x, at_rows(c * 128, 128), pl.ds(i * 128, 128)]
                     if peer is None:
-                        own_copies[m].append(local(src, dst))
+                        move(src, dst)
                     else:
                         swaps[m].append((send(src, dst, peer), pc, px, i))
             return
         if m in (VALUE, UP):
             wide = shard.shape[1] // 4
-            for peer, pc, px in ((None, c, x),) + mates:
+            for peer, pc, px in mates + ((None, c, x),):
                 src = shard.at[:, at_rows((pc * 2 + px) * wide, wide, 128)]
                 if peer is None:
-                    own_copies[m].append(local(src, piece(m, c, x)))
+                    move(src, piece(m, c, x))
                 else:
                     swaps[m].append((send(src, piece(m, c, x), peer), pc, px, 0))
             return
         tall = shard.shape[0] // 2
-        own_copies[m].append(local(shard.at[at_rows(x * tall, tall), :], piece(m, c, x)))
         swaps[m].append((send(shard.at[at_rows((1 - x) * tall, tall), :], piece(m, c, x), xn), c, 1 - x, 0))
-
-    z_sends, y_sends = {}, {}
+        move(shard.at[at_rows(x * tall, tall), :], piece(m, c, x))
+
+    z_ids, z_sends, y_sends = {}, {}, {}
 
     def swap_finish(m):
-        for copy in own_copies[m]:
-            copy.wait()
         for handle, pc, px, i in swaps[m]:
             if m == MIX:
                 received(handle, ref.mix_in.at[px, at_rows(pc * 128, 128), pl.ds(i * 128, 128)])
@@ -679,77 +708,106 @@
             row_loop(rb, 64, combine)
 
     def y_own(m):
-        y_sends[m] = [send(block(m, z, y), block(m, z, y), yn)]
+        y_sends[m] = [(3, send(block(m, z, y), block(m, z, y), yn))]
 
     def z_start(m):
-        z_sends[m] = [None] + [send(block(m, z, y), block(m, z, y), zs[d]) for d in range(1, depth)]
-
-    def y_forward(m, steps=range(1, depth)):
-        for d in steps:
-            zz = (z + depth - d) % depth
-            received(z_sends[m][d], block(m, zz, y))
-            y_sends[m].append(send(block(m, zz, y), block(m, zz, y), yn))
+        own = block(m, z, y)
+        ids = [new_id() for _ in range(3)]
+        z_ids[m] = ids
+        z_sends[m] = [
+            send(own, own, place(partner, c, y, x), ids[2]),
+            send(own, own, place(far_mid, c, y, x), ids[1], middle),
+            send(own, own, place(far_mid, c, y, x), ids[0], outer),
+        ]
+
+    def z_pass(m, steps=(1, 0)):
+        for i in steps:
+            there = block(m, line[i], y)
+            pl.when(middle)(functools.partial(received, z_ids[m][i], there))
+            z_sends[m].append(send(there, there, place(partner, c, y, x), z_ids[m][i], middle))
+
+    def y_forward(m, steps=(2, 1, 0)):
+        for i in steps:
+            there = block(m, line[i], y)
+            if i == 2:
+                received(z_ids[m][i], there)
+            else:
+                pl.when(outer)(functools.partial(received, z_ids[m][i], there))
+            y_sends[m].append((i, send(there, there, yn)))
 
     def y_finish(m):
-        for d in range(depth):
-            received(y_sends[m][d], block(m, (z + depth - d) % depth, 1 - y))
+        for i, handle in y_sends[m]:
+            received(handle, block(m, line[i], 1 - y))
 
     def group_rows(c, x):
         return at_rows((c * 2 + x) * rows, rows)
 
-    def gather_start(buf):
-        own = buf.at[group_rows(c, x), :]
-        return [send(own, own, xn), send(own, own, sib)]
+    def part_rows(c, x, first, count):
+        return at_rows((c * 2 + x) * rows + first, count)
+
+    def gather_start(buf, first=0, count=None):
+        count = rows if count is None else count
+        own = buf.at[part_rows(c, x, first, count), :]
+        return [(first, count), send(own, own, xn), send(own, own, sib)]
 
     def gather_relay(buf, handles):
-        other = buf.at[group_rows(c, 1 - x), :]
-        received(handles[0], other)
+        other = buf.at[part_rows(c, 1 - x, *handles[0]), :]
+        received(handles[1], other)
         handles.append(send(other, other, sib))
 
     def gather_finish(buf, handles):
-        received(handles[1], buf.at[group_rows(1 - c, x), :])
-        received(handles[2], buf.at[group_rows(1 - c, 1 - x), :])
+        received(handles[2], buf.at[part_rows(1 - c, x, *handles[0]), :])
+        received(handles[3], buf.at[part_rows(1 - c, 1 - x, *handles[0]), :])
 
     total = ref.total
-    stage = ref.stage
-    staged = [None, None, None]
-
-    def stage_out(k, extra=None):
-        if staged[k] is not None:
-            sent(staged[k])
-
+    stage = [ref.stage.at[0], ref.stage.at[1], ref.stage.at[2], ref.hidden_mul]
+    staged = [[], [], [], []]
+
+    def stage_out(k, first, count, extra=None):
         def put(r):
             at = pl.ds(r, 32)
             v = total[at, :]
             if extra is not None:
                 v = v + extra[at, :].astype(F32)
-            stage[k, at, :] = v.astype(LOW)
-
-        row_loop(rows, 32, put)
-
-    def reduce_early(partial, sibs, cross):
-        partial(1 - c, 1 - x)
-        stage_out(0)
-        h0 = staged[0] = send(stage.at[0], sibs.at[0], sib)
-        partial(1 - c, x)
-        stage_out(1)
-        h1 = staged[1] = send(stage.at[1], sibs.at[1], sib)
+            stage[k][at, :] = v.astype(LOW)
+
+        row_loop(count, 32, put, first)
+
+    def stage_free(k):
+        for handle in staged[k]:
+            sent(handle)
+        staged[k] = []
+
+    def reduce_early(partial, sibs, cross, slot=2):
+        halves = (pl.ds(0, rows // 2), pl.ds(rows // 2, rows // 2))
+        for k, px in ((0, 1 - x), (1, x)):
+            partial(1 - c, px)
+            stage_free(k)
+            stage_out(k, 0, rows)
+            staged[k] = [send(stage[k], sibs[k], sib)]
+        first, second = staged[0][0], staged[1][0]
         partial(c, 1 - x)
-        received(h0, sibs.at[0])
-        stage_out(2, sibs.at[0])
-        h2 = staged[2] = send(stage.at[2], cross, xn)
-        return h1, h2
-
-    def reduce_late(partial, sibs, cross, handles):
+        received(first, sibs[0])
+        stage_free(slot)
+        for i, half in enumerate(halves):
+            stage_out(slot, i * (rows // 2), rows // 2, sibs[0])
+            staged[slot].append(send(stage[slot].at[half, :], cross.at[half, :], xn))
+        return second, list(zip(staged[slot], (cross.at[half, :] for half in halves)))
+
+    def reduce_late(partial, sibs, cross, handles, consume):
         partial(c, x)
-        received(handles[0], sibs.at[1])
-        received(handles[1], cross)
+        received(handles[0], sibs[1])
+        for i, (handle, half) in enumerate(handles[1]):
+            received(handle, half)
+            consume(i * (rows // 2), rows // 2)
 
     def reduced(r, size, sibs, cross):
         at = pl.ds(r, size)
-        return total[at, :] + sibs[1, at, :].astype(F32) + cross[at, :].astype(F32)
-
-    sibs_a, cross_a, sibs_b, cross_b = ref.sibs_a, ref.cross_a, ref.sibs_b, ref.cross_b
+        return total[at, :] + sibs[1][at, :].astype(F32) + cross[at, :].astype(F32)
+
+    sibs_a, sibs_b = ((r.at[0], r.at[1]) for r in (ref.sibs_a, ref.sibs_b))
+    cross_a, cross_b = ref.cross_a, ref.cross_b
+    sibs_c, cross_c = (ref.gc.at[2 * rows : 3 * rows, :], ref.gc.at[3 * rows : 4 * rows, :]), ref.update_in
 
     w_up = weights[UP]
     y_out = {
@@ -764,37 +822,49 @@
     f_in = {m: ref.fi[m] for m in SHARDED}
     gy, gz, gf = {}, {}, {}
 
-    def y_grad_send(m, product):
+    def y_grad_send(m, product, steps=(0, 1, 2, 3)):
         rb, cb = block_shape[m]
-        gy[m] = []
-        for d in list(range(1, depth)) + [0]:
-            zz = (z + d) % depth
-            at = at_rows(zz * rb, rb)
-            y_out[m][at, :] = product(zz, 1 - y).astype(LOW)
-            gy[m].append(send(y_out[m].at[at, :], y_in[m].at[at, :], yn))
-
-    def y_grad_add(m, product, steps=(*range(1, depth), 0)):
+        if m not in gy:
+            gy[m], gz[m] = {}, [new_id() for _ in range(4)]
+        for i in steps:
+            at = at_rows(line[i] * rb, rb)
+            y_out[m][at, :] = product(line[i], 1 - y).astype(LOW)
+            gy[m][i] = send(y_out[m].at[at, :], y_in[m].at[at, :], yn)
+
+    def y_grad_add(m, product, steps=(0, 1, 2, 3)):
         rb, cb = block_shape[m]
-        gz.setdefault(m, [])
-        for d in steps:
-            zz = (z + d) % depth
-            at = at_rows(zz * rb, rb)
-            own = product(zz, y)
-            received(gy[m][(d - 1) % depth], y_in[m].at[at, :])
+        for i in steps:
+            at = at_rows(line[i] * rb, rb)
+            own = product(line[i], y)
+            received(gy[m][i], y_in[m].at[at, :])
             y_in[m][at, :] = (own + y_in[m][at, :].astype(F32)).astype(LOW)
-            if d:
-                gz[m].append(send(y_in[m].at[at, :], z_in[m].at[d - 1], zs[d]))
+            if i < 3:
+                send(
+                    y_in[m].at[at, :], z_in[m].at[i], place(partner, c, y, x), gz[m][i], outer if i < 2 else None
+                )
+
+    def z_relay(m, steps=(0, 1)):
+        rb, cb = block_shape[m]
+        for i in steps:
+            at = at_rows(line[i] * rb, rb)
+
+            @pl.when(middle)
+            def _(i=i, at=at):
+                received(gz[m][i], z_in[m].at[i])
+                y_in[m][at, :] = (y_in[m][at, :].astype(F32) + z_in[m][i].astype(F32)).astype(LOW)
+
+            send(y_in[m].at[at, :], z_in[m].at[3], place(line[i], c, y, x), gz[m][3], middle)
 
     def z_grad_add(m):
         rb, cb = block_shape[m]
-        for d in range(1, depth):
-            received(gz[m][d - 1], z_in[m].at[d - 1])
+        for i in (2, 3):
+            received(gz[m][i], z_in[m].at[i])
 
         def add(r):
             at = at_rows(z * rb + r, 64)
             v = y_in[m][at, :].astype(F32)
-            for d in range(1, depth):
-                v = v + z_in[m][d - 1, pl.ds(r, 64), :].astype(F32)
+            for i in (2, 3):
+                v = v + z_in[m][i, pl.ds(r, 64), :].astype(F32)
             y_in[m][at, :] = v.astype(LOW)
 
         row_loop(rb, 64, add)
@@ -806,7 +876,7 @@
                 return y_in[m].at[at_rows(z * rb, rb), at_rows(px * (cb // 2), cb // 2, 128)]
 
             gf[m].append((send(part(1 - x), land, xn), f_in[m].at[at_rows((1 - x) * rb, rb), :]))
-            gf[m].append((local(part(x), land), None))
+            move(part(x), land)
             return
         half = rb // 2
 
@@ -823,14 +893,11 @@
 
         for peer, pc, px in mates:
             gf[m].append((send(part(pc, px), land_at(c, x), peer), land_at(pc, px)))
-        gf[m].append((local(part(c, x), land_at(c, x)), None))
+        move(part(c, x), land_at(c, x))
 
     def grad_out(m):
         for handle, landed in gf[m]:
-            if landed is None:
-                handle.wait()
-            else:
-                received(handle, landed)
+            received(handle, landed)
         if m != MIX:
             return
         out, src = ref.g_mix, f_in[MIX]
@@ -866,8 +933,8 @@
     swap_start(VALUE)
     mix_align()
     h_small = small_relay(h_small)
+    swap_start(MERGE)
     swap_start(MIX)
-    swap_start(MERGE)
     swap_finish(VALUE)
     y_own(VALUE)
     z_start(VALUE)
@@ -890,11 +957,12 @@
     row_loop(rows, 16, norm_one)
     h_nl = gather_start(nl)
     swap_start(UP)
+    swap_finish(MERGE)
+    y_own(MERGE)
     swap_finish(MIX)
     y_own(MIX)
+    z_pass(VALUE)
     z_start(MIX)
-    swap_finish(MERGE)
-    y_own(MERGE)
     z_start(MERGE)
 
     def cot_low(r):
@@ -937,16 +1005,19 @@
     row_loop(rows, 16, mixed)
     h_ml = gather_start(ml)
     swap_start(DOWN)
+    row_loop(rows, 32, cot_low)
+    y_forward(VALUE)
+    z_pass(MIX, (1,))
+    gather_relay(nl, h_nl)
+    h_gc = gather_start(gc)
+    y_forward(MIX, [2])
+    z_pass(MIX, (0,))
+    gather_finish(nl, h_nl)
     swap_finish(UP)
     z_start(UP)
-    row_loop(rows, 32, cot_low)
-    y_forward(VALUE)
+    y_forward(MIX, [1])
     y_own(UP)
-    gather_relay(nl, h_nl)
-    h_gc = gather_start(gc)
-    swap_finish(DOWN)
-    z_start(DOWN)
-    gather_finish(nl, h_nl)
+    z_pass(MERGE)
     y_finish(VALUE)
 
     value_low, value_slope = ref.value_low, ref.value_slope
@@ -964,11 +1035,16 @@
         row_loop(rows, 32, act)
 
     row_loop(4 * rows, rows, value_block)
+    y_forward(MIX, [0])
     gather_relay(ml, h_ml)
-    y_forward(MIX)
+    y_forward(MERGE)
+    swap_finish(DOWN)
+    z_start(DOWN)
+    gather_finish(ml, h_ml)
+    z_pass(UP, (1,))
     y_own(DOWN)
-    gather_finish(ml, h_ml)
     gather_relay(gc, h_gc)
+    z_pass(UP, (0,))
     y_finish(MIX)
 
     w_mix, reset_w = weights[MIX], ref.reset_w
@@ -1047,7 +1123,8 @@
         row_loop(rows, 32, act)
 
     row_loop(4 * rows, rows, reset_block)
-    y_forward(MERGE)
+    y_forward(UP, [2])
+    z_pass(DOWN, (1,))
     for handle, (_, pc, px) in zip(h_probs, mates):
         received(handle, probs_low.at[group_rows(pc, px), :])
 
@@ -1066,7 +1143,8 @@
         row_loop(stretch, 32, act)
 
     row_loop(4 * rows, stretch, attend)
-    y_forward(UP, (1,))
+    y_forward(UP, [1])
+    z_pass(DOWN, (0,))
     y_finish(MERGE)
 
     def merge_partial(c, x):
@@ -1075,11 +1153,11 @@
         total[:, own_cols] += mm(ml[at, :], w_hidden())
 
     h_red = reduce_early(merge_partial, sibs_a, cross_a)
+    y_forward(UP, [0])
     for handle, (_, pc, px) in zip(h_update, mates):
         received(handle, update_in.at[:, at_rows((pc * 2 + px) * part_w, part_w, 128)])
     gather_finish(gc, h_gc)
-    y_forward(UP, (2, 3))
-    reduce_late(merge_partial, sibs_a, cross_a, h_red)
+    y_forward(DOWN, [2])
 
     after, hidden_mul, update_mul = ref.after, ref.hidden_mul, ref.update_mul
 
@@ -1097,16 +1175,25 @@
         cen, rate = centre(av)
         n2[at_rows(q * rows + r, 16), :] = (cen * rate * gains[1:2, :]).astype(LOW)
 
-    row_loop(rows, 16, norm_two)
-    h_n2 = gather_start(n2)
-    y_forward(DOWN, (1,))
-    gather_relay(n2, h_n2)
-    y_forward(DOWN, (2,))
-    gather_finish(n2, h_n2)
-    y_forward(DOWN, (3,))
+    h_n2 = []
+
+    def take_merge(first, count):
+        row_loop(count, 16, norm_two, first, 2)
+        h_n2.append(gather_start(n2, first, count))
+
+    reduce_late(merge_partial, sibs_a, cross_a, h_red, take_merge)
+    y_forward(DOWN, [1])
+    gather_relay(n2, h_n2[0])
+    y_forward(DOWN, [0])
+    gather_relay(n2, h_n2[1])
+    for handles in h_n2:
+        gather_finish(n2, handles)
     y_finish(UP)
 
     up_low, up_slope = ref.up_low, ref.up_slope
+    for m in SHARDED:
+        for swap in swaps[m]:
+            sent(swap[0])
 
     def up_block(r):
         total[...] = mm(n2[pl.ds(r, rows), :], weights[UP][...])
@@ -1135,6 +1222,9 @@
     y_grad_send(DOWN, down_product)
     y_finish(DOWN)
 
+    def down_partial(c, x):
+        total[...] = mm(up_low[group_rows(c, x), :], weights[DOWN][...])
+
     def up_back(r):
         at = pl.ds(r, rows)
         total[...] = mm_nt(gc[at, :], weights[DOWN][...])
@@ -1151,16 +1241,14 @@
     def two_partial(c, x):
         total[...] = mm_nt(grad_up[group_rows(c, x), :], weights[UP][...])
 
-    def down_partial(c, x):
-        total[...] = mm(up_low[group_rows(c, x), :], weights[DOWN][...])
-
     def up_product(zz, yy):
         return mm_tn(n2[:, rows_of(UP, zz)], grad_up[:, cols_of(UP, yy)])
 
     h_red = reduce_early(two_partial, sibs_a, cross_a)
     y_grad_send(UP, up_product)
-    y_grad_add(DOWN, down_product)
-    reduce_late(two_partial, sibs_a, cross_a, h_red)
+    y_grad_add(DOWN, down_product, (0, 1))
+    for handle in h_gc[1:]:
+        sent(handle)
 
     gain_sum, update_back = ref.gain_sum, hidden_mul
     gain_sum[...] = jnp.zeros_like(gain_sum)
@@ -1179,8 +1267,13 @@
         u = jax.nn.sigmoid(update_in[at, :].astype(F32))
         update_mul[at, :] = (back * (1.0 - u)).astype(LOW)
 
-    row_loop(rows, 16, norm_two_back)
-    h_gm = gather_start(gm)
+    h_gm = []
+
+    def take_two(first, count):
+        row_loop(count, 16, norm_two_back, first, 2)
+        h_gm.append(gather_start(gm, first, count))
+
+    reduce_late(two_partial, sibs_a, cross_a, h_red, take_two)
     for handle in h_update:
         sent(handle)
     update_grad = mix_pack.at[:, 0:256]
@@ -1191,16 +1284,19 @@
     ]
     update_grad[own_rows, :] = update_back[:, own_cols]
 
-    h_red = reduce_early(down_partial, sibs_b, cross_b)
-    y_grad_add(UP, up_product, (1, 2))
-    gather_relay(gm, h_gm)
-    y_grad_add(UP, up_product, (3,))
-    gather_finish(gm, h_gm)
+    y_grad_add(DOWN, down_product, (2, 3))
+    z_relay(DOWN)
+    y_grad_add(UP, up_product, (0, 1))
+    gather_relay(gm, h_gm[0])
+    gather_relay(gm, h_gm[1])
+    y_grad_add(UP, up_product, (2,))
+    for handles in h_gm:
+        gather_finish(gm, handles)
 
     def merge_product(zz, yy):
         return mm_tn(gated[:, rows_of(MERGE, zz)], gm[:, cols_of(MERGE, yy)])
 
-    for handle in z_sends[UP][1:] + y_sends[UP] + h_gc:
+    for handle in z_sends[UP] + [h for _, h in y_sends[UP]]:
         sent(handle)
     y_grad_send(MERGE, merge_product)
 
@@ -1227,7 +1323,7 @@
 
     def probs_back(r):
         at = pl.ds(r, stretch)
-        grad_probs[at, :] = mm_nt(grad_att[at, :], value_low[at, :])
+        grad_probs[at, :] = mm_nt(grad_att[at, :], value_low[at, :]).astype(LOW)
 
     row_loop(4 * rows, stretch, probs_back)
     h_probs = [
@@ -1247,9 +1343,6 @@
             + mm_nt(mix_pack[at, hidden_at], w_hidden())
         )
 
-    y_grad_add(UP, up_product, (0,))
-    h_mixed = reduce_early(mixed_partial, sibs_a, cross_a)
-    z_grad_add(DOWN)
 
     def value_back(r):
         at = pl.ds(r, stretch)
@@ -1267,15 +1360,9 @@
     def value_product(zz, yy):
         return mm_tn(nl[:, rows_of(VALUE, zz)], grad_value[:, cols_of(VALUE, yy)])
 
-    y_grad_send(VALUE, value_product)
-    y_grad_add(MERGE, merge_product, (1,))
-    reduce_late(down_partial, sibs_b, cross_b, h_red)
-
-    def finish(r):
-        at = pl.ds(r, 16)
-        ref.result[at, :] = (after[at, :] + reduced(r, 16, sibs_b, cross_b)).astype(LOW)
-
-    row_loop(rows, 16, finish)
+    y_grad_send(VALUE, value_product, (0, 1))
+    y_grad_add(UP, up_product, (3,))
+    z_relay(UP)
 
     for i, handle in enumerate(h_probs):
         received(handle, probs_in.at[i])
@@ -1287,7 +1374,9 @@
     for n in range(rows // stretch):
         at = pl.ds(n * stretch, stretch)
         to = at_rows(q * rows + n * stretch, stretch)
-        g = grad_probs[to, :] + probs_in[0, at, :] + probs_in[1, at, :] + probs_in[2, at, :]
+        g = grad_probs[to, :].astype(F32)
+        for i in range(3):
+            g = g + probs_in[i, at, :].astype(F32)
         pr = probs[at, :]
         gs = (pr * (g - jnp.sum(pr * g, axis=-1, keepdims=True))).astype(LOW)
         gq = mm(gs, key[at, :]) * scale
@@ -1305,8 +1394,9 @@
     attn_rows = (grads_q, grads_o, grads_k, lag_sum)
     own_shared = shared_grad.at[own_rows, :]
     h_shared = [send(own_shared, own_shared, peer) for peer, _, _ in mates]
-
-    y_grad_add(MERGE, merge_product, (2, 3, 0))
+    h_mixed = reduce_early(mixed_partial, sibs_a, cross_a)
+
+
     for handle, (_, pc, px) in zip(h_shared, mates):
         received(handle, shared_grad.at[group_rows(pc, px), :])
 
@@ -1314,12 +1404,15 @@
         return mm_tn(ml[:, rows_of(MIX, zz)], mix_pack[:, cols_of(MIX, yy)])
 
     y_grad_send(MIX, mix_product)
+    y_grad_add(MERGE, merge_product)
+    y_grad_send(VALUE, value_product, (2, 3))
+    y_grad_add(VALUE, value_product, (0, 1))
+    z_grad_add(DOWN)
 
     def mixed_own(cc, xx):
         mixed_partial(cc, xx)
         total[...] += mm_nt(shared_grad[own_rows, :], w_shared())
 
-    reduce_late(mixed_own, sibs_a, cross_a, h_mixed)
 
     def to_time(r):
         v = reduced(r, 16, sibs_a, cross_a)
@@ -1327,14 +1420,14 @@
             at = pl.ds(r * tiles + s, 16, stride=tiles)
             out_time[at, :] = out_time[at, :] * v[:, s * 128 : (s + 1) * 128]
 
-    row_loop(rows, 16, to_time)
+    reduce_late(mixed_own, sibs_a, cross_a, h_mixed, lambda first, count: row_loop(count, 16, to_time, first, 2))
 
     def value_partial(cc, xx):
         total[...] = mm_nt(grad_value[group_rows(cc, xx), :], weights[VALUE][...])
 
     h_red = reduce_early(value_partial, sibs_b, cross_b)
-    y_grad_add(VALUE, value_product)
-    z_grad_add(UP)
+    z_relay(MERGE)
+    y_grad_add(MIX, mix_product, (0,))
 
     held = ref.held
     ema = load_ema()
@@ -1375,6 +1468,10 @@
             s, dw, dr, dom = lax.fori_loop(0, CHUNK, back, carry, unroll=2)
             return s * kept(k), dw, dr, dom
 
+        if part:
+            y_grad_add(MIX, mix_product, (1,))
+            z_relay(VALUE)
+            z_relay(MIX, (0,))
         zero = jnp.zeros_like(rate)
         sums.append(lax.fori_loop(0, chunks, chunk, (zero, zero, zero, jnp.zeros_like(omega))))
     small = ref.small_by_time
@@ -1393,8 +1490,30 @@
             for j in range(half):
                 small[pl.ds((p * 2 * half + part * half + j) * tiles, tiles), :] = parts[p][j]
 
-    y_grad_add(MIX, mix_product, (1,))
-    reduce_late(value_partial, sibs_b, cross_b, h_red)
+    tile_rows = ref.tile_rows
+    states = 4 * ema.shape[1]
+    gain_two = jnp.sum(gain_sum[1], axis=0, keepdims=True)
+    for t in range(tiles):
+        at = (t % 2) * depth + t // 2
+        tile_rows[at, 0:states, :] = small[pl.ds(t, states, stride=tiles), :]
+        tail = jnp.concatenate(
+            [
+                jnp.zeros((1, 128), F32),
+                gain_two[:, t * 128 : (t + 1) * 128],
+                sums[0][3][t : t + 1],
+                attn_rows[t // 2],
+                jnp.zeros((4, 128), F32),
+            ],
+            axis=0,
+        )
+        tile_rows[at, states : states + 8, :] = tail
+    sib_in, z_small, x_small, y_small = ref.sib_in, ref.z_small, ref.x_small, ref.y_small
+    h_sib = send(tile_rows.at[pl.ds((1 - c) * depth, depth)], sib_in, sib)
+    y_grad_add(MIX, mix_product, (2,))
+    z_relay(MIX, (1,))
+    received(h_sib, sib_in)
+    sib_in[...] += tile_rows[pl.ds(c * depth, depth)]
+    h_zs = [send(sib_in.at[(z + d) % depth], z_small.at[d - 1], zs[d]) for d in range(1, depth)]
 
     def norm_one_back(r):
         at = pl.ds(r, 16)
@@ -1409,52 +1528,56 @@
         back = rate * (g - jnp.mean(g, axis=-1, keepdims=True) - unit * jnp.mean(g * unit, axis=-1, keepdims=True))
         ref.grad_tokens[at, :] = (back + update_mul[at, :].astype(F32)).astype(LOW)
 
-    row_loop(rows, 16, norm_one_back)
-    y_grad_add(MIX, mix_product, (2,))
-
-    tile_rows = ref.tile_rows
-    states = 4 * ema.shape[1]
+    reduce_late(
+        value_partial, sibs_b, cross_b, h_red, lambda first, count: row_loop(count, 16, norm_one_back, first, 2)
+    )
+    for handle in h_update:
+        sent(handle)
+    h_down = reduce_early(down_partial, sibs_c, cross_c, 3)
+    z_grad_add(UP)
+    one_rows, one_z, one_sum, one_plane = ref.one_rows, ref.one_z, ref.one_sum, ref.one_plane
     gain_one = jnp.sum(gain_sum[0], axis=0, keepdims=True)
-    gain_two = jnp.sum(gain_sum[1], axis=0, keepdims=True)
     for t in range(tiles):
-        at = (t % 2) * depth + t // 2
-        tile_rows[at, 0:states, :] = small[pl.ds(t, states, stride=tiles), :]
-        tail = jnp.concatenate(
-            [
-                gain_one[:, t * 128 : (t + 1) * 128],
-                gain_two[:, t * 128 : (t + 1) * 128],
-                sums[0][3][t : t + 1],
-                attn_rows[t // 2],
-                jnp.zeros((4, 128), F32),
-            ],
-            axis=0,
-        )
-        tile_rows[at, states : states + 8, :] = tail
-    sib_in, z_small, x_small, y_small = ref.sib_in, ref.z_small, ref.x_small, ref.y_small
-    h_sib = send(tile_rows.at[pl.ds((1 - c) * depth, depth)], sib_in, sib)
-    y_grad_add(MIX, mix_product, (3, 0))
-    z_grad_add(MERGE)
-    received(h_sib, sib_in)
-    sib_in[...] += tile_rows[pl.ds(c * depth, depth)]
-    h_zs = [send(sib_in.at[(z + d) % depth], z_small.at[d - 1], zs[d]) for d in range(1, depth)]
-    z_grad_add(VALUE)
+        one_rows[t] = jnp.broadcast_to(gain_one[:, t * 128 : (t + 1) * 128], (8, 128))
+    h_one = [send(one_rows.at[pl.ds((z + d) % depth * 2, 2)], one_z.at[d - 1], zs[d]) for d in range(1, depth)]
     for d, handle in enumerate(h_zs):
         received(handle, z_small.at[d])
     x_small[0] = sib_in[z] + z_small[0] + z_small[1] + z_small[2]
     h_x = send(x_small.at[0], x_small.at[1], xn)
-    z_grad_add(MIX)
+    y_grad_add(MIX, mix_product, (3,))
+    z_grad_add(MERGE)
+    for d, handle in enumerate(h_one):
+        received(handle, one_z.at[d])
+    one_sum[...] = one_rows[pl.ds(z * 2, 2)] + one_z[0] + one_z[1] + one_z[2]
+    h_one = [send(one_sum.at[p[0]], one_plane.at[i], place(z, *p)) for i, p in enumerate(plane)]
     received(h_x, x_small.at[1])
     y_small[0] = x_small[0] + x_small[1]
     h_y = send(y_small.at[0], y_small.at[1], yn)
-    for m in (DOWN, UP, MERGE, VALUE, MIX):
+    y_grad_add(VALUE, value_product, (2, 3))
+    z_grad_add(MIX)
+    z_grad_add(VALUE)
+
+    def finish(r):
+        at = pl.ds(r, 16)
+        ref.result[at, :] = (after[at, :] + reduced(r, 16, sibs_c, cross_c)).astype(LOW)
+
+    reduce_late(down_partial, sibs_c, cross_c, h_down, lambda first, count: row_loop(count, 16, finish, first, 2))
+    for m in (DOWN, UP, MERGE):
         grad_out(m)
     received(h_y, y_small.at[1])
     totals = y_small[0] + y_small[1]
-    states = 4 * ema.shape[1]
     ref.small_out[...] = pltpu.roll(totals, (128 - shift) % 128, 1)
+    one = one_sum[c]
+    for i, handle in enumerate(h_one):
+        received(handle, one_plane.at[i])
+        one = one + one_plane[i]
+    ref.small_out[states : states + 1, :] = pltpu.roll(one, (128 - shift) % 128, 1)[0:1]
+    for m in (MIX, VALUE):
+        grad_out(m)
     ref.attn_out[...] = pltpu.roll(totals[states : states + 8], (128 - c * 64 - fs * 16) % 128, 1)
     for handle in pending:
         sent(handle)
+    assert used[0] <= COPIES
 
 
 def pack_small(norm_gains, ema_params, attn_params):
@@ -1514,7 +1637,7 @@
         small_out=shape((small_rows, 128), F32),
         attn_out=shape((8, 128), F32),
     )
-    copies = pltpu.SemaphoreType.DMA((200,))
+    copies = pltpu.SemaphoreType.DMA((COPIES,))
 
     def low(*dims):
         return pltpu.VMEM(dims, LOW)
@@ -1525,11 +1648,11 @@
     scratch = dict(
         send_sems=copies,
         recv_sems=copies,
-        local_sems=pltpu.SemaphoreType.DMA((24,)),
+        local_sems=pltpu.SemaphoreType.DMA((32,)),
         w=tuple(low(*d) for d in quarters),
         yo=tuple(low(quarters[m][0], quarters[m][1] // 2) for m in (UP, DOWN)),
         yi=tuple(low(r, k // 2) for r, k in quarters),
-        zi=tuple(low(depth - 1, r // depth, k // 2) for r, k in quarters),
+        zi=tuple(low(4, r // depth, k // 2) for r, k in quarters),
         mix_win=low(mix_proj.shape[0], window),
         small_all=low(8 * depth, 32, 128),
         ema_in=full(4 * states * tiles, 128),
@@ -1556,8 +1679,8 @@
         shared_pre=full(rows, Z),
         query=low(rows, Z),
         key=low(rows, Z),
-        grad_probs=full(group, STRETCH),
-        probs_in=full(3, rows, STRETCH),
+        grad_probs=low(group, STRETCH),
+        probs_in=low(3, rows, STRETCH),
         mix_pack=low(group, 10 * STRIP),
         by_time=full(rows * tiles, 128),
         out_time=full(rows * tiles, 128),
@@ -1580,6 +1703,10 @@
         z_small=full(depth - 1, small_rows, 128),
         x_small=full(2, small_rows, 128),
         y_small=full(2, small_rows, 128),
+        one_rows=full(tiles, 8, 128),
+        one_z=full(depth - 1, 2, 8, 128),
+        one_sum=full(2, 8, 128),
+        one_plane=full(7, 8, 128),
     )
     in_vmem = pl.BlockSpec(memory_space=pltpu.VMEM)
     specs = jax.tree.map(lambda _: in_vmem, inputs)
@@ -1615,6 +1742,7 @@
 
 
 VMEM_BYTES = 64 << 20
+COPIES = 256
 
 
 def solution(mesh):
@@ -1643,6 +1771,6 @@
         P(None, (DP, FS), None),
         P((DP, FS)),
     )
-    fits = mesh.shape[DP] // 2 * 4 * STRIP == V and mesh.shape[FS] * 4 * STRIP == V
+    fits = mesh.shape[DP] == 8 and mesh.shape[DP] // 2 * 4 * STRIP == V and mesh.shape[FS] * 4 * STRIP == V
     body = functools.partial(layer_on_device, mesh.shape[DP] // 2) if fits else on_device
     return jax.shard_map(body, mesh=mesh, in_specs=in_specs, out_specs=out_specs, check_vma=False)

time: 303 us -> 258 us (0.85)
  Pallas kernels: 287 us -> 242 us
    pallas_call x1, Pallas kernels: 285 us -> 240 us  [layer_on_device(): pl.pallas_call(functools.partial(layer_kernel, (in_tree, out_tree, scratc...]
where the time goes in v3:
time: 258 us
  Pallas kernels  242 us (94%)
  local copies, waits for them, and re-layouts  14 us (5%)
    pallas_call x1, Pallas kernels, layer_on_device(): pl.pallas_call(functools.partial(layer_kernel, (in_tree, out_tree, scratc...  240 us
    unnamed x25, local copies, waits for them, and re-layouts  13 us

profile of v3, /device:TPU:0, one launch (start us, length us, event | category | flops | bytes accessed | tf_op | source)
XLA Modules:
  0.0 257.7 jit_solution(7287418759359919656)
XLA Ops:
  0.6 0.0 copy-start.9
  0.7 0.7 copy-done.9
  1.3 0.1 reshape.27
  1.4 0.6 copy-done.10
  2.0 0.1 fusion.1
  2.1 0.1 pad.7.clone
  2.1 0.7 copy.21
  2.9 0.1 reshape.26
  3.0 0.7 maximum_maximum_fusion.refs_2_
  3.6 1.8 copy.22.refs_4_
  5.5 240.4 %layer.1 = (f32[8,128]{1,0:T(8,128)}, bf16[128,512]{1,0:T(8,128)(2,1)}, bf16[4,128,384]{2,1,0:T(8,128)(2,1)}, bf16[256,256]{1,0:T(8,128)(2,1)}, bf16[128,1024]{1...) custom-call(bf16[256,1024]{1,0:T(8,128)(2,1)} %refs_0_.1, ...), custom_call_target="tpu_custom_call" | custom-call | tf_op jit(solution)/shard_map/layer/pallas_call | solution.py:1720
  245.9 0.0 copy-start.8
  245.9 0.7 copy-done.8
  246.6 1.0 copy-done
  247.6 1.0 copy-done.1
  248.7 1.0 copy-done.2
  249.6 0.9 copy-done.3
  250.6 0.9 copy-done.4
  251.5 0.9 copy-done.5
  252.4 0.9 copy-done.6
  253.3 0.8 copy-done.7
  254.1 1.9 finish.1
  256.0 0.7 copy.24
  256.7 1.0 copy.23
  (10 shorter events, 0.0 us)
Async XLA Ops:
  0.6 0.7 copy-start.9
  1.3 0.7 copy-start.10
  245.9 0.7 copy-start.8
  246.6 1.0 copy-start
  247.6 1.0 copy-start.1
  248.7 1.0 copy-start.2
  249.6 0.9 copy-start.3
  250.6 0.9 copy-start.4
  251.5 0.9 copy-start.5
  252.4 0.9 copy-start.6
  253.3 0.8 copy-start.7

commit v4 on v3

--- a/solution.py
+++ b/solution.py
@@ -424,6 +424,7 @@
 F32 = jnp.float32
 LOW = jnp.bfloat16
 SHARDED = VALUE, MIX, MERGE, UP, DOWN = range(5)
+TOK, COT = 5, 6
 
 
 def mm(a, b):
@@ -479,12 +480,6 @@
     mates = ((sib, 1 - c, x), (xn, c, 1 - x), (xc, 1 - c, 1 - x))
     plane = [(pc, py, px) for pc in range(2) for py in range(2) for px in range(2)][1:]
     plane = [((c + pc) % 2, (y + py) % 2, (x + px) % 2) for pc, py, px in plane]
-
-    barrier = pltpu.get_barrier_semaphore()
-    peers = [place(z, *p) for p in plane] + zs[1:]
-    for peer in peers:
-        pl.semaphore_signal(barrier, inc=1, device_id=peer, device_id_type=MESH)
-    pl.semaphore_wait(barrier, len(peers))
 
     send_sems, recv_sems, local_sems = ref.send_sems, ref.recv_sems, ref.local_sems
     used, used_local, pending = [0], [0], []
@@ -546,6 +541,19 @@
         return (places < ends[-1]).astype(F32)
 
     small_all, packed = ref.small_all, ref.packed
+    states_at = ref.ema_params.shape[1]
+    params = jnp.zeros((states_at, 128), F32)
+    for p in range(4):
+        v = ref.ema_params[p].astype(F32)
+        v = jnp.concatenate([v, jnp.zeros((states_at, 128 - v.shape[1]), F32)], axis=1)
+        params = params + (pltpu.roll(v, p * 32, 1) if p else v)
+    packed[0:states_at, :] = params.astype(LOW)
+    singles = [ref.norm_gains[p : p + 1, :] for p in range(3)] + [ref.attn_params[...]]
+    row = jnp.zeros((1, 128), F32)
+    for p, v in enumerate(singles):
+        v = jnp.concatenate([v.astype(F32), jnp.zeros((1, 128 - v.shape[1]), F32)], axis=1)
+        row = row + (pltpu.roll(v, p * 32, 1) if p else v)
+    packed[16:32, :] = jnp.broadcast_to(row, (16, 128)).astype(LOW)
     lane_group = lax.broadcasted_iota(jnp.int32, (1, 128), 1) // 32
 
     def slot(pc, py, px, pz):
@@ -592,24 +600,15 @@
     shift = fs * 32
 
     def mix_align():
-        raw, win = ref.s[MIX], ref.mix_win
-        last = raw.shape[1] // 128 * 128
-
-        def step(r):
-            at = pl.ds(r, 32)
-            before = jnp.zeros((32, 128), F32)
-            for t in range(win.shape[1] // 128):
-                if t * 128 < last:
-                    v = raw[at, t * 128 : (t + 1) * 128].astype(F32)
-                else:
-                    v = jnp.concatenate(
-                        [raw[at, last:].astype(F32), jnp.zeros((32, 128 - raw.shape[1] + last), F32)], axis=1
-                    )
-                v = pltpu.roll(v, shift, 1)
-                win[at, t * 128 : (t + 1) * 128] = jnp.where(lane < shift, before, v).astype(LOW)
-                before = v
-
-        row_loop(raw.shape[0], 32, step)
+        raw, win, line_up = ref.s[MIX], ref.mix_win, ref.by_time
+        line_up[0 : win.shape[1], :] = jnp.zeros((win.shape[1], 128), F32)
+
+        def load(r):
+            line_up[at_rows(shift + r, 32, 32), :] = raw[pl.ds(r, 32), :].astype(F32)
+
+        row_loop(raw.shape[0], 32, load)
+        for t in range(win.shape[1] // 128):
+            win[:, t * 128 : (t + 1) * 128] = line_up[t * 128 : (t + 1) * 128, :].T.astype(LOW)
 
     weights = {m: ref.w[m] for m in SHARDED}
     block_shape = {m: (w.shape[0] // depth, w.shape[1] // 2) for m, w in weights.items()}
@@ -639,13 +638,20 @@
         near[m] = spare.at[top : top + tall, 0:wide]
         loads[m] = local(ref.s[m], near[m])
         top += tall
-    for m in loads:
-        loads[m].wait()
+    for k in (TOK, COT):
+        loads[k] = local(ref.acts[k - TOK], (tok, cot)[k - TOK])
+    barrier = pltpu.get_barrier_semaphore()
+    peers = [place(z, *p) for p in plane] + zs[1:]
+    for peer in peers:
+        pl.semaphore_signal(barrier, inc=1, device_id=peer, device_id_type=MESH)
+    pl.semaphore_wait(barrier, len(peers))
 
     swaps = {m: [] for m in SHARDED}
 
     def swap_start(m):
         shard = near[m]
+        if m in loads:
+            loads[m].wait()
         if m == MIX:
             first, last = 1 - (fs + 2) // 3, fs // 3
             middle = 1 - first - last
@@ -900,34 +906,27 @@
             received(handle, landed)
         if m != MIX:
             return
-        out, src = ref.g_mix, f_in[MIX]
+        out, src, line_up = ref.g_mix, f_in[MIX], ref.by_time
         first, last = (fs == 0).astype(F32), (fs == 3).astype(F32)
         mid = 1.0 - first - last
         first, last, mid = (jnp.broadcast_to(v, (1, 128)) for v in (first, last, mid))
 
+        def get(p, t):
+            return src[p, :, t * 128 : (t + 1) * 128].astype(F32)
+
+        for tile in range(9):
+            v = first * (get(tile // 2, tile % 2) if tile < 8 else src[q, :, 256:384].astype(F32))
+            if tile == 0:
+                v = v + (mid + last) * get(3, 0)
+            else:
+                v = v + mid * get((tile - 1) % 4, 1 + (tile - 1) // 4)
+                v = v + last * get((tile - 1) // 2, 1 + (tile - 1) % 2)
+            line_up[tile * 128 : (tile + 1) * 128, :] = v.T
+
         def write(r):
-            at = pl.ds(r, 16)
-
-            def get(p, t):
-                return src[p, at, t * 128 : (t + 1) * 128].astype(F32)
-
-            turned = []
-            for tile in range(9):
-                v = first * (get(tile // 2, tile % 2) if tile < 8 else src[q, at, 256:384].astype(F32))
-                if tile == 0:
-                    v = v + (mid + last) * get(3, 0)
-                else:
-                    v = v + mid * get((tile - 1) % 4, 1 + (tile - 1) // 4)
-                    v = v + last * get((tile - 1) // 2, 1 + (tile - 1) % 2)
-                turned.append(pltpu.roll(v, (128 - shift) % 128, 1))
-            for tile in range(9):
-                v = turned[tile]
-                if tile < 8:
-                    v = jnp.where(lane < 128 - shift, v, turned[tile + 1])
-                wide = min(128, out.shape[1] - tile * 128)
-                out[at, tile * 128 : tile * 128 + wide] = v[:, :wide].astype(LOW)
-
-        row_loop(out.shape[0], 16, write)
+            out[pl.ds(r, 32), :] = line_up[at_rows(shift + r, 32, 32), :].astype(LOW)
+
+        row_loop(out.shape[0], 32, write)
 
     h_small = small_start()
     swap_start(VALUE)
@@ -954,6 +953,7 @@
             by_time[pl.ds(r * tiles + s, 16, stride=tiles), :] = v[:, s * 128 : (s + 1) * 128]
 
     small_finish(h_small)
+    loads[TOK].wait()
     row_loop(rows, 16, norm_one)
     h_nl = gather_start(nl)
     swap_start(UP)
@@ -1005,6 +1005,7 @@
     row_loop(rows, 16, mixed)
     h_ml = gather_start(ml)
     swap_start(DOWN)
+    loads[COT].wait()
     row_loop(rows, 32, cot_low)
     y_forward(VALUE)
     z_pass(MIX, (1,))
@@ -1016,7 +1017,6 @@
     swap_finish(UP)
     z_start(UP)
     y_forward(MIX, [1])
-    y_own(UP)
     z_pass(MERGE)
     y_finish(VALUE)
 
@@ -1036,6 +1036,7 @@
 
     row_loop(4 * rows, rows, value_block)
     y_forward(MIX, [0])
+    y_own(UP)
     gather_relay(ml, h_ml)
     y_forward(MERGE)
     swap_finish(DOWN)
@@ -1471,7 +1472,9 @@
         if part:
             y_grad_add(MIX, mix_product, (1,))
             z_relay(VALUE)
-            z_relay(MIX, (0,))
+            for handle in h_update:
+                sent(handle)
+            h_down = reduce_early(down_partial, sibs_c, cross_c, 3)
         zero = jnp.zeros_like(rate)
         sums.append(lax.fori_loop(0, chunks, chunk, (zero, zero, zero, jnp.zeros_like(omega))))
     small = ref.small_by_time
@@ -1510,10 +1513,10 @@
     sib_in, z_small, x_small, y_small = ref.sib_in, ref.z_small, ref.x_small, ref.y_small
     h_sib = send(tile_rows.at[pl.ds((1 - c) * depth, depth)], sib_in, sib)
     y_grad_add(MIX, mix_product, (2,))
-    z_relay(MIX, (1,))
     received(h_sib, sib_in)
     sib_in[...] += tile_rows[pl.ds(c * depth, depth)]
     h_zs = [send(sib_in.at[(z + d) % depth], z_small.at[d - 1], zs[d]) for d in range(1, depth)]
+    z_relay(MIX)
 
     def norm_one_back(r):
         at = pl.ds(r, 16)
@@ -1531,21 +1534,20 @@
     reduce_late(
         value_partial, sibs_b, cross_b, h_red, lambda first, count: row_loop(count, 16, norm_one_back, first, 2)
     )
-    for handle in h_update:
-        sent(handle)
-    h_down = reduce_early(down_partial, sibs_c, cross_c, 3)
-    z_grad_add(UP)
     one_rows, one_z, one_sum, one_plane = ref.one_rows, ref.one_z, ref.one_sum, ref.one_plane
     gain_one = jnp.sum(gain_sum[0], axis=0, keepdims=True)
     for t in range(tiles):
         one_rows[t] = jnp.broadcast_to(gain_one[:, t * 128 : (t + 1) * 128], (8, 128))
     h_one = [send(one_rows.at[pl.ds((z + d) % depth * 2, 2)], one_z.at[d - 1], zs[d]) for d in range(1, depth)]
+    y_grad_add(MIX, mix_product, (3,))
+    z_grad_add(UP)
+    z_grad_add(MERGE)
+    y_grad_add(VALUE, value_product, (2, 3))
     for d, handle in enumerate(h_zs):
         received(handle, z_small.at[d])
     x_small[0] = sib_in[z] + z_small[0] + z_small[1] + z_small[2]
     h_x = send(x_small.at[0], x_small.at[1], xn)
-    y_grad_add(MIX, mix_product, (3,))
-    z_grad_add(MERGE)
+    z_grad_add(MIX)
     for d, handle in enumerate(h_one):
         received(handle, one_z.at[d])
     one_sum[...] = one_rows[pl.ds(z * 2, 2)] + one_z[0] + one_z[1] + one_z[2]
@@ -1553,8 +1555,6 @@
     received(h_x, x_small.at[1])
     y_small[0] = x_small[0] + x_small[1]
     h_y = send(y_small.at[0], y_small.at[1], yn)
-    y_grad_add(VALUE, value_product, (2, 3))
-    z_grad_add(MIX)
     z_grad_add(VALUE)
 
     def finish(r):
@@ -1580,17 +1580,6 @@
     assert used[0] <= COPIES
 
 
-def pack_small(norm_gains, ema_params, attn_params):
-    states, mine = ema_params.shape[2], ema_params.shape[1]
-    last = jnp.pad(attn_params, (0, mine - attn_params.shape[0]))
-    rows = [
-        jnp.transpose(ema_params, (2, 0, 1)).reshape(states, 4 * mine),
-        jnp.concatenate([norm_gains.reshape(-1), last])[None],
-        jnp.zeros((32 - states - 1, 4 * mine), LOW),
-    ]
-    return jnp.concatenate(rows, axis=0)
-
-
 def finish_kernel(result, grad_tokens, value, mix, merge, up, down, small, attn, *outs):
     for src, out in zip((result, grad_tokens, value, mix, merge, up, down), outs):
 
@@ -1599,11 +1588,10 @@
 
         row_loop(out.shape[0], 32, widen)
     gains, ema, per = outs[7:]
-    mine, states = ema.shape[1:]
+    states, mine = ema.shape[1:]
     gains[...] = small[4 * states : 4 * states + 3, :mine]
-    turned = small[0 : 4 * states, :].T
     for p in range(4):
-        ema[p] = turned[:mine, p * states : (p + 1) * states]
+        ema[p] = small[p * states : (p + 1) * states, :mine]
     per[...] = attn[3:4, : per.shape[1]]
 
 
@@ -1619,12 +1607,15 @@
     states = ema_params.shape[2]
     small_rows = 4 * states + 8
     shape = jax.ShapeDtypeStruct
-    shards = (value_proj, mix_proj, merge_proj, up_proj, down_proj)
+    mix_turned = mix_proj.T
+    ema_turned = jnp.swapaxes(ema_params, 1, 2)
+    shards = (value_proj, mix_turned, merge_proj, up_proj, down_proj)
     inputs = dict(
-        tok=tokens,
-        cot=cotangent,
+        acts=(tokens, cotangent),
         lens=lengths,
-        packed=pack_small(norm_gains, ema_params, attn_params),
+        norm_gains=norm_gains,
+        ema_params=ema_turned,
+        attn_params=attn_params[None],
         s=shards,
     )
     landings = [w.shape for w in shards]
@@ -1633,7 +1624,7 @@
         result=shape((rows, width), LOW),
         grad_tokens=shape((rows, width), LOW),
         fi=tuple(shape(d, LOW) for d in landings),
-        g_mix=shape(mix_proj.shape, LOW),
+        g_mix=shape(mix_turned.shape, LOW),
         small_out=shape((small_rows, 128), F32),
         attn_out=shape((8, 128), F32),
     )
@@ -1655,10 +1646,13 @@
         zi=tuple(low(4, r // depth, k // 2) for r, k in quarters),
         mix_win=low(mix_proj.shape[0], window),
         small_all=low(8 * depth, 32, 128),
+        packed=low(32, 128),
         ema_in=full(4 * states * tiles, 128),
         omega_in=full(tiles, 128),
         gains=full(8, width),
         attn=full(8, 128),
+        tok=low(rows, width),
+        cot=low(rows, width),
         nl=low(group, width),
         ml=low(group, width),
         n2=low(group, width),
@@ -1712,7 +1706,7 @@
     specs = jax.tree.map(lambda _: in_vmem, inputs)
     anywhere = pl.BlockSpec(memory_space=pl.ANY)
     specs.update(
-        lens=pl.BlockSpec(memory_space=pltpu.SMEM), s=tuple(in_vmem if m == MIX else anywhere for m in SHARDED)
+        lens=pl.BlockSpec(memory_space=pltpu.SMEM), acts=(anywhere,) * 2, s=tuple(in_vmem if m == MIX else anywhere for m in SHARDED)
     )
     in_leaves, in_tree = jax.tree.flatten(inputs)
     out_leaves, out_tree = jax.tree.flatten(outputs)
@@ -1729,15 +1723,17 @@
     by = types.SimpleNamespace(**jax.tree.unflatten(out_tree, outs))
     grads = list(by.fi)
     grads[MIX] = by.g_mix
-    wide = [shape(g.shape, F32) for g in (*grads, norm_gains, ema_params)]
+    wide = [shape(g.shape, F32) for g in (*grads, norm_gains, ema_turned)]
     *finals, attn_grad = pl.pallas_call(
         finish_kernel,
         out_shape=(shape((rows, width), LOW), shape((rows, width), LOW), *wide, shape((1, attn_params.shape[0]), F32)),
         in_specs=[in_vmem] * 9,
         out_specs=(in_vmem,) * 10,
-        compiler_params=pltpu.CompilerParams(vmem_limit_bytes=32 << 20),
+        compiler_params=pltpu.CompilerParams(vmem_limit_bytes=VMEM_BYTES),
         name="finish",
     )(by.result, by.grad_tokens, *grads, by.small_out, by.attn_out)
+    finals[2 + MIX] = finals[2 + MIX].T
+    finals[-1] = jnp.swapaxes(finals[-1], 1, 2)
     return (*finals, attn_grad[0])
 
 

time: 258 us -> 236 us (0.915)
  local copies, waits for them, and re-layouts: 14 us -> 0 us
  Pallas kernels: 242 us -> 235 us
    unnamed x25 -> x0, local copies, waits for them, and re-layouts: 13 us -> none
    pallas_call x1, Pallas kernels: 240 us -> 231 us  [layer_on_device(): pl.pallas_call(functools.partial(layer_kernel, (in_tree, out_tree, scratc...]
where the time goes in v4:
time: 236 us
  Pallas kernels  235 us (100%)
    pallas_call x1, Pallas kernels, layer_on_device(): pl.pallas_call(functools.partial(layer_kernel, (in_tree, out_tree, scratc...  231 us

profile of v4, /device:TPU:0, one launch (start us, length us, event | category | flops | bytes accessed | tf_op | source)
XLA Modules:
  0.0 235.9 jit_solution(8224363652764693283)
XLA Ops:
  0.6 231.4 %layer.1 = (f32[8,128]{1,0:T(8,128)}, bf16[128,512]{1,0:T(8,128)(2,1)}, bf16[4,128,384]{2,1,0:T(8,128)(2,1)}, bf16[256,256]{1,0:T(8,128)(2,1)}, bf16[128,1024]{1...) custom-call(bf16[256,1024]{1,0:T(8,128)(2,1)} %refs_0_.1, ...), custom_call_target="tpu_custom_call" | custom-call | tf_op jit(solution)/shard_map/layer/pallas_call | solution.py:1714
  232.0 3.7 %finish.1 = (bf16[256,1024]{1,0:T(8,128)(2,1)}, bf16[256,1024]{1,0:T(8,128)(2,1)}, f32[128,512]{1,0:T(8,128)}, f32[1056,128]{1,0:T(8,128)}, f32[256,256]{1,0:T(8...) custom-call(bf16[256,1024]{1,0:T(8,128)(2,1)} %get-tuple-element.29., ...), custom_call_target="tpu_custom_call" | custom-call | tf_op jit(solution)/shard_map/finish/pallas_call | solution.py:1727

commit v5 on v4

--- a/solution.py
+++ b/solution.py
@@ -716,29 +716,45 @@
     def y_own(m):
         y_sends[m] = [(3, send(block(m, z, y), block(m, z, y), yn))]
 
-    def z_start(m):
-        own = block(m, z, y)
+    def z_start(m, far=False):
+        own = block(m, z, 1 - y if far else y)
         ids = [new_id() for _ in range(3)]
-        z_ids[m] = ids
-        z_sends[m] = [
-            send(own, own, place(partner, c, y, x), ids[2]),
-            send(own, own, place(far_mid, c, y, x), ids[1], middle),
-            send(own, own, place(far_mid, c, y, x), ids[0], outer),
-        ]
-
-    def z_pass(m, steps=(1, 0)):
+        z_ids[m, far] = ids
+        z_sends.setdefault(m, []).extend(
+            [
+                send(own, own, place(partner, c, y, x), ids[2]),
+                send(own, own, place(far_mid, c, y, x), ids[1], middle),
+                send(own, own, place(far_mid, c, y, x), ids[0], outer),
+            ]
+        )
+
+    def z_received(m, i, far, when):
+        there = block(m, line[i], 1 - y if far else y)
+        pl.when(when)(functools.partial(received, z_ids[m, far][i], there))
+        return there
+
+    def z_pass(m, steps=(1, 0), far=False):
         for i in steps:
-            there = block(m, line[i], y)
-            pl.when(middle)(functools.partial(received, z_ids[m][i], there))
-            z_sends[m].append(send(there, there, place(partner, c, y, x), z_ids[m][i], middle))
+            there = z_received(m, i, far, middle)
+            z_sends[m].append(send(there, there, place(partner, c, y, x), z_ids[m, far][i], middle))
+
+    def z_far(m):
+        received(y_sends[m][0][1], block(m, z, 1 - y))
+        z_start(m, True)
+
+    def z_finish(m):
+        for far in (False, True):
+            received(z_ids[m, far][2], block(m, partner, 1 - y if far else y))
+            for i in (1, 0):
+                z_received(m, i, far, outer)
 
     def y_forward(m, steps=(2, 1, 0)):
         for i in steps:
             there = block(m, line[i], y)
             if i == 2:
-                received(z_ids[m][i], there)
+                received(z_ids[m, False][i], there)
             else:
-                pl.when(outer)(functools.partial(received, z_ids[m][i], there))
+                z_received(m, i, False, outer)
             y_sends[m].append((i, send(there, there, yn)))
 
     def y_finish(m):
@@ -784,21 +800,26 @@
             sent(handle)
         staged[k] = []
 
-    def reduce_early(partial, sibs, cross, slot=2):
-        halves = (pl.ds(0, rows // 2), pl.ds(rows // 2, rows // 2))
+    def reduce_first(partial, sibs):
         for k, px in ((0, 1 - x), (1, x)):
             partial(1 - c, px)
             stage_free(k)
             stage_out(k, 0, rows)
             staged[k] = [send(stage[k], sibs[k], sib)]
-        first, second = staged[0][0], staged[1][0]
+        return staged[0][0], staged[1][0]
+
+    def reduce_cross(partial, sibs, cross, handles, slot=2):
+        halves = (pl.ds(0, rows // 2), pl.ds(rows // 2, rows // 2))
         partial(c, 1 - x)
-        received(first, sibs[0])
+        received(handles[0], sibs[0])
         stage_free(slot)
         for i, half in enumerate(halves):
             stage_out(slot, i * (rows // 2), rows // 2, sibs[0])
             staged[slot].append(send(stage[slot].at[half, :], cross.at[half, :], xn))
-        return second, list(zip(staged[slot], (cross.at[half, :] for half in halves)))
+        return handles[1], list(zip(staged[slot], (cross.at[half, :] for half in halves)))
+
+    def reduce_early(partial, sibs, cross):
+        return reduce_cross(partial, sibs, cross, reduce_first(partial, sibs))
 
     def reduce_late(partial, sibs, cross, handles, consume):
         partial(c, x)
@@ -817,8 +838,8 @@
 
     w_up = weights[UP]
     y_out = {
-        DOWN: ref.yo[1],
-        UP: ref.yo[0],
+        DOWN: ref.mix_pack.at[:, 384 : 384 + block_shape[DOWN][1]],
+        UP: ref.yo,
         MERGE: ref.gc.at[0 : weights[MERGE].shape[0], 0 : block_shape[MERGE][1]],
         MIX: w_up.at[:, 0 : block_shape[MIX][1]],
         VALUE: w_up.at[:, block_shape[MIX][1] : block_shape[MIX][1] + block_shape[VALUE][1]],
@@ -874,6 +895,58 @@
             y_in[m][at, :] = v.astype(LOW)
 
         row_loop(rb, 64, add)
+        to_owners(m)
+
+    far_land = [ref.mix_in.at[i // 2, pl.ds(i % 2 * 128, 128), :] for i in range(4)]
+    y_last = ref.mix_win.at[:, 0 : block_shape[MERGE][1]]
+
+    def sides(m):
+        return (False, y_in[m], [z_in[m].at[i] for i in range(4)]), (True, y_out[m], far_land)
+
+    def first_send(m, product):
+        rb, cb = block_shape[m]
+        for far, _, _ in sides(m):
+            gz[m, far] = [new_id() for _ in range(4)]
+        for i in range(4):
+            at = at_rows(line[i] * rb, rb)
+            for far, buf, land in sides(m):
+                buf[at, :] = product(line[i], 1 - y if far else y).astype(LOW)
+                if i < 3:
+                    send(
+                        buf.at[at, :], land[i], place(partner, c, y, x), gz[m, far][i], outer if i < 2 else None
+                    )
+
+    def first_relay(m):
+        rb, cb = block_shape[m]
+        for i in (0, 1):
+            at = at_rows(line[i] * rb, rb)
+            for far, buf, land in sides(m):
+
+                @pl.when(middle)
+                def _(i=i, at=at, far=far, buf=buf, land=land):
+                    received(gz[m, far][i], land[i])
+                    buf[at, :] = (buf[at, :].astype(F32) + land[i][...].astype(F32)).astype(LOW)
+
+                send(buf.at[at, :], land[3], place(line[i], c, y, x), gz[m, far][3], middle)
+
+    def first_turn(m):
+        rb, cb = block_shape[m]
+        at = at_rows(z * rb, rb)
+        for far, buf, land in sides(m):
+            for i in (2, 3):
+                received(gz[m, far][i], land[i])
+            buf[at, :] = (buf[at, :].astype(F32) + land[2][...].astype(F32) + land[3][...].astype(F32)).astype(LOW)
+        gy[m] = send(y_out[m].at[at, :], y_last, yn)
+
+    def first_finish(m):
+        rb, cb = block_shape[m]
+        at = at_rows(z * rb, rb)
+        received(gy[m], y_last)
+        y_in[m][at, :] = (y_in[m][at, :].astype(F32) + y_last[...].astype(F32)).astype(LOW)
+        to_owners(m)
+
+    def to_owners(m):
+        rb, cb = block_shape[m]
         gf[m] = []
         if m in (MERGE, DOWN):
             land = f_in[m].at[at_rows(x * rb, rb), :]
@@ -929,14 +1002,14 @@
         row_loop(out.shape[0], 32, write)
 
     h_small = small_start()
+    mix_align()
+    swap_start(MIX)
+    h_small = small_relay(h_small)
     swap_start(VALUE)
-    mix_align()
-    h_small = small_relay(h_small)
     swap_start(MERGE)
-    swap_start(MIX)
-    swap_finish(VALUE)
-    y_own(VALUE)
-    z_start(VALUE)
+    swap_finish(MIX)
+    y_own(MIX)
+    z_start(MIX)
 
     nl, ml, n2, gc, gm = (ref.nl, ref.ml, ref.n2, ref.gc, ref.gm)
     by_time, out_time, back_time = ref.by_time, ref.out_time, ref.back_time
@@ -955,15 +1028,9 @@
     small_finish(h_small)
     loads[TOK].wait()
     row_loop(rows, 16, norm_one)
-    h_nl = gather_start(nl)
-    swap_start(UP)
-    swap_finish(MERGE)
-    y_own(MERGE)
-    swap_finish(MIX)
-    y_own(MIX)
-    z_pass(VALUE)
-    z_start(MIX)
-    z_start(MERGE)
+    swap_finish(VALUE)
+    y_own(VALUE)
+    z_start(VALUE)
 
     def cot_low(r):
         at = pl.ds(r, 32)
@@ -1004,21 +1071,26 @@
 
     row_loop(rows, 16, mixed)
     h_ml = gather_start(ml)
+    swap_start(UP)
+    h_nl = gather_start(nl)
+    swap_finish(MERGE)
+    z_start(MERGE)
+    z_pass(MIX, (1,))
+    y_forward(MIX, [2])
     swap_start(DOWN)
     loads[COT].wait()
     row_loop(rows, 32, cot_low)
+    z_pass(MIX, (0,))
+    y_forward(MIX, [1])
+    z_pass(VALUE)
+    gather_relay(ml, h_ml)
+    y_forward(MIX, [0])
+    y_own(MERGE)
     y_forward(VALUE)
-    z_pass(MIX, (1,))
-    gather_relay(nl, h_nl)
-    h_gc = gather_start(gc)
-    y_forward(MIX, [2])
-    z_pass(MIX, (0,))
-    gather_finish(nl, h_nl)
     swap_finish(UP)
     z_start(UP)
-    y_forward(MIX, [1])
+    gather_finish(ml, h_ml)
     z_pass(MERGE)
-    y_finish(VALUE)
 
     value_low, value_slope = ref.value_low, ref.value_slope
     vq = value_low.shape[1]
@@ -1034,18 +1106,6 @@
 
         row_loop(rows, 32, act)
 
-    row_loop(4 * rows, rows, value_block)
-    y_forward(MIX, [0])
-    y_own(UP)
-    gather_relay(ml, h_ml)
-    y_forward(MERGE)
-    swap_finish(DOWN)
-    z_start(DOWN)
-    gather_finish(ml, h_ml)
-    z_pass(UP, (1,))
-    y_own(DOWN)
-    gather_relay(gc, h_gc)
-    z_pass(UP, (0,))
     y_finish(MIX)
 
     w_mix, reset_w = weights[MIX], ref.reset_w
@@ -1107,6 +1167,8 @@
         send(update_out.at[group_rows(pc, px), :], update_in.at[:, own_cols], peer) for peer, pc, px in mates
     ]
     update_in[:, own_cols] = update_out[group_rows(c, x), :]
+    gather_relay(nl, h_nl)
+    h_gc = gather_start(gc)
 
     reset_gate, reset_slope = ref.reset_gate, ref.reset_slope
 
@@ -1124,8 +1186,17 @@
         row_loop(rows, 32, act)
 
     row_loop(4 * rows, rows, reset_block)
+    y_forward(MERGE)
+    swap_finish(DOWN)
+    z_start(DOWN)
+    y_own(DOWN)
+    z_pass(UP, (1,))
+    gather_finish(nl, h_nl)
+    y_finish(VALUE)
+    row_loop(4 * rows, rows, value_block)
+    z_pass(UP, (0,))
+    y_own(UP)
     y_forward(UP, [2])
-    z_pass(DOWN, (1,))
     for handle, (_, pc, px) in zip(h_probs, mates):
         received(handle, probs_low.at[group_rows(pc, px), :])
 
@@ -1144,8 +1215,8 @@
         row_loop(stretch, 32, act)
 
     row_loop(4 * rows, stretch, attend)
+    z_pass(DOWN, (1,))
     y_forward(UP, [1])
-    z_pass(DOWN, (0,))
     y_finish(MERGE)
 
     def merge_partial(c, x):
@@ -1154,11 +1225,12 @@
         total[:, own_cols] += mm(ml[at, :], w_hidden())
 
     h_red = reduce_early(merge_partial, sibs_a, cross_a)
+    z_pass(DOWN, (0,))
     y_forward(UP, [0])
     for handle, (_, pc, px) in zip(h_update, mates):
         received(handle, update_in.at[:, at_rows((pc * 2 + px) * part_w, part_w, 128)])
-    gather_finish(gc, h_gc)
-    y_forward(DOWN, [2])
+    gather_relay(gc, h_gc)
+    z_far(DOWN)
 
     after, hidden_mul, update_mul = ref.after, ref.hidden_mul, ref.update_mul
 
@@ -1183,12 +1255,13 @@
         h_n2.append(gather_start(n2, first, count))
 
     reduce_late(merge_partial, sibs_a, cross_a, h_red, take_merge)
-    y_forward(DOWN, [1])
+    z_pass(DOWN, (1,), True)
     gather_relay(n2, h_n2[0])
-    y_forward(DOWN, [0])
+    z_pass(DOWN, (0,), True)
     gather_relay(n2, h_n2[1])
     for handles in h_n2:
         gather_finish(n2, handles)
+    gather_finish(gc, h_gc)
     y_finish(UP)
 
     up_low, up_slope = ref.up_low, ref.up_slope
@@ -1221,7 +1294,7 @@
         return mm_tn(up_low[:, rows_of(DOWN, zz)], gc[:, cols_of(DOWN, yy)])
 
     y_grad_send(DOWN, down_product)
-    y_finish(DOWN)
+    z_finish(DOWN)
 
     def down_partial(c, x):
         total[...] = mm(up_low[group_rows(c, x), :], weights[DOWN][...])
@@ -1287,10 +1360,10 @@
 
     y_grad_add(DOWN, down_product, (2, 3))
     z_relay(DOWN)
-    y_grad_add(UP, up_product, (0, 1))
     gather_relay(gm, h_gm[0])
+    y_grad_add(UP, up_product, (0,))
     gather_relay(gm, h_gm[1])
-    y_grad_add(UP, up_product, (2,))
+    y_grad_add(UP, up_product, (1,))
     for handles in h_gm:
         gather_finish(gm, handles)
 
@@ -1299,8 +1372,6 @@
 
     for handle in z_sends[UP] + [h for _, h in y_sends[UP]]:
         sent(handle)
-    y_grad_send(MERGE, merge_product)
-
     grad_probs, probs_in = ref.grad_probs, ref.probs_in
 
     def gated_back(r):
@@ -1319,6 +1390,8 @@
 
         row_loop(rows, 32, act)
 
+    for handle in gy[DOWN].values():
+        sent(handle)
     row_loop(4 * rows, rows, gated_back)
     grad_att = reset_gate
 
@@ -1330,6 +1403,7 @@
     h_probs = [
         send(grad_probs.at[group_rows(pc, px), :], probs_in.at[i], peer) for i, (peer, pc, px) in enumerate(mates)
     ]
+    first_send(MERGE, merge_product)
     for handle, (_, pc, px) in zip(h_update, mates):
         received(handle, update_grad.at[group_rows(pc, px), :])
 
@@ -1362,7 +1436,7 @@
         return mm_tn(nl[:, rows_of(VALUE, zz)], grad_value[:, cols_of(VALUE, yy)])
 
     y_grad_send(VALUE, value_product, (0, 1))
-    y_grad_add(UP, up_product, (3,))
+    y_grad_add(UP, up_product, (2, 3))
     z_relay(UP)
 
     for i, handle in enumerate(h_probs):
@@ -1405,10 +1479,13 @@
         return mm_tn(ml[:, rows_of(MIX, zz)], mix_pack[:, cols_of(MIX, yy)])
 
     y_grad_send(MIX, mix_product)
-    y_grad_add(MERGE, merge_product)
+    first_relay(MERGE)
     y_grad_send(VALUE, value_product, (2, 3))
     y_grad_add(VALUE, value_product, (0, 1))
     z_grad_add(DOWN)
+    for handle in h_update:
+        sent(handle)
+    h_down = reduce_first(down_partial, sibs_c)
 
     def mixed_own(cc, xx):
         mixed_partial(cc, xx)
@@ -1427,7 +1504,6 @@
         total[...] = mm_nt(grad_value[group_rows(cc, xx), :], weights[VALUE][...])
 
     h_red = reduce_early(value_partial, sibs_b, cross_b)
-    z_relay(MERGE)
     y_grad_add(MIX, mix_product, (0,))
 
     held = ref.held
@@ -1469,15 +1545,19 @@
             s, dw, dr, dom = lax.fori_loop(0, CHUNK, back, carry, unroll=2)
             return s * kept(k), dw, dr, dom
 
+        zero = jnp.zeros_like(rate)
+        carry = lax.fori_loop(0, chunks // 2, chunk, (zero, zero, zero, jnp.zeros_like(omega)))
         if part:
+            y_grad_add(MIX, mix_product, (2,))
+        else:
             y_grad_add(MIX, mix_product, (1,))
             z_relay(VALUE)
-            for handle in h_update:
-                sent(handle)
-            h_down = reduce_early(down_partial, sibs_c, cross_c, 3)
-        zero = jnp.zeros_like(rate)
-        sums.append(lax.fori_loop(0, chunks, chunk, (zero, zero, zero, jnp.zeros_like(omega))))
-    small = ref.small_by_time
+        sums.append(lax.fori_loop(chunks // 2, chunks, chunk, carry))
+        if not part:
+            h_down = reduce_cross(down_partial, sibs_c, cross_c, h_down, 3)
+            z_relay(MIX, (0,))
+            first_turn(MERGE)
+    small = ref.by_time
     rate_scale = ema.shape[1] ** (-0.5)
     for part in range(2):
         js = slice(part * half, (part + 1) * half)
@@ -1512,11 +1592,10 @@
         tile_rows[at, states : states + 8, :] = tail
     sib_in, z_small, x_small, y_small = ref.sib_in, ref.z_small, ref.x_small, ref.y_small
     h_sib = send(tile_rows.at[pl.ds((1 - c) * depth, depth)], sib_in, sib)
-    y_grad_add(MIX, mix_product, (2,))
+    z_relay(MIX, (1,))
     received(h_sib, sib_in)
     sib_in[...] += tile_rows[pl.ds(c * depth, depth)]
     h_zs = [send(sib_in.at[(z + d) % depth], z_small.at[d - 1], zs[d]) for d in range(1, depth)]
-    z_relay(MIX)
 
     def norm_one_back(r):
         at = pl.ds(r, 16)
@@ -1541,7 +1620,7 @@
     h_one = [send(one_rows.at[pl.ds((z + d) % depth * 2, 2)], one_z.at[d - 1], zs[d]) for d in range(1, depth)]
     y_grad_add(MIX, mix_product, (3,))
     z_grad_add(UP)
-    z_grad_add(MERGE)
+    first_finish(MERGE)
     y_grad_add(VALUE, value_product, (2, 3))
     for d, handle in enumerate(h_zs):
         received(handle, z_small.at[d])
@@ -1641,7 +1720,7 @@
         recv_sems=copies,
         local_sems=pltpu.SemaphoreType.DMA((32,)),
         w=tuple(low(*d) for d in quarters),
-        yo=tuple(low(quarters[m][0], quarters[m][1] // 2) for m in (UP, DOWN)),
+        yo=low(width, fq // 2),
         yi=tuple(low(r, k // 2) for r, k in quarters),
         zi=tuple(low(4, r // depth, k // 2) for r, k in quarters),
         mix_win=low(mix_proj.shape[0], window),
@@ -1658,7 +1737,7 @@
         n2=low(group, width),
         gc=low(group, width),
         gm=low(group, width),
-        mix_in=low(2, 2 * mix_proj.shape[0], 3 * STRIP),
+        mix_in=low(2, 2 * mix_proj.shape[0], 4 * STRIP),
         reset_w=low(width, 256),
         value_low=low(group, vq),
         value_slope=low(group, vq),
@@ -1691,7 +1770,6 @@
         hidden_mul=low(rows, width),
         update_mul=low(rows, width),
         gain_sum=full(2, 16, width),
-        small_by_time=full(4 * states * tiles, 128),
         tile_rows=full(tiles, small_rows, 128),
         sib_in=full(depth, small_rows, 128),
         z_small=full(depth - 1, small_rows, 128),

time: 236 us -> 222 us (0.941)
  Pallas kernels: 235 us -> 221 us
    pallas_call x1, Pallas kernels: 231 us -> 218 us  [layer_on_device(): pl.pallas_call(functools.partial(layer_kernel, (in_tree, out_tree, scratc...]
where the time goes in v5:
time: 222 us
  Pallas kernels  221 us (100%)
    pallas_call x1, Pallas kernels, layer_on_device(): pl.pallas_call(functools.partial(layer_kernel, (in_tree, out_tree, scratc...  218 us

profile of v5, /device:TPU:0, one launch (start us, length us, event | category | flops | bytes accessed | tf_op | source)
XLA Modules:
  0.0 222.1 jit_solution(16740148028852351644)
XLA Ops:
  0.6 217.6 %layer.1 = (f32[8,128]{1,0:T(8,128)}, bf16[128,512]{1,0:T(8,128)(2,1)}, bf16[4,128,384]{2,1,0:T(8,128)(2,1)}, bf16[256,256]{1,0:T(8,128)(2,1)}, bf16[128,1024]{1...) custom-call(bf16[256,1024]{1,0:T(8,128)(2,1)} %refs_0_.1, ...), custom_call_target="tpu_custom_call" | custom-call | tf_op jit(solution)/shard_map/layer/pallas_call | solution.py:1792
  218.3 3.7 %finish.1 = (bf16[256,1024]{1,0:T(8,128)(2,1)}, bf16[256,1024]{1,0:T(8,128)(2,1)}, f32[128,512]{1,0:T(8,128)}, f32[1056,128]{1,0:T(8,128)}, f32[256,256]{1,0:T(8...) custom-call(bf16[256,1024]{1,0:T(8,128)(2,1)} %get-tuple-element.29., ...), custom_call_target="tpu_custom_call" | custom-call | tf_op jit(solution)/shard_map/finish/pallas_call | solution.py:1805

commit v6 on v5

--- a/solution.py
+++ b/solution.py
@@ -1256,21 +1256,13 @@
 
     reduce_late(merge_partial, sibs_a, cross_a, h_red, take_merge)
     z_pass(DOWN, (1,), True)
-    gather_relay(n2, h_n2[0])
-    z_pass(DOWN, (0,), True)
-    gather_relay(n2, h_n2[1])
-    for handles in h_n2:
-        gather_finish(n2, handles)
-    gather_finish(gc, h_gc)
-    y_finish(UP)
-
     up_low, up_slope = ref.up_low, ref.up_slope
     for m in SHARDED:
         for swap in swaps[m]:
             sent(swap[0])
 
     def up_block(r):
-        total[...] = mm(n2[pl.ds(r, rows), :], weights[UP][...])
+        total[...] = mm(n2[at_rows(r, rows), :], weights[UP][...])
 
         def act(s):
             v = total[pl.ds(s, 16), :]
@@ -1280,7 +1272,22 @@
 
         row_loop(rows, 16, act)
 
-    row_loop(4 * rows, rows, up_block)
+    def up_rows(c, x):
+        up_block(pl.multiple_of((c * 2 + x) * rows, rows))
+
+    gather_relay(n2, h_n2[0])
+    z_pass(DOWN, (0,), True)
+    y_finish(UP)
+    up_rows(c, x)
+    for handles in h_n2:
+        received(handles[2], n2.at[part_rows(1 - c, x, *handles[0]), :])
+    up_rows(1 - c, x)
+    gather_relay(n2, h_n2[1])
+    up_rows(c, 1 - x)
+    for handles in h_n2:
+        received(handles[3], n2.at[part_rows(1 - c, 1 - x, *handles[0]), :])
+    up_rows(1 - c, 1 - x)
+    gather_finish(gc, h_gc)
 
     def cols_of(m, yy):
         cb = block_shape[m][1]
@@ -1360,26 +1367,20 @@
 
     y_grad_add(DOWN, down_product, (2, 3))
     z_relay(DOWN)
-    gather_relay(gm, h_gm[0])
-    y_grad_add(UP, up_product, (0,))
-    gather_relay(gm, h_gm[1])
-    y_grad_add(UP, up_product, (1,))
-    for handles in h_gm:
-        gather_finish(gm, handles)
-
     def merge_product(zz, yy):
         return mm_tn(gated[:, rows_of(MERGE, zz)], gm[:, cols_of(MERGE, yy)])
 
-    for handle in z_sends[UP] + [h for _, h in y_sends[UP]]:
+    for handle in z_sends[UP] + [h for _, h in y_sends[UP]] + list(gy[DOWN].values()):
         sent(handle)
     grad_probs, probs_in = ref.grad_probs, ref.probs_in
-
-    def gated_back(r):
-        at = pl.ds(r, rows)
-        total[:, :vq] = mm_nt(gm[at, :], weights[MERGE][...])
+    grad_att = reset_gate
+
+    def gated_back(c, x):
+        first = (c * 2 + x) * rows
+        total[:, :vq] = mm_nt(gm[at_rows(first, rows), :], weights[MERGE][...])
 
         def act(s):
-            to = at_rows(r + s, 32)
+            to = at_rows(first + s, 32)
             g = total[pl.ds(s, 32), :vq]
             back = (g * reset_slope[to, :].astype(F32)).astype(LOW)
             mix_pack[to, 384:640] = back[:, 0:256]
@@ -1390,19 +1391,27 @@
 
         row_loop(rows, 32, act)
 
-    for handle in gy[DOWN].values():
-        sent(handle)
-    row_loop(4 * rows, rows, gated_back)
-    grad_att = reset_gate
-
-    def probs_back(r):
-        at = pl.ds(r, stretch)
-        grad_probs[at, :] = mm_nt(grad_att[at, :], value_low[at, :]).astype(LOW)
-
-    row_loop(4 * rows, stretch, probs_back)
+        def probs_back(r):
+            at = at_rows(first + r, stretch)
+            grad_probs[at, :] = mm_nt(grad_att[at, :], value_low[at, :]).astype(LOW)
+
+        row_loop(rows, stretch, probs_back)
+
+    gated_back(c, x)
+    gather_relay(gm, h_gm[0])
+    y_grad_add(UP, up_product, (0,))
+    for handles in h_gm:
+        received(handles[2], gm.at[part_rows(1 - c, x, *handles[0]), :])
+    gated_back(1 - c, x)
+    gather_relay(gm, h_gm[1])
+    gated_back(c, 1 - x)
+    for handles in h_gm:
+        received(handles[3], gm.at[part_rows(1 - c, 1 - x, *handles[0]), :])
+    gated_back(1 - c, 1 - x)
     h_probs = [
         send(grad_probs.at[group_rows(pc, px), :], probs_in.at[i], peer) for i, (peer, pc, px) in enumerate(mates)
     ]
+    y_grad_add(UP, up_product, (1,))
     first_send(MERGE, merge_product)
     for handle, (_, pc, px) in zip(h_update, mates):
         received(handle, update_grad.at[group_rows(pc, px), :])
@@ -1437,7 +1446,6 @@
 
     y_grad_send(VALUE, value_product, (0, 1))
     y_grad_add(UP, up_product, (2, 3))
-    z_relay(UP)
 
     for i, handle in enumerate(h_probs):
         received(handle, probs_in.at[i])
@@ -1479,6 +1487,7 @@
         return mm_tn(ml[:, rows_of(MIX, zz)], mix_pack[:, cols_of(MIX, yy)])
 
     y_grad_send(MIX, mix_product)
+    z_relay(UP)
     first_relay(MERGE)
     y_grad_send(VALUE, value_product, (2, 3))
     y_grad_add(VALUE, value_product, (0, 1))

time: 222 us -> 221 us (level)
  no operation moved by 1% of the time
where the time goes in v6:
time: 221 us
  Pallas kernels  220 us (100%)
    pallas_call x1, Pallas kernels, layer_on_device(): pl.pallas_call(functools.partial(layer_kernel, (in_tree, out_tree, scratc...  216 us

profile of v6, /device:TPU:0, one launch (start us, length us, event | category | flops | bytes accessed | tf_op | source)
XLA Modules:
  0.0 220.9 jit_solution(16948698754695621452)
XLA Ops:
  0.6 216.5 %layer.1 = (f32[8,128]{1,0:T(8,128)}, bf16[128,512]{1,0:T(8,128)(2,1)}, bf16[4,128,384]{2,1,0:T(8,128)(2,1)}, bf16[256,256]{1,0:T(8,128)(2,1)}, bf16[128,1024]{1...) custom-call(bf16[256,1024]{1,0:T(8,128)(2,1)} %refs_0_.1, ...), custom_call_target="tpu_custom_call" | custom-call | tf_op jit(solution)/shard_map/layer/pallas_call | solution.py:1801
  217.1 3.7 %finish.1 = (bf16[256,1024]{1,0:T(8,128)(2,1)}, bf16[256,1024]{1,0:T(8,128)(2,1)}, f32[128,512]{1,0:T(8,128)}, f32[1056,128]{1,0:T(8,128)}, f32[256,256]{1,0:T(8...) custom-call(bf16[256,1024]{1,0:T(8,128)(2,1)} %get-tuple-element.29., ...), custom_call_target="tpu_custom_call" | custom-call | tf_op jit(solution)/shard_map/finish/pallas_call | solution.py:1814

commit v7 on v6

--- a/solution.py
+++ b/solution.py
@@ -793,7 +793,7 @@
                 v = v + extra[at, :].astype(F32)
             stage[k][at, :] = v.astype(LOW)
 
-        row_loop(count, 32, put, first)
+        row_loop(count, 32, put, first, 2)
 
     def stage_free(k):
         for handle in staged[k]:
@@ -1027,7 +1027,7 @@
 
     small_finish(h_small)
     loads[TOK].wait()
-    row_loop(rows, 16, norm_one)
+    row_loop(rows, 16, norm_one, 0, 2)
     swap_finish(VALUE)
     y_own(VALUE)
     z_start(VALUE)

time: 221 us -> 223 us (level)
  no operation moved by 1% of the time
where the time goes in v7:
time: 223 us
  Pallas kernels  222 us (100%)
    pallas_call x1, Pallas kernels, layer_on_device(): pl.pallas_call(functools.partial(layer_kernel, (in_tree, out_tree, scratc...  218 us

profile of v7, /device:TPU:0, one launch (start us, length us, event | category | flops | bytes accessed | tf_op | source)
XLA Modules:
  0.0 222.7 jit_solution(13389996825271553247)
XLA Ops:
  0.6 218.2 %layer.1 = (f32[8,128]{1,0:T(8,128)}, bf16[128,512]{1,0:T(8,128)(2,1)}, bf16[4,128,384]{2,1,0:T(8,128)(2,1)}, bf16[256,256]{1,0:T(8,128)(2,1)}, bf16[128,1024]{1...) custom-call(bf16[256,1024]{1,0:T(8,128)(2,1)} %refs_0_.1, ...), custom_call_target="tpu_custom_call" | custom-call | tf_op jit(solution)/shard_map/layer/pallas_call | solution.py:1801
  218.9 3.7 %finish.1 = (bf16[256,1024]{1,0:T(8,128)(2,1)}, bf16[256,1024]{1,0:T(8,128)(2,1)}, f32[128,512]{1,0:T(8,128)}, f32[1056,128]{1,0:T(8,128)}, f32[256,256]{1,0:T(8...) custom-call(bf16[256,1024]{1,0:T(8,128)(2,1)} %get-tuple-element.29., ...), custom_call_target="tpu_custom_call" | custom-call | tf_op jit(solution)/shard_map/finish/pallas_call | solution.py:1814
